TPU v7x, 32 devices: a whole 2x2x4 slice. The times are simulated.
32 devices in a mesh: ep: 8 (over z, x), ws: 4 (over y, core).
Axes of the slice: x: 2, y: 2, z: 4, core: 2. Of those that a mesh axis runs over, the one named last changes fastest.
Arguments:
- hidden_in: bfloat16 [8192, 2048], P(('ep', 'ws')), may hold values from -36 to 36
- attn_gain: bfloat16 [2048], P('ws'), may hold values from 0.5 to 1.5
- w_query: bfloat16 [2048, 4096], P('ws'), may hold values from -0.125 to 0.125
- key_projection: bfloat16 [2048, 512], P('ws'), may hold values from -0.125 to 0.125
- value_projection: bfloat16 [2048, 512], P('ws'), may hold values from -0.125 to 0.125
- query_gain: float32 [128], replicated, may hold values from 0.5 to 1.5
- key_gain: float32 [128], replicated, may hold values from 0.5 to 1.5
- w_output: bfloat16 [4096, 2048], P('ws'), may hold values from -0.375 to 0.375
- ffn_gain: bfloat16 [2048], P('ws'), may hold values from 0.5 to 1.5
- w_router: bfloat16 [2048, 32], P('ws'), may hold values from -0.0625 to 0.0625
- routes: int32 [8192, 8], P(('ep', 'ws')), may hold values from 0 to 31, as said below
- w_gate: bfloat16 [32, 2048, 768], P(('ep', 'ws')), may hold values from -0.125 to 0.125
- w_up: bfloat16 [32, 2048, 768], P(('ep', 'ws')), may hold values from -0.125 to 0.125
- w_down: bfloat16 [32, 768, 2048], P(('ep', 'ws')), may hold values from -1.25 to 1.25
- cotangent: bfloat16 [8192, 2048], P(('ep', 'ws')), may hold values from -36 to 36
Outputs:
- hidden_out: bfloat16 [8192, 2048], P(('ep', 'ws'))
- grad_in: float32 [8192, 2048], P(('ep', 'ws'))
- grad_attn_gain: float32 [2048], P(('ep', 'ws'))
- grad_query: float32 [2048, 4096], P(('ep', 'ws'))
- grad_key: float32 [2048, 512], P(('ep', 'ws'))
- grad_value: float32 [2048, 512], P(('ep', 'ws'))
- grad_query_gain: float32 [128], replicated
- grad_key_gain: float32 [128], replicated
- grad_output: float32 [4096, 2048], P(('ep', 'ws'))
- grad_ffn_gain: float32 [2048], P(('ep', 'ws'))
- grad_router: float32 [2048, 32], P(('ep', 'ws'))
- grad_gate: float32 [32, 2048, 768], P(('ep', 'ws'))
- grad_up: float32 [32, 2048, 768], P(('ep', 'ws'))
- grad_down: float32 [32, 768, 2048], P(('ep', 'ws'))
- root_mean_squares: float32 [4], replicated
Inputs may be any that keep to these rules, and one draw needn't show every extreme that they name: `routes`: in each aligned block of 256 rows (the rows of one device) every expert is named by at most 80 rows, and one expert, the same in every block, is named by exactly 80 rows of each block; the 8 experts of a row differ.
All inputs are finite; a program needn't handle non-finite values.
Results may differ from a plain program's by a relative error of at most 0.017.
Values may be sent and summed in bfloat16 or wider, within the bound.
A program may use at most 384 MiB of HBM per device.

v0:
```python
import jax
import jax.numpy as jnp
from jax import lax
from jax.sharding import PartitionSpec as P

BLOCK = 256


epsilon = 1e-06
rope_base = 1000000.0
masked_value = -1e30


def plain_product(left, right):
    return jnp.dot(left, right, preferred_element_type=jnp.float32)


def contract_rows(left, right):
    return lax.dot_general(
        left, right, (((0,), (0,)), ((), ())), preferred_element_type=jnp.float32
    )


def contract_last(left, right):
    return lax.dot_general(
        left, right, (((1,), (1,)), ((), ())), preferred_element_type=jnp.float32
    )


def rope_tables(positions, head_size):
    indices = jnp.arange(head_size // 2, dtype=jnp.float32)
    frequency = rope_base ** (-2.0 * indices / head_size)
    angles = positions.astype(jnp.float32)[:, None] * frequency[None, :]
    angles = jnp.concatenate([angles, angles], axis=-1)
    return (jnp.cos(angles)[:, None, :], jnp.sin(angles)[:, None, :])


def rotate(layer_inputs, cosine_table, sine_table):
    halfway = layer_inputs.shape[-1] // 2
    turned = jnp.concatenate([-layer_inputs[..., halfway:], layer_inputs[..., :halfway]], axis=-1)
    return layer_inputs * cosine_table + turned * sine_table


def unrotate(gradients, cosine_table, sine_table):
    halfway = gradients.shape[-1] // 2
    sined = gradients * sine_table
    return gradients * cosine_table + jnp.concatenate(
        [sined[..., halfway:], -sined[..., :halfway]], axis=-1
    )


def norm_forward(layer_inputs):
    scaling = lax.rsqrt(jnp.mean(layer_inputs * layer_inputs, axis=-1, keepdims=True) + epsilon)
    return (layer_inputs * scaling, scaling)


def norm_backward(grad_normed, normed, scaling):
    return scaling * (grad_normed - normed * jnp.mean(grad_normed * normed, axis=-1, keepdims=True))


def local(
    hidden_in,
    attn_gain,
    w_query,
    key_projection,
    value_projection,
    query_gain,
    key_gain,
    w_output,
    ffn_gain,
    w_router,
    routes,
    w_gate,
    w_up,
    w_down,
    cotangent,
):
    tokens_here = hidden_in.shape[0]
    model_width = hidden_in.shape[1]
    head_size = query_gain.shape[0]
    top_count = routes.shape[1]
    shard_count = lax.axis_size("ws")
    device_count = lax.axis_size(("ep", "ws"))
    local_experts = w_gate.shape[0]
    expert_count = local_experts * device_count
    capacity = 5 * tokens_here * top_count // (4 * expert_count)
    seq_length = tokens_here * shard_count
    head_count = w_query.shape[1] // head_size
    kv_heads = key_projection.shape[1] // head_size
    group_size = head_count // kv_heads
    factor = head_size ** (-0.5)
    gathered = (
        lax.all_gather(attn_gain, "ws", axis=0, tiled=True),
        lax.all_gather(w_query, "ws", axis=0, tiled=True),
        lax.all_gather(key_projection, "ws", axis=0, tiled=True),
        lax.all_gather(value_projection, "ws", axis=0, tiled=True),
        lax.all_gather(w_output, "ws", axis=0, tiled=True),
        lax.all_gather(ffn_gain, "ws", axis=0, tiled=True),
        lax.all_gather(w_router, "ws", axis=0, tiled=True),
    )
    attn_full, query_full, key_full, value_full, output_full, ffn_full, router_full = gathered
    attn_scale = attn_full.astype(jnp.float32)
    ffn_scale = ffn_full.astype(jnp.float32)
    source = hidden_in.astype(jnp.float32)
    first_normed, first_scale = norm_forward(source)
    first_input = (first_normed * attn_scale).astype(jnp.bfloat16)
    query_raw = plain_product(first_input, query_full).reshape(tokens_here, head_count, head_size)
    key_raw = plain_product(first_input, key_full).reshape(tokens_here, kv_heads, head_size)
    value_rows = plain_product(first_input, value_full).astype(jnp.bfloat16)
    query_positions = lax.axis_index("ws") * tokens_here + jnp.arange(tokens_here, dtype=jnp.int32)
    cosine_table, sine_table = rope_tables(query_positions, head_size)
    query_normed, query_scale = norm_forward(query_raw)
    query_rot = rotate(query_normed * query_gain, cosine_table, sine_table).astype(jnp.bfloat16)
    key_normed, key_scale = norm_forward(key_raw)
    key_rot = rotate(key_normed * key_gain, cosine_table, sine_table).astype(jnp.bfloat16)
    all_keys, all_values = (
        lax.all_gather(
            key_rot.reshape(tokens_here, kv_heads * head_size), "ws", axis=0, tiled=True
        ),
        lax.all_gather(value_rows, "ws", axis=0, tiled=True),
    )
    all_keys = all_keys.reshape(seq_length, kv_heads, head_size)
    all_values = all_values.reshape(seq_length, kv_heads, head_size)
    key_blocks = jnp.arange(seq_length, dtype=jnp.int32) // BLOCK
    allowed = key_blocks[None, :] <= (query_positions // BLOCK)[:, None]
    attended_list = []
    lse_list = []
    for head_group in range(kv_heads):
        query_rows_all = query_rot[:, head_group * group_size : (head_group + 1) * group_size, :]
        keys_here = all_keys[:, head_group, :]
        values_here = all_values[:, head_group, :]
        scores = (
            jnp.einsum("qgd,kd->gqk", query_rows_all, keys_here, preferred_element_type=jnp.float32)
            * factor
        )
        scores = jnp.where(allowed[None], scores, masked_value)
        row_peaks = jnp.max(scores, axis=-1, keepdims=True)
        exponent = jnp.exp(scores - row_peaks)
        totals = jnp.sum(exponent, axis=-1, keepdims=True)
        probabilities = (exponent / totals).astype(jnp.bfloat16)
        attended_list.append(
            jnp.einsum(
                "gqk,kd->qgd", probabilities, values_here, preferred_element_type=jnp.float32
            )
        )
        lse_list.append(row_peaks + jnp.log(totals))
    attended = (
        jnp.concatenate(attended_list, axis=1)
        .reshape(tokens_here, head_count * head_size)
        .astype(jnp.bfloat16)
    )
    branch = plain_product(attended, output_full)
    middle = source + branch
    second_normed, second_scale = norm_forward(middle)
    second_input = (second_normed * ffn_scale).astype(jnp.bfloat16)
    logits = plain_product(second_input, router_full)
    expert_ids = jnp.arange(expert_count, dtype=jnp.int32)
    route_hits = routes[:, :, None] == expert_ids[None, None, :]
    picked = jnp.sum(jnp.where(route_hits, logits[:, None, :], 0.0), axis=2)
    shifted = jnp.exp(picked - jnp.max(picked, axis=1, keepdims=True))
    shares = shifted / jnp.sum(shifted, axis=1, keepdims=True)
    pair_count = tokens_here * top_count
    pair_expert = routes.reshape(pair_count)
    pair_hits = (pair_expert[:, None] == expert_ids[None, :]).astype(jnp.int32)
    earlier = jnp.cumsum(pair_hits, axis=0) - pair_hits
    pair_rank = jnp.sum(earlier * pair_hits, axis=1)
    pair_slot = pair_expert * capacity + pair_rank
    slot_pair = (
        jnp.full((expert_count * capacity,), pair_count, jnp.int32)
        .at[pair_slot]
        .set(jnp.arange(pair_count, dtype=jnp.int32))
    )
    slot_token = jnp.where(slot_pair < pair_count, slot_pair // top_count, tokens_here)
    padded_input = jnp.concatenate(
        [second_input, jnp.zeros((1, model_width), jnp.bfloat16)], axis=0
    )
    send_rows = padded_input[slot_token].reshape(
        device_count, local_experts * capacity, model_width
    )
    received = lax.all_to_all(send_rows, ("ep", "ws"), split_axis=0, concat_axis=0, tiled=True)
    expert_rows = received.reshape(device_count, local_experts, capacity, model_width)
    expert_index = 0
    rows_in = expert_rows[:, expert_index].reshape(device_count * capacity, model_width)
    gate_values = plain_product(rows_in, w_gate[expert_index])
    up_values = plain_product(rows_in, w_up[expert_index])
    hidden_units = (gate_values / (1.0 + jnp.exp(-gate_values)) * up_values).astype(jnp.bfloat16)
    output_list = [
        plain_product(hidden_units, w_down[expert_index])
        .astype(jnp.bfloat16)
        .reshape(device_count, capacity, model_width)
    ]
    rows_list = [rows_in]
    gate_list = [gate_values]
    up_list = [up_values]
    units_list = [hidden_units]
    output_rows = jnp.stack(output_list, axis=1).reshape(
        device_count, local_experts * capacity, model_width
    )
    returned = lax.all_to_all(
        output_rows, ("ep", "ws"), split_axis=0, concat_axis=0, tiled=True
    ).reshape(expert_count * capacity, model_width)
    pair_out = returned[pair_slot].reshape(tokens_here, top_count, model_width)
    expert_sum = jnp.sum(shares[:, :, None] * pair_out.astype(jnp.float32), axis=1)
    hidden_out = (middle + expert_sum).astype(jnp.bfloat16)
    grad_top = cotangent.astype(jnp.float32)
    share_grad = jnp.sum(pair_out.astype(jnp.float32) * grad_top[:, None, :], axis=2)
    pair_grad = (
        (shares[:, :, None] * grad_top[:, None, :])
        .astype(jnp.bfloat16)
        .reshape(pair_count, model_width)
    )
    padded_grad = jnp.concatenate([pair_grad, jnp.zeros((1, model_width), jnp.bfloat16)], axis=0)
    send_grads = padded_grad[slot_pair].reshape(device_count, local_experts * capacity, model_width)
    grads_in = lax.all_to_all(send_grads, ("ep", "ws"), split_axis=0, concat_axis=0, tiled=True)
    grads_in = grads_in.reshape(device_count, local_experts, capacity, model_width)
    expert_index = 0
    out_grad = grads_in[:, expert_index].reshape(device_count * capacity, model_width)
    hidden_grad = contract_last(out_grad, w_down[expert_index])
    down_grads = [contract_rows(units_list[expert_index], out_grad)]
    gate_values = gate_list[expert_index]
    sigmoid_gate = 1.0 / (1.0 + jnp.exp(-gate_values))
    gate_grad = (
        hidden_grad
        * up_list[expert_index]
        * sigmoid_gate
        * (1.0 + gate_values * (1.0 - sigmoid_gate))
    ).astype(jnp.bfloat16)
    up_grad = (hidden_grad * (gate_values / (1.0 + jnp.exp(-gate_values)))).astype(jnp.bfloat16)
    gate_grads = [contract_rows(rows_list[expert_index], gate_grad)]
    up_grads = [contract_rows(rows_list[expert_index], up_grad)]
    row_grad = contract_last(gate_grad, w_gate[expert_index]) + contract_last(
        up_grad, w_up[expert_index]
    )
    row_grads = [row_grad.astype(jnp.bfloat16).reshape(device_count, capacity, model_width)]
    grad_gate = jnp.stack(gate_grads, axis=0)
    grad_up = jnp.stack(up_grads, axis=0)
    grad_down = jnp.stack(down_grads, axis=0)
    back_rows = jnp.stack(row_grads, axis=1).reshape(
        device_count, local_experts * capacity, model_width
    )
    rows_back = lax.all_to_all(
        back_rows, ("ep", "ws"), split_axis=0, concat_axis=0, tiled=True
    ).reshape(expert_count * capacity, model_width)
    pair_row_grad = rows_back[pair_slot].reshape(tokens_here, top_count, model_width)
    share_center = jnp.sum(shares * share_grad, axis=1, keepdims=True)
    picked_grad = shares * (share_grad - share_center)
    logit_grad = jnp.sum(jnp.where(route_hits, picked_grad[:, :, None], 0.0), axis=1).astype(
        jnp.bfloat16
    )
    router_grad = contract_rows(second_input, logit_grad)
    second_grad = jnp.sum(pair_row_grad.astype(jnp.float32), axis=1) + contract_last(
        logit_grad, router_full
    )
    ffn_gain_grad = jnp.sum(second_grad * second_normed, axis=0)
    middle_grad = grad_top + norm_backward(second_grad * ffn_scale, second_normed, second_scale)
    branch_grad = middle_grad.astype(jnp.bfloat16)
    output_grad = contract_rows(attended, branch_grad)
    attended_grad = (
        contract_last(branch_grad, output_full)
        .astype(jnp.bfloat16)
        .reshape(tokens_here, head_count, head_size)
    )
    query_grads = []
    key_grads = []
    value_grads = []
    for head_group in range(kv_heads):
        query_rows_all = query_rot[:, head_group * group_size : (head_group + 1) * group_size, :]
        keys_here = all_keys[:, head_group, :]
        values_here = all_values[:, head_group, :]
        head_grad = attended_grad[:, head_group * group_size : (head_group + 1) * group_size, :]
        scores = (
            jnp.einsum("qgd,kd->gqk", query_rows_all, keys_here, preferred_element_type=jnp.float32)
            * factor
        )
        scores = jnp.where(allowed[None], scores, masked_value)
        probabilities = jnp.exp(scores - lse_list[head_group])
        prob_grad = jnp.einsum(
            "qgd,kd->gqk", head_grad, values_here, preferred_element_type=jnp.float32
        )
        value_grads.append(
            jnp.einsum(
                "gqk,qgd->kd",
                probabilities.astype(jnp.bfloat16),
                head_grad,
                preferred_element_type=jnp.float32,
            )
        )
        center = jnp.sum(probabilities * prob_grad, axis=-1, keepdims=True)
        score_grad = (probabilities * (prob_grad - center)).astype(jnp.bfloat16)
        query_grads.append(
            jnp.einsum("gqk,kd->qgd", score_grad, keys_here, preferred_element_type=jnp.float32)
            * factor
        )
        key_grads.append(
            jnp.einsum(
                "gqk,qgd->kd", score_grad, query_rows_all, preferred_element_type=jnp.float32
            )
            * factor
        )
    key_grad_all = jnp.stack(key_grads, axis=1).reshape(seq_length, kv_heads * head_size)
    value_grad_all = jnp.stack(value_grads, axis=1).reshape(seq_length, kv_heads * head_size)
    key_sum, value_sum = (
        lax.psum_scatter(
            key_grad_all.astype(jnp.bfloat16), "ws", scatter_dimension=0, tiled=True
        ).astype(jnp.float32),
        lax.psum_scatter(
            value_grad_all.astype(jnp.bfloat16), "ws", scatter_dimension=0, tiled=True
        ).astype(jnp.float32),
    )
    query_rot_grad = jnp.concatenate(query_grads, axis=1)
    query_unrot = unrotate(query_rot_grad, cosine_table, sine_table)
    query_gain_grad = jnp.sum(query_unrot * query_normed, axis=(0, 1))
    query_raw_grad = (
        norm_backward(query_unrot * query_gain, query_normed, query_scale)
        .astype(jnp.bfloat16)
        .reshape(tokens_here, head_count * head_size)
    )
    key_unrot = unrotate(
        key_sum.reshape(tokens_here, kv_heads, head_size), cosine_table, sine_table
    )
    key_gain_grad = jnp.sum(key_unrot * key_normed, axis=(0, 1))
    key_raw_grad = (
        norm_backward(key_unrot * key_gain, key_normed, key_scale)
        .astype(jnp.bfloat16)
        .reshape(tokens_here, kv_heads * head_size)
    )
    value_grad_low = value_sum.astype(jnp.bfloat16)
    query_weight_grad = contract_rows(first_input, query_raw_grad)
    key_weight_grad = contract_rows(first_input, key_raw_grad)
    value_weight_grad = contract_rows(first_input, value_grad_low)
    first_grad = (
        contract_last(query_raw_grad, query_full)
        + contract_last(key_raw_grad, key_full)
        + contract_last(value_grad_low, value_full)
    )
    attn_gain_grad = jnp.sum(first_grad * first_normed, axis=0)
    grad_in = middle_grad + norm_backward(first_grad * attn_scale, first_normed, first_scale)
    summed = (
        lax.psum_scatter(attn_gain_grad, ("ep", "ws"), scatter_dimension=0, tiled=True),
        lax.psum_scatter(query_weight_grad, ("ep", "ws"), scatter_dimension=0, tiled=True),
        lax.psum_scatter(key_weight_grad, ("ep", "ws"), scatter_dimension=0, tiled=True),
        lax.psum_scatter(value_weight_grad, ("ep", "ws"), scatter_dimension=0, tiled=True),
        lax.psum_scatter(output_grad, ("ep", "ws"), scatter_dimension=0, tiled=True),
        lax.psum_scatter(ffn_gain_grad, ("ep", "ws"), scatter_dimension=0, tiled=True),
        lax.psum_scatter(router_grad, ("ep", "ws"), scatter_dimension=0, tiled=True),
    )
    sum_attn_gain, sum_query, sum_key, sum_value, sum_output, sum_ffn_gain, sum_router = summed
    partial_squares = jnp.stack(
        [
            jnp.sum(source * source),
            jnp.sum(branch * branch),
            jnp.sum(expert_sum * expert_sum),
            jnp.sum(grad_in * grad_in),
        ]
    )
    square_total, query_gain_total, key_gain_total = lax.psum(
        (partial_squares, query_gain_grad, key_gain_grad), ("ep", "ws")
    )
    root_mean_squares = jnp.sqrt(square_total / (tokens_here * device_count * model_width))
    return (
        hidden_out,
        grad_in,
        sum_attn_gain,
        sum_query,
        sum_key,
        sum_value,
        query_gain_total,
        key_gain_total,
        sum_output,
        sum_ffn_gain,
        sum_router,
        grad_gate,
        grad_up,
        grad_down,
        root_mean_squares,
    )


def solution(mesh):
    return jax.shard_map(
        local,
        mesh=mesh,
        in_specs=(
            P(("ep", "ws"), None),
            P("ws"),
            P("ws", None),
            P("ws", None),
            P("ws", None),
            P(),
            P(),
            P("ws", None),
            P("ws"),
            P("ws", None),
            P(("ep", "ws"), None),
            P(("ep", "ws"), None, None),
            P(("ep", "ws"), None, None),
            P(("ep", "ws"), None, None),
            P(("ep", "ws"), None),
        ),
        out_specs=(
            P(("ep", "ws"), None),
            P(("ep", "ws"), None),
            P(("ep", "ws")),
            P(("ep", "ws"), None),
            P(("ep", "ws"), None),
            P(("ep", "ws"), None),
            P(),
            P(),
            P(("ep", "ws"), None),
            P(("ep", "ws")),
            P(("ep", "ws"), None),
            P(("ep", "ws"), None, None),
            P(("ep", "ws"), None, None),
            P(("ep", "ws"), None, None),
            P(),
        ),
        check_vma=False,
    )
```

profile of v0, /device:TPU:1, one launch (start us, length us, event | category | flops | bytes accessed | tf_op | source)
XLA Modules:
  0.0 2631.4 jit_solution(8854184210789970434)
XLA Ops:
  18.4 16.3 all-gather.9.cloned.1.call-done
  38.2 20.7 all-gather.13.cloned.1.call-done
  79.3 15.9 reduce-window.6
  121.3 82.7 %all-gather.17.cloned.1.call-done = bf16[2048,4096]{1,0:T(8,128)(2,1)} async-done(((bf16[512,4096]{1,0:T(8,128)(2,1)}), bf16[2048,4096]{1,0:T(8,128)(2,1)}) %all-gather.17.cloned.1.call-update) | async-done | bytes 16777232 | tf_op jit(solution)/shard_map/all_gather | solution.py:94
  263.7 47.7 %all-gather.19.cloned.1.call-done = bf16[4096,2048]{1,0:T(8,128)(2,1)} async-done(((bf16[1024,2048]{1,0:T(8,128)(2,1)}), bf16[4096,2048]{1,0:T(8,128)(2,1)}) %all-gather.19.cloned.1.call-update) | async-done | bytes 16777232 | tf_op jit(solution)/shard_map/all_gather | solution.py:97
  327.0 21.5 gather_fusion
  356.0 56.3 %all_gather.35 = bf16[2048,32]{0,1:T(8,128)(2,1)S(1)} all-gather(bf16[512,32]{0,1:T(8,128)(2,1)S(1)} %copy-done.84), channel_id=1, replica_groups=mesh['ep'=8,'ws'=4] {'ws'}, dimensions={0}, use_global_device_ids=true | all-gather | bytes 163840 | tf_op jit(solution)/shard_map/all_gather | solution.py:99
  430.6 24.7 gather_fusion.2
  455.3 127.7 %all-to-all-done = bf16[32,80,2048]{2,1,0:T(8,128)(2,1)} async-done(((bf16[32,80,2048]{2,1,0:T(8,128)(2,1)}), bf16[32,80,2048]{2,1,0:T(8,128)(2,1)}, u32[]{:S(2)}, u32[]{:S(2)}) %all-to-all-start) | async-done | bytes 10485792 | tf_op jit(solution)/shard_map/all_to_all | solution.py:180
  619.7 202.8 %all-to-all-done.2 = bf16[32,80,2048]{2,1,0:T(8,128)(2,1)} async-done(((bf16[32,80,2048]{2,1,0:T(8,128)(2,1)}), bf16[32,80,2048]{2,1,0:T(8,128)(2,1)}, u32[]{:S(2)}, u32[]{:S(2)}) %all-to-all-start.2) | async-done | bytes 10485792 | tf_op jit(solution)/shard_map/all_to_all | solution.py:214
  822.5 19.8 multiply_convert_fusion
  879.1 16.5 add_convert_fusion
  895.5 199.8 %all-to-all-done.1 = bf16[32,80,2048]{2,1,0:T(8,128)(2,1)} async-done(((bf16[32,80,2048]{2,1,0:T(8,128)(2,1)}), bf16[32,80,2048]{2,1,0:T(8,128)(2,1)}, u32[]{:S(2)}, u32[]{:S(2)}) %all-to-all-start.1) | async-done | bytes 10485792 | tf_op jit(solution)/shard_map/all_to_all | solution.py:199
  1105.6 21.8 gather_fusion.1
  1137.1 198.1 %all-to-all-done.3 = bf16[32,80,2048]{2,1,0:T(8,128)(2,1)} async-done(((bf16[32,80,2048]{2,1,0:T(8,128)(2,1)}), bf16[32,80,2048]{2,1,0:T(8,128)(2,1)}, u32[]{:S(2)}, u32[]{:S(2)}) %all-to-all-start.3) | async-done | bytes 10485792 | tf_op jit(solution)/shard_map/all_to_all | solution.py:241
  1335.2 21.8 gather_fusion.3
  1465.5 24.1 reduce-scatter.10.cloned.1.call-done
  1499.9 14.8 fusion.135
  1562.1 14.3 convolution_bitcast_fusion
  1634.6 42.9 %all-reduce.4 = (f32[2048]{0:T(1024)S(1)}, f32[128]{0:T(128)}, f32[128]{0:T(128)}, f32[2048]{0:T(1024)S(1)}, f32[4]{0:T(128)S(1)}) all-reduce(f32[2048]{0:T(1024)S(1)} %get-tuple-element.19, f32[128]{0:T(128)S(1)} %bitcast_reduce_fusion, f32[128]{0:T(128)S(1)} %bitcast_reduce_fusion.1, ...), channel_id=4, replica_groups=mesh['ep'=8,'ws'=4] {'ep','ws'}, use_global_device_ids=true, to_apply=%region_35.36.clone | all-reduce | flops 4356 | bytes 34848
  1679.2 82.2 %reduce-scatter.18.cloned.1.call-done = f32[64,512]{1,0:T(8,128)} async-done(((f32[2048,512]{1,0:T(8,128)}), f32[64,512]{1,0:T(8,128)}) %reduce-scatter.18.cloned.1.call-update) | async-done | bytes 131088 | tf_op jit(solution)/shard_map/reduce_scatter | solution.py:342
  1761.4 140.5 %reduce-scatter.16.cloned.1.call-done = f32[64,512]{1,0:T(8,128)} async-done(((f32[2048,512]{1,0:T(8,128)}), f32[64,512]{1,0:T(8,128)}) %reduce-scatter.16.cloned.1.call-update) | async-done | bytes 131088 | tf_op jit(solution)/shard_map/reduce_scatter | solution.py:341
  1901.9 362.2 %reduce-scatter.20.cloned.1.call-done = f32[128,2048]{1,0:T(8,128)} async-done(((f32[4096,2048]{1,0:T(8,128)}), f32[128,2048]{1,0:T(8,128)}) %reduce-scatter.20.cloned.1.call-update) | async-done | bytes 1048592 | tf_op jit(solution)/shard_map/reduce_scatter | solution.py:343
  2264.1 360.6 %reduce-scatter.14.cloned.1.call-done = f32[64,4096]{1,0:T(8,128)} async-done(((f32[2048,4096]{1,0:T(8,128)}), f32[64,4096]{1,0:T(8,128)}) %reduce-scatter.14.cloned.1.call-update) | async-done | bytes 1048592 | tf_op jit(solution)/shard_map/reduce_scatter | solution.py:340
  (449 shorter events, 479.6 us)
Async XLA Ops:
  7.2 815.3 %copy-start = (bf16[1,768,2048]{2,1,0:T(8,128)(2,1)S(1)}, bf16[1,768,2048]{2,1,0:T(8,128)(2,1)}, u32[]{:S(2)}) copy-start(bf16[1,768,2048]{2,1,0:T(8,128)(2,1)} %param.28) | copy-start | bytes 9437188
  7.2 27.5 %all-gather.9.cloned.1.call-start = ((), (), s32[]{:S(2)}) async-start(), calls=%async_computation.11 | async-start | bytes 2621440 | tf_op jit(solution)/shard_map/all_gather | solution.py:96
  7.9 50.9 %all-gather.13.cloned.1.call-start = ((), (), s32[]{:S(2)}) async-start(), calls=%async_computation.13 | async-start | bytes 2621440 | tf_op jit(solution)/shard_map/all_gather | solution.py:95
  8.7 102.6 %all-gather.11.cloned.1.call-start = ((), (), s32[]{:S(2)}) async-start(), calls=%async_computation.12 | async-start | bytes 1310720 | tf_op jit(solution)/shard_map/all_gather | solution.py:120
  15.4 188.6 %copy-start.58 = (f32[4,1,512]{2,1,0:T(1,128)}, f32[4,1,512]{2,1,0:T(1,128)S(1)}, u32[]{:S(2)}) copy-start(f32[4,1,512]{2,1,0:T(1,128)S(1)} %convert_element_type.197) | copy-start | bytes 24580
  16.1 51.6 %copy-start.39 = (f32[256,128]{1,0:T(8,128)}, f32[256,128]{1,0:T(8,128)S(1)}, u32[]{:S(2)}) copy-start(f32[256,128]{1,0:T(8,128)S(1)} %get-tuple-element.63) | copy-start | bytes 393220
  16.1 208.8 %copy-start.37 = (f32[256,128]{1,0:T(8,128)}, f32[256,128]{1,0:T(8,128)S(1)}, u32[]{:S(2)}) copy-start(f32[256,128]{1,0:T(8,128)S(1)} %get-tuple-element.62) | copy-start | bytes 393220
  38.1 75.5 %all-gather.15.cloned.1.call-start = ((), (), s32[]{:S(2)}) async-start(), calls=%async_computation.14 | async-start | bytes 1310720 | tf_op jit(solution)/shard_map/all_gather | solution.py:117
  70.3 133.7 %all-gather.17.cloned.1.call-start = ((), (), s32[]{:S(2)}) async-start(), calls=%async_computation.15 | async-start | bytes 20971520 | tf_op jit(solution)/shard_map/all_gather | solution.py:94
  70.9 240.4 %all-gather.19.cloned.1.call-start = ((), (), s32[]{:S(2)}) async-start(), calls=%async_computation.16 | async-start | bytes 20971520 | tf_op jit(solution)/shard_map/all_gather | solution.py:97
  77.7 245.7 %copy-start.66 = (f32[4,1,512]{2,1,0:T(1,128)}, f32[4,1,512]{2,1,0:T(1,128)S(1)}, u32[]{:S(2)}) copy-start(f32[4,1,512]{2,1,0:T(1,128)S(1)} %convert_element_type.198) | copy-start | bytes 24580
  348.5 234.5 %all-to-all-start = ((bf16[32,80,2048]{2,1,0:T(8,128)(2,1)}), bf16[32,80,2048]{2,1,0:T(8,128)(2,1)}, u32[]{:S(2)}, u32[]{:S(2)}) async-start(bf16[32,80,2048]{2,1,0:T(8,128)(2,1)} %bitcast.433), calls=%async_computation | async-start | bytes 20971520 | tf_op jit(solution)/shard_map/all_to_all | solution.py:180
  353.2 61.4 %copy-start.69 = (s32[256,8]{0,1:T(8,128)S(1)}, s32[256,8]{0,1:T(8,128)}, u32[]{:S(2)}) copy-start(s32[256,8]{0,1:T(8,128)} %param.25) | copy-start | bytes 24580
  583.0 239.5 %all-to-all-start.2 = ((bf16[32,80,2048]{2,1,0:T(8,128)(2,1)}), bf16[32,80,2048]{2,1,0:T(8,128)(2,1)}, u32[]{:S(2)}, u32[]{:S(2)}) async-start(bf16[32,80,2048]{2,1,0:T(8,128)(2,1)} %bitcast.434), calls=%async_computation.2 | async-start | bytes 20971520 | tf_op jit(solution)/shard_map/all_to_all | solution.py:214
  855.7 239.7 %all-to-all-start.1 = ((bf16[32,80,2048]{2,1,0:T(8,128)(2,1)}), bf16[32,80,2048]{2,1,0:T(8,128)(2,1)}, u32[]{:S(2)}, u32[]{:S(2)}) async-start(bf16[32,80,2048]{2,1,0:T(8,128)(2,1)} %bitcast.441), calls=%async_computation.1 | async-start | bytes 20971520 | tf_op jit(solution)/shard_map/all_to_all | solution.py:199
  1095.4 239.8 %all-to-all-start.3 = ((bf16[32,80,2048]{2,1,0:T(8,128)(2,1)}), bf16[32,80,2048]{2,1,0:T(8,128)(2,1)}, u32[]{:S(2)}, u32[]{:S(2)}) async-start(bf16[32,80,2048]{2,1,0:T(8,128)(2,1)} %bitcast.440), calls=%async_computation.3 | async-start | bytes 20971520 | tf_op jit(solution)/shard_map/all_to_all | solution.py:241
  1105.4 356.0 %reduce-scatter.12.cloned.1.call-start = ((), (), s32[]{:S(2)}) async-start(), calls=%async_computation.18 | async-start | bytes 1310720 | tf_op jit(solution)/shard_map/reduce_scatter | solution.py:306
  1419.1 70.5 %reduce-scatter.10.cloned.1.call-start = ((), (), s32[]{:S(2)}) async-start(), calls=%async_computation.17 | async-start | bytes 1310720 | tf_op jit(solution)/shard_map/reduce_scatter | solution.py:303
  1459.7 161.8 %reduce-scatter.22.cloned.1.call-start = ((), (), s32[]{:S(2)}) async-start(), calls=%async_computation.23 | async-start | bytes 1081344
  1461.3 300.1 %reduce-scatter.18.cloned.1.call-start = ((), (), s32[]{:S(2)}) async-start(), calls=%async_computation.21 | async-start | bytes 4325376 | tf_op jit(solution)/shard_map/reduce_scatter | solution.py:342
  1465.3 436.6 %reduce-scatter.16.cloned.1.call-start = ((), (), s32[]{:S(2)}) async-start(), calls=%async_computation.20 | async-start | bytes 4325376 | tf_op jit(solution)/shard_map/reduce_scatter | solution.py:341
  1498.3 765.7 %reduce-scatter.20.cloned.1.call-start = ((), (), s32[]{:S(2)}) async-start(), calls=%async_computation.22 | async-start | bytes 34603008 | tf_op jit(solution)/shard_map/reduce_scatter | solution.py:343
  1514.8 1109.9 %reduce-scatter.14.cloned.1.call-start = ((), (), s32[]{:S(2)}) async-start(), calls=%async_computation.19 | async-start | bytes 34603008 | tf_op jit(solution)/shard_map/reduce_scatter | solution.py:340
  1626.0 998.6 %copy-start.1 = (bf16[1,768,2048]{2,1,0:T(8,128)(2,1)S(1)}, bf16[1,768,2048]{2,1,0:T(8,128)(2,1)}, u32[]{:S(2)}) copy-start(bf16[1,768,2048]{2,1,0:T(8,128)(2,1)} %param.28) | copy-start | bytes 9437188
  (117 other events, 1095.6 us)
Sparse Core Ops, SparseCore 0:
  9.6 25.0 all-gather.8
  36.3 22.5 all-gather.12
  61.0 16.7 all-gather.10
  79.8 16.7 all-gather.14
  98.0 105.9 all-gather.16
  205.4 105.9 all-gather.18
  1419.3 29.4 reduce-scatter.11
  1459.8 29.7 reduce-scatter.9
  1491.9 129.5 reduce-scatter.21
  1624.2 137.1 reduce-scatter.17
  1764.4 137.4 reduce-scatter.15
  1904.7 359.3 reduce-scatter.19
  2267.0 357.5 reduce-scatter.13
where the time goes:
time: 2640 us; the launch traced here: 2630 us
  waiting for transfers between devices  1880 us (71%)
  matrix products  299 us (11%)
  local copies, waits for them, and re-layouts  157 us (6%)
  other arithmetic  138 us (5%)
  blocking collectives  110 us (4%)
  starting transfers between devices  34.7 us (1%)
    reduce_scatter x1, waiting for transfers between devices, local(): lax.psum_scatter(output_grad, ('ep', 'ws'), scatter_dimension=0, tiled=True)  362 us
    reduce_scatter x1, waiting for transfers between devices, local(): lax.psum_scatter(query_weight_grad, ('ep', 'ws'), scatter_dimension=0, ti...  361 us
    all_to_all x1, waiting for transfers between devices, local(): lax.all_to_all(send_grads, ('ep', 'ws'), split_axis=0, concat_axis=0, til...  203 us
    all_to_all x1, waiting for transfers between devices, local(): lax.all_to_all(output_rows, ('ep', 'ws'), split_axis=0, concat_axis=0, ti...  200 us
    all_to_all x1, waiting for transfers between devices, local(): lax.all_to_all(back_rows, ('ep', 'ws'), split_axis=0, concat_axis=0, tile...  198 us
    reduce_scatter x1, waiting for transfers between devices, local(): lax.psum_scatter(key_weight_grad, ('ep', 'ws'), scatter_dimension=0, tile...  140 us
    all_to_all x1, waiting for transfers between devices, local(): lax.all_to_all(send_rows, ('ep', 'ws'), split_axis=0, concat_axis=0, tile...  128 us
    all_gather x1, waiting for transfers between devices, local(): lax.all_gather(w_query, 'ws', axis=0, tiled=True)  82.7 us
  transfers between devices with their start and end apart: 17, of which 14 were waited for; matrix products, arithmetic and copies ran while one was open for 16% of the time, Pallas kernels for 0%

commit v1 on v0

v1 whole, which is shorter than its diff:
```python
import functools

import jax
import jax.numpy as jnp
from jax import lax
from jax.experimental import pallas as pl
from jax.experimental.pallas import tpu as pltpu
from jax.sharding import Mesh
from jax.sharding import PartitionSpec as P

BLOCK = 256
EPS = 1e-06
ROPE_BASE = 1000000.0
F32 = jnp.float32
BF16 = jnp.bfloat16
VMEM_LIMIT = 60 * 1024 * 1024


def dot(left, right):
    return jnp.dot(left, right, preferred_element_type=F32)


def dot_tn(left, right):
    return lax.dot_general(left, right, (((0,), (0,)), ((), ())), preferred_element_type=F32)


def dot_nt(left, right):
    return lax.dot_general(left, right, (((1,), (1,)), ((), ())), preferred_element_type=F32)


def rope_tables(seq_length, head_size):
    indices = jnp.arange(head_size // 2, dtype=F32)
    frequency = ROPE_BASE ** (-2.0 * indices / head_size)
    angles = jnp.arange(seq_length, dtype=F32)[:, None] * frequency[None, :]
    cosine, sine = jnp.cos(angles), jnp.sin(angles)
    return jnp.concatenate([cosine, cosine], axis=1), jnp.concatenate([-sine, sine], axis=1)


def norm_forward(values):
    scaling = lax.rsqrt(jnp.mean(values * values, axis=-1, keepdims=True) + EPS)
    return values * scaling, scaling


def norm_backward(grad_normed, normed, scaling):
    return scaling * (grad_normed - normed * jnp.mean(grad_normed * normed, axis=-1, keepdims=True))


def half_turn(values):
    return pltpu.roll(values, values.shape[-1] // 2, 1)


def rotate(values, cosine, signed_sine):
    return values * cosine + half_turn(values) * signed_sine


def unrotate(grads, cosine, signed_sine):
    return grads * cosine - half_turn(grads) * signed_sine


def attention_forward(
    heads_a_step, hidden_ref, gain_ref, wq_ref, wkv_ref, query_gain_ref, key_gain_ref, cosine_ref, sine_ref, wo_ref,
    input_ref, query_raw_ref, key_raw_ref, value_ref, attended_ref, branch_ref, total_ref, key_rot_ref,
):
    step = pl.program_id(0)
    head_size = cosine_ref.shape[1]
    seq_length = cosine_ref.shape[0]
    blocks = seq_length // BLOCK
    factor = head_size ** (-0.5)

    @pl.when(step == 0)
    def _():
        for block in range(blocks):
            rows = pl.ds(block * BLOCK, BLOCK)
            normed, _ = norm_forward(hidden_ref[rows, :].astype(F32))
            first_input = (normed * gain_ref[...]).astype(BF16)
            input_ref[rows, :] = first_input
            key_value = dot(first_input, wkv_ref[...])
            key_raw = key_value[:, :head_size]
            key_raw_ref[rows, :] = key_raw
            value_ref[rows, :] = key_value[:, head_size:].astype(BF16)
            key_normed, _ = norm_forward(key_raw)
            key_rot_ref[rows, :] = rotate(
                key_normed * key_gain_ref[...], cosine_ref[rows, :], sine_ref[rows, :]
            ).astype(BF16)

    for block in range(blocks):
        rows = pl.ds(block * BLOCK, BLOCK)
        seen = pl.ds(0, (block + 1) * BLOCK)
        query_raw = dot(input_ref[rows, :], wq_ref[...])
        query_raw_ref[rows, :] = query_raw
        for head in range(heads_a_step):
            columns = slice(head * head_size, (head + 1) * head_size)
            query_normed, _ = norm_forward(query_raw[:, columns])
            query_rot = rotate(
                query_normed * query_gain_ref[...], cosine_ref[rows, :], sine_ref[rows, :]
            ).astype(BF16)
            scores = dot_nt(query_rot, key_rot_ref[seen, :]) * factor
            exponent = jnp.exp(scores - jnp.max(scores, axis=-1, keepdims=True))
            probs = (exponent / jnp.sum(exponent, axis=-1, keepdims=True)).astype(BF16)
            attended_ref[rows, columns] = dot(probs, value_ref[seen, :]).astype(BF16)
        partial = dot(attended_ref[rows, :], wo_ref[...])

        @pl.when(step == 0)
        def _():
            total_ref[rows, :] = partial

        @pl.when(step > 0)
        def _():
            total_ref[rows, :] += partial

    @pl.when(step == pl.num_programs(0) - 1)
    def _():
        branch_ref[...] = total_ref[...].astype(BF16)


def attention_backward(
    heads_a_step, grad_ref, wo_ref, attended_ref, query_raw_ref, key_raw_ref, value_ref, input_ref, wq_ref, wkv_ref,
    query_gain_ref, key_gain_ref, cosine_ref, sine_ref,
    wo_grad_ref, wq_grad_ref, wkv_grad_ref, first_grad_ref, query_gain_grad_ref, key_gain_grad_ref,
    total_ref, key_rot_ref, key_grad_ref, value_grad_ref, query_grad_ref, turned_ref,
):
    step = pl.program_id(0)
    head_size = cosine_ref.shape[1]
    seq_length = cosine_ref.shape[0]
    blocks = seq_length // BLOCK
    factor = head_size ** (-0.5)

    @pl.when(step == 0)
    def _():
        key_normed, _ = norm_forward(key_raw_ref[...])
        key_rot_ref[...] = rotate(key_normed * key_gain_ref[...], cosine_ref[...], sine_ref[...]).astype(BF16)
        key_grad_ref[...] = jnp.zeros_like(key_grad_ref)
        value_grad_ref[...] = jnp.zeros_like(value_grad_ref)
        query_gain_grad_ref[...] = jnp.zeros_like(query_gain_grad_ref)
        for block in range(blocks):
            rows = pl.ds(block * BLOCK, BLOCK)
            turned_ref[:, rows] = input_ref[rows, :].T

    wo_grad_ref[...] = dot_tn(attended_ref[...], grad_ref[...]).astype(BF16)
    for block in range(blocks):
        rows = pl.ds(block * BLOCK, BLOCK)
        seen = pl.ds(0, (block + 1) * BLOCK)
        attended_grad = dot_nt(grad_ref[rows, :], wo_ref[...]).astype(BF16)
        for head in range(heads_a_step):
            columns = slice(head * head_size, (head + 1) * head_size)
            query_normed, query_scale = norm_forward(query_raw_ref[rows, columns])
            cosine, sine = cosine_ref[rows, :], sine_ref[rows, :]
            query_rot = rotate(query_normed * query_gain_ref[...], cosine, sine).astype(BF16)
            head_grad = attended_grad[:, columns]
            keys, values = key_rot_ref[seen, :], value_ref[seen, :]
            scores = dot_nt(query_rot, keys) * factor
            exponent = jnp.exp(scores - jnp.max(scores, axis=-1, keepdims=True))
            probs = exponent / jnp.sum(exponent, axis=-1, keepdims=True)
            prob_grad = dot_nt(head_grad, values)
            value_grad_ref[seen, :] += dot_tn(probs.astype(BF16), head_grad)
            center = jnp.sum(probs * prob_grad, axis=-1, keepdims=True)
            score_grad = (probs * (prob_grad - center)).astype(BF16)
            key_grad_ref[seen, :] += dot_tn(score_grad, query_rot) * factor
            query_rot_grad = dot(score_grad, keys) * factor
            unrotated = unrotate(query_rot_grad, cosine, sine)
            query_gain_grad_ref[0:1, :] += jnp.sum(unrotated * query_normed, axis=0, keepdims=True)
            query_grad_ref[rows, columns] = norm_backward(
                unrotated * query_gain_ref[...], query_normed, query_scale
            ).astype(BF16)
        partial = dot_nt(query_grad_ref[rows, :], wq_ref[...])

        @pl.when(step == 0)
        def _():
            total_ref[rows, :] = partial

        @pl.when(step > 0)
        def _():
            total_ref[rows, :] += partial

    wq_grad_ref[...] = dot(turned_ref[...], query_grad_ref[...]).astype(BF16)

    @pl.when(step == pl.num_programs(0) - 1)
    def _():
        key_normed, key_scale = norm_forward(key_raw_ref[...])
        unrotated = unrotate(key_grad_ref[...], cosine_ref[...], sine_ref[...])
        key_gain_grad_ref[...] = jnp.zeros_like(key_gain_grad_ref)
        key_gain_grad_ref[0:1, :] = jnp.sum(unrotated * key_normed, axis=0, keepdims=True)
        key_grad = norm_backward(unrotated * key_gain_ref[...], key_normed, key_scale)
        query_grad_ref[:, :head_size] = key_grad.astype(BF16)
        query_grad_ref[:, head_size : 2 * head_size] = value_grad_ref[...].astype(BF16)
        both = query_grad_ref[:, : 2 * head_size]
        wkv_grad_ref[...] = dot(turned_ref[...], both).astype(BF16)
        for block in range(blocks):
            rows = pl.ds(block * BLOCK, BLOCK)
            first_grad_ref[rows, :] = (
                total_ref[rows, :] + dot_nt(query_grad_ref[rows, : 2 * head_size], wkv_ref[...])
            ).astype(BF16)


def whole(shape):
    return pl.BlockSpec(shape, lambda step: (0,) * len(shape), pipeline_mode=pl.Buffered(1))


def run_forward(hidden_all, gain, weights, wo, query_gain, key_gain, cosine, sine):
    seq_length, width = hidden_all.shape
    head_size = query_gain.shape[1]
    heads_here = wo.shape[0] // head_size
    pair = 2
    wide = pair * head_size
    steps = heads_here // pair
    return pl.pallas_call(
        functools.partial(attention_forward, pair),
        grid=(steps,),
        in_specs=[
            whole((seq_length, width)),
            whole((1, width)),
            pl.BlockSpec((width, wide), lambda step: (0, step)),
            pl.BlockSpec((width, wide), lambda step: (0, steps), pipeline_mode=pl.Buffered(1)),
            whole((1, head_size)),
            whole((1, head_size)),
            whole((seq_length, head_size)),
            whole((seq_length, head_size)),
            pl.BlockSpec((wide, width), lambda step: (step, 0)),
        ],
        out_specs=[
            whole((seq_length, width)),
            pl.BlockSpec((seq_length, wide), lambda step: (0, step)),
            whole((seq_length, head_size)),
            whole((seq_length, head_size)),
            pl.BlockSpec((seq_length, wide), lambda step: (0, step)),
            whole((seq_length, width)),
        ],
        out_shape=[
            jax.ShapeDtypeStruct((seq_length, width), BF16),
            jax.ShapeDtypeStruct((seq_length, heads_here * head_size), F32),
            jax.ShapeDtypeStruct((seq_length, head_size), F32),
            jax.ShapeDtypeStruct((seq_length, head_size), BF16),
            jax.ShapeDtypeStruct((seq_length, heads_here * head_size), BF16),
            jax.ShapeDtypeStruct((seq_length, width), BF16),
        ],
        scratch_shapes=[
            pltpu.VMEM((seq_length, width), F32),
            pltpu.VMEM((seq_length, head_size), BF16),
        ],
        compiler_params=pltpu.CompilerParams(vmem_limit_bytes=VMEM_LIMIT),
        cost_estimate=pl.CostEstimate(flops=16 * 10**9, bytes_accessed=40 * 10**6, transcendentals=6 * 10**6),
    )(hidden_all, gain, weights, weights, query_gain, key_gain, cosine, sine, wo)


def run_backward(grad_all, wo, attended, query_raw, key_raw, value, first_input, weights, query_gain, key_gain, cosine, sine):
    seq_length, width = grad_all.shape
    head_size = query_gain.shape[1]
    heads_here = wo.shape[0] // head_size
    pair = 2
    wide = pair * head_size
    steps = heads_here // pair
    return pl.pallas_call(
        functools.partial(attention_backward, pair),
        grid=(steps,),
        in_specs=[
            whole((seq_length, width)),
            pl.BlockSpec((wide, width), lambda step: (step, 0)),
            pl.BlockSpec((seq_length, wide), lambda step: (0, step)),
            pl.BlockSpec((seq_length, wide), lambda step: (0, step)),
            whole((seq_length, head_size)),
            whole((seq_length, head_size)),
            whole((seq_length, width)),
            pl.BlockSpec((width, wide), lambda step: (0, step)),
            pl.BlockSpec((width, wide), lambda step: (0, steps), pipeline_mode=pl.Buffered(1)),
            whole((1, head_size)),
            whole((1, head_size)),
            whole((seq_length, head_size)),
            whole((seq_length, head_size)),
        ],
        out_specs=[
            pl.BlockSpec((wide, width), lambda step: (step, 0)),
            pl.BlockSpec((width, wide), lambda step: (0, step)),
            whole((width, wide)),
            whole((seq_length, width)),
            whole((8, head_size)),
            whole((8, head_size)),
        ],
        out_shape=[
            jax.ShapeDtypeStruct((heads_here * head_size, width), BF16),
            jax.ShapeDtypeStruct((width, heads_here * head_size), BF16),
            jax.ShapeDtypeStruct((width, wide), BF16),
            jax.ShapeDtypeStruct((seq_length, width), BF16),
            jax.ShapeDtypeStruct((8, head_size), F32),
            jax.ShapeDtypeStruct((8, head_size), F32),
        ],
        scratch_shapes=[
            pltpu.VMEM((seq_length, width), F32),
            pltpu.VMEM((seq_length, head_size), BF16),
            pltpu.VMEM((seq_length, head_size), F32),
            pltpu.VMEM((seq_length, head_size), F32),
            pltpu.VMEM((seq_length, wide), BF16),
            pltpu.VMEM((width, seq_length), BF16),
        ],
        compiler_params=pltpu.CompilerParams(vmem_limit_bytes=VMEM_LIMIT),
        cost_estimate=pl.CostEstimate(flops=35 * 10**9, bytes_accessed=60 * 10**6, transcendentals=6 * 10**6),
    )(grad_all, wo, attended, query_raw, key_raw, value, first_input, weights, weights, query_gain, key_gain, cosine, sine)


def local(
    hidden_in, attn_gain, w_query, key_projection, value_projection, query_gain, key_gain, w_output, ffn_gain, w_router,
    routes, w_gate, w_up, w_down, cotangent,
):
    tokens_here, width = hidden_in.shape
    head_size = query_gain.shape[0]
    top_count = routes.shape[1]
    planes, across, shards = lax.axis_size("z"), lax.axis_size("x"), lax.axis_size("w")
    rings = planes * across
    device_count = rings * shards
    in_plane = across * shards
    experts = device_count
    capacity = 5 * tokens_here * top_count // (4 * experts)
    seq_length = tokens_here * shards
    plane, column, shard = lax.axis_index("z"), lax.axis_index("x"), lax.axis_index("w")

    small = jnp.concatenate([w_router, attn_gain[:, None], ffn_gain[:, None]], axis=1)
    depth = w_query.shape[0]
    merged = jnp.concatenate(
        [
            w_query.reshape(depth, shards, -1),
            key_projection.reshape(depth, shards, -1),
            value_projection.reshape(depth, shards, -1),
        ],
        axis=2,
    ).reshape(depth, -1)
    hidden_all = lax.all_gather(hidden_in, "w", axis=0, tiled=True)
    small_all = lax.all_gather(small, "w", axis=0, tiled=True)
    weights = lax.all_to_all(merged, "w", split_axis=1, concat_axis=0, tiled=True)
    router_full = small_all[:, :experts]
    attn_scale = small_all[:, experts].astype(F32)[None, :]
    ffn_scale = small_all[:, experts + 1].astype(F32)[None, :]
    cosine, sine = rope_tables(seq_length, head_size)
    query_gain_row, key_gain_row = query_gain[None, :], key_gain[None, :]

    routes_z = lax.all_gather(routes, "z", axis=0, tiled=False)
    plane_experts = plane * in_plane + jnp.arange(in_plane, dtype=jnp.int32)
    hits = jnp.any(routes_z[:, :, :, None] == plane_experts[None, None, None, :], axis=2)
    lower = (
        jnp.arange(tokens_here)[:, None] > jnp.arange(tokens_here)[None, :]
    ).astype(BF16)
    ranks = jnp.einsum("st,zte->zse", lower, hits.astype(BF16), preferred_element_type=F32).astype(jnp.int32)
    ranks = jnp.where(hits, ranks, -1)
    chosen = (
        ranks.transpose(0, 2, 1)[:, :, None, :] == jnp.arange(capacity, dtype=jnp.int32)[None, None, :, None]
    )
    chosen_flat = chosen.reshape(planes, in_plane * capacity, tokens_here).astype(BF16)

    def send_out(rows_z):
        packed = jnp.einsum("zst,ztd->zsd", chosen_flat, rows_z, preferred_element_type=F32).astype(BF16)
        packed = packed.reshape(planes, in_plane, capacity, width).transpose(1, 0, 2, 3)
        got = lax.all_to_all(
            packed.reshape(in_plane, planes * capacity, width), ("x", "w"), split_axis=0, concat_axis=0, tiled=True
        )
        return got.reshape(in_plane * planes * capacity, width)

    def send_back(rows):
        got = lax.all_to_all(
            rows.reshape(in_plane, planes * capacity, width), ("x", "w"), split_axis=0, concat_axis=0, tiled=True
        )
        got = got.reshape(in_plane, planes, capacity, width).transpose(1, 0, 2, 3)
        got = got.reshape(planes, in_plane * capacity, width)
        summed = jnp.einsum("zst,zsd->ztd", chosen_flat, got, preferred_element_type=F32).astype(BF16)
        return lax.psum_scatter(summed.reshape(planes * tokens_here, width), "z", scatter_dimension=0, tiled=True)

    cotangent_z = lax.all_gather(cotangent, "z", axis=0, tiled=False)
    grads_in = send_out(cotangent_z)

    first_input, query_raw, key_raw, value, attended, branch_part = run_forward(
        hidden_all, attn_scale, weights, w_output, query_gain_row, key_gain_row, cosine, sine
    )
    branch = lax.psum_scatter(branch_part, "w", scatter_dimension=0, tiled=True).astype(F32)
    source = hidden_in.astype(F32)
    first_normed, first_scale = norm_forward(source)
    middle = source + branch
    second_normed, second_scale = norm_forward(middle)
    second_input = (second_normed * ffn_scale).astype(BF16)
    rows_z = lax.all_gather(second_input, "z", axis=0, tiled=False)
    rows_in = send_out(rows_z)

    logits = dot(second_input, router_full)
    expert_ids = jnp.arange(experts, dtype=jnp.int32)
    routed = jnp.any(routes[:, :, None] == expert_ids[None, None, :], axis=1)
    peaks = jnp.max(jnp.where(routed, logits, -jnp.inf), axis=1, keepdims=True)
    shifted = jnp.where(routed, jnp.exp(jnp.where(routed, logits - peaks, 0.0)), 0.0)
    shares = shifted / jnp.sum(shifted, axis=1, keepdims=True)
    shares_z = lax.all_to_all(
        shares.reshape(tokens_here, planes, in_plane).transpose(1, 2, 0), "z", split_axis=0, concat_axis=0, tiled=True
    )
    slot_shares = jnp.sum(jnp.where(chosen, shares_z[:, :, None, :], 0.0), axis=3)
    slot_shares = slot_shares.transpose(1, 0, 2).reshape(in_plane, planes * capacity)
    shares_in = lax.all_to_all(slot_shares, ("x", "w"), split_axis=0, concat_axis=0, tiled=True).reshape(-1, 1)

    gate = dot(rows_in, w_gate[0])
    up = dot(rows_in, w_up[0])
    sigmoid = 1.0 / (1.0 + jnp.exp(-gate))
    hidden_units = (gate * sigmoid * up).astype(BF16)
    pair_out = dot(hidden_units, w_down[0]).astype(BF16)
    top_rows = grads_in.astype(F32)
    pair_values = pair_out.astype(F32)
    share_grad_slots = jnp.sum(pair_values * top_rows, axis=1)
    weighted = (shares_in * pair_values).astype(BF16)
    pair_grad = (shares_in * top_rows).astype(BF16)
    hidden_grad = dot_nt(pair_grad, w_down[0])
    gate_grad = (hidden_grad * up * sigmoid * (1.0 + gate * (1.0 - sigmoid))).astype(BF16)
    up_grad = (hidden_grad * (gate * sigmoid)).astype(BF16)
    row_grad = (dot_nt(gate_grad, w_gate[0]) + dot_nt(up_grad, w_up[0])).astype(BF16)
    grad_down = dot_tn(hidden_units, pair_grad)[None]
    grad_gate = dot_tn(rows_in, gate_grad)[None]
    grad_up = dot_tn(rows_in, up_grad)[None]

    back_shares = lax.all_to_all(
        share_grad_slots.reshape(in_plane, planes * capacity), ("x", "w"), split_axis=0, concat_axis=0, tiled=True
    ).reshape(in_plane, planes, capacity).transpose(1, 0, 2)
    share_grad_z = jnp.sum(jnp.where(chosen, back_shares[:, :, :, None], 0.0), axis=2)
    share_grad = lax.all_to_all(share_grad_z, "z", split_axis=0, concat_axis=0, tiled=True)
    share_grad = share_grad.reshape(experts, tokens_here).T
    row_grad_sum = send_back(row_grad).astype(F32)
    expert_sum = send_back(weighted).astype(F32)
    hidden_out = (middle + expert_sum).astype(BF16)

    grad_top = cotangent.astype(F32)
    share_center = jnp.sum(shares * share_grad, axis=1, keepdims=True)
    logit_grad = (shares * (share_grad - share_center)).astype(BF16)
    router_grad = dot_tn(second_input, logit_grad)
    second_grad = row_grad_sum + dot_nt(logit_grad, router_full)
    ffn_gain_grad = jnp.sum(second_grad * second_normed, axis=0)
    middle_grad = grad_top + norm_backward(second_grad * ffn_scale, second_normed, second_scale)
    grad_all = lax.all_gather(middle_grad.astype(BF16), "w", axis=0, tiled=True)

    wo_grad, wq_grad, wkv_grad, first_part, query_gain_grad, key_gain_grad = run_backward(
        grad_all, w_output, attended, query_raw, key_raw, value, first_input, weights, query_gain_row, key_gain_row, cosine, sine
    )
    first_grad = lax.psum_scatter(first_part, "w", scatter_dimension=0, tiled=True).astype(F32)
    attn_gain_grad = jnp.sum(first_grad * first_normed, axis=0)
    grad_in = middle_grad + norm_backward(first_grad * attn_scale, first_normed, first_scale)

    wo_mine = lax.psum_scatter(wo_grad, ("z", "x"), scatter_dimension=0, tiled=True)
    moves = [(ring * shards + part, part * rings + ring) for ring in range(rings) for part in range(shards)]
    sum_output = lax.ppermute(wo_mine, ("z", "x", "w"), moves).astype(F32)
    wq_mine = lax.psum_scatter(
        jnp.concatenate([wq_grad, wkv_grad], axis=1), ("z", "x"), scatter_dimension=0, tiled=True
    )
    mine = wq_mine.shape[0] // shards
    collected = lax.all_to_all(wq_mine, "w", split_axis=0, concat_axis=0, tiled=True).reshape(shards, mine, -1)
    collected = collected.transpose(1, 0, 2).astype(F32)
    query_columns = w_query.shape[1] // shards
    key_columns = key_projection.shape[1] // shards
    sum_query = collected[:, :, :query_columns].reshape(mine, -1)
    sum_key = collected[:, :, query_columns : query_columns + key_columns].reshape(mine, -1)
    sum_value = collected[:, :, query_columns + key_columns :].reshape(mine, -1)
    small_grads = jnp.concatenate([router_grad, ffn_gain_grad[:, None], attn_gain_grad[:, None]], axis=1)
    small_mine = lax.psum_scatter(small_grads, ("z", "x", "w"), scatter_dimension=0, tiled=True)
    squares = jnp.stack(
        [jnp.sum(source * source), jnp.sum(branch * branch), jnp.sum(expert_sum * expert_sum), jnp.sum(grad_in * grad_in)]
    )
    totals = lax.psum(
        jnp.concatenate([query_gain_grad[0], key_gain_grad[0], squares]), ("z", "x", "w")
    )
    root_mean_squares = jnp.sqrt(totals[2 * head_size :] / (tokens_here * device_count * width))
    return (
        hidden_out,
        grad_in,
        small_mine[:, experts + 1],
        sum_query,
        sum_key,
        sum_value,
        totals[:head_size],
        totals[head_size : 2 * head_size],
        sum_output,
        small_mine[:, experts],
        small_mine[:, :experts],
        grad_gate,
        grad_up,
        grad_down,
        root_mean_squares,
    )


def solution(mesh):
    rings, shards = mesh.shape["ep"], mesh.shape["ws"]
    planes = 4 if rings % 4 == 0 else 1
    fine = Mesh(mesh.devices.reshape(planes, rings // planes, shards), ("z", "x", "w"))
    every = ("z", "x", "w")
    rows, deep = P(every, None), P(every, None, None)
    return jax.shard_map(
        local,
        mesh=fine,
        in_specs=(
            rows, P("w"), P("w", None), P("w", None), P("w", None), P(), P(), P("w", None), P("w"), P("w", None),
            rows, deep, deep, deep, rows,
        ),
        out_specs=(
            rows, rows, P(every), rows, rows, rows, P(), P(), rows, P(every), rows, deep, deep, deep, P(),
        ),
        check_vma=False,
    )
```

time: 2640 us -> 1560 us (0.59)
  waiting for transfers between devices: 1880 us -> 786 us
  blocking collectives: 110 us -> 281 us
  Pallas kernels: 0 us -> 127 us
  matrix products: 299 us -> 174 us
  local copies, waits for them, and re-layouts: 157 us -> 62.6 us
  other arithmetic: 138 us -> 64.1 us
    reduce_scatter x6, waiting for transfers between devices: 970 us -> 242 us  [the longest x2 142 us: send_back(): lax.psum_scatter(summed.reshape(planes * tokens_here, width), 'z', scatte...]
    all_to_all x4 -> x7, waiting for transfers between devices: 729 us -> 233 us  [the longest x1 128 us: send_back(): lax.all_to_all(rows.reshape(in_plane, planes * capacity, width), ('x', 'w...]
    all_to_all x0 -> x3, blocking collectives: none -> 139 us  [the longest x1 123 us: send_back(): lax.all_to_all(rows.reshape(in_plane, planes * capacity, width), ('x', 'w...]
    pallas_call x0 -> x2, Pallas kernels: none -> 127 us  [the longest x1 73.2 us: run_backward(): pl.pallas_call(functools.partial(attention_backward, pair), grid=(steps,)...]
    dot_general x47 -> x17, matrix products: 297 us -> 174 us  [the longest x4 51.8 us: dot_nt(): lax.dot_general(left, right, (((1,), (1,)), ((), ())), preferred_element_...]
    unnamed x14 -> x12, waiting for transfers between devices: 11.3 us -> 127 us
    gather x4 -> x0, local copies, waits for them, and re-layouts: 89.8 us -> none  [the longest x1 24.7 us: local(): padded_grad[slot_pair]]
    reduce_sum x19 -> x3, other arithmetic: 62 us -> 5.6 us  [the longest x1 2.06 us: local(): attn_gain_grad = jnp.sum(first_grad * first_normed, axis=0)]
  transfers between devices with their start and end apart: 17 -> 19, of which waited for: 14 -> 13; matrix products, arithmetic and copies ran while one was open for 16% -> 11% of each run, Pallas kernels for 0% -> 0%
where the time goes in v1:
time: 1560 us; the launch traced here: 1550 us
  waiting for transfers between devices  786 us (50%)
  blocking collectives  281 us (18%)
  matrix products  174 us (11%)
  Pallas kernels  127 us (8%)
  other arithmetic  64.1 us (4%)
  local copies, waits for them, and re-layouts  62.6 us (4%)
  starting transfers between devices  41.9 us (3%)
    reduce_scatter x2, waiting for transfers between devices, send_back(): lax.psum_scatter(summed.reshape(planes * tokens_here, width), 'z', scatte...  142 us
    all_to_all x1, waiting for transfers between devices, send_back(): lax.all_to_all(rows.reshape(in_plane, planes * capacity, width), ('x', 'w...  128 us
    unnamed x12, waiting for transfers between devices  127 us
    all_to_all x1, blocking collectives, send_back(): lax.all_to_all(rows.reshape(in_plane, planes * capacity, width), ('x', 'w...  123 us
    all_to_all x2, waiting for transfers between devices, send_out(): lax.all_to_all(packed.reshape(in_plane, planes * capacity, width), ('x',...  97.2 us
    all_gather x1, blocking collectives, local(): small_all = lax.all_gather(small, 'w', axis=0, tiled=True)  83.6 us
    all_gather x1, waiting for transfers between devices, local(): cotangent_z = lax.all_gather(cotangent, 'z', axis=0, tiled=False)  80.8 us
    pallas_call x1, Pallas kernels, run_backward(): pl.pallas_call(functools.partial(attention_backward, pair), grid=(steps,)...  73.2 us
  transfers between devices with their start and end apart: 19, of which 13 were waited for; matrix products, arithmetic and copies ran while one was open for 11% of the time, Pallas kernels for 0%

profile of v1, /device:TPU:1, one launch (start us, length us, event | category | flops | bytes accessed | tf_op | source)
XLA Modules:
  0.0 1551.6 jit_solution(5173419013593021733)
XLA Ops:
  19.4 83.6 %all_gather.28 = bf16[2048,34]{0,1:T(8,128)(2,1)S(1)} all-gather(bf16[512,34]{0,1:T(8,128)(2,1)S(1)} %pad_maximum_fusion.5), channel_id=1, replica_groups=mesh['z'=4,'x'=2,'w'=4] {'w'}, dimensions={0}, use_global_device_ids=true | all-gather | bytes 174080 | tf_op jit(solution)/shard_map/all_gather | solution.py:326
  106.9 54.1 %shard_map.262 = (bf16[1024,2048]{1,0:T(8,128)(2,1)}, f32[1024,1024]{1,0:T(8,128)}, f32[1024,128]{1,0:T(8,128)}, bf16[1024,128]{1,0:T(8,128)(2,1)}, bf16[1024,10...) custom-call(bf16[1024,2048]{1,0:T(8,128)(2,1)} %all-gather.8.cloned.1.call-done.hidden_ref, ...), custom_call_target="tpu_custom_call" | custom-call | flops 16000000000 | bytes 40000000 | tf_op jit(solution)/shard_map/pallas_call | solution.py:206
  161.7 43.6 %reduce-scatter.10.cloned.1.call-done = bf16[256,2048]{1,0:T(8,128)(2,1)} async-done(((bf16[1024,2048]{1,0:T(8,128)(2,1)}), bf16[256,2048]{1,0:T(8,128)(2,1)}) %reduce-scatter.10.cloned.1.call-update) | async-done | bytes 1048592 | tf_op jit(solution)/shard_map/reduce_scatter | solution.py:370
  222.3 68.9 %all-gather.12.cloned.1.call-done = bf16[1024,2048]{1,0:T(8,128)(2,1)} async-done(((bf16[256,2048]{1,0:T(8,128)(2,1)}), bf16[1024,2048]{1,0:T(8,128)(2,1)}) %all-gather.12.cloned.1.call-update) | async-done | bytes 4194320 | tf_op jit(solution)/shard_map/all_gather | solution.py:376
  317.0 80.8 %all-gather.14.cloned.1.call-done = bf16[1024,2048]{1,0:T(8,128)(2,1)} async-done(((bf16[256,2048]{1,0:T(8,128)(2,1)}), bf16[1024,2048]{1,0:T(8,128)(2,1)}) %all-gather.14.cloned.1.call-update) | async-done | bytes 4194320 | tf_op jit(solution)/shard_map/all_gather | solution.py:364
  417.1 14.1 all-to-all-done.3
  454.5 14.7 multiply_convert_fusion.2
  469.2 83.0 %all-to-all-done.5 = bf16[8,320,2048]{2,1,0:T(8,128)(2,1)} async-done(((bf16[8,320,2048]{2,1,0:T(8,128)(2,1)}), bf16[8,320,2048]{2,1,0:T(8,128)(2,1)}, u32[]{:S(2)}, u32[]{:S(2)}) %all-to-all-start.5) | async-done | bytes 10485792 | tf_op jit(solution)/shard_map/all_to_all | solution.py:350
  552.2 15.0 fusion.1
  604.2 19.0 %multiply_convert_fusion = (bf16[2560,768]{1,0:T(8,128)(2,1)}, bf16[2560,768]{1,0:T(8,128)(2,1)}) fusion(f32[2560,768]{1,0:T(8,128)} %copy-done.26, f32[2560,768]{1,0:T(8,128)} %get-tuple-element.69, bf16[2560,2048]{1,0:T(8,128)(2,1)} %bitcast.172, bf16[1,768,2048]{2,1,0:T(8,128)(2,1)S(1)} %copy-done), kind=kOutput, calls=%fused_computation.10 | convolution fusion | flops 8078622720 | bytes 37224448 | tf_op jit(solution)/shard_map/dot_general | solution.py:28
  623.2 13.6 fusion.11
  636.8 16.0 %add_convert_fusion = bf16[2560,2048]{1,0:T(8,128)(2,1)} fusion(f32[2560,2048]{1,0:T(8,128)} %fusion.11, bf16[2560,768]{1,0:T(8,128)(2,1)} %get-tuple-element.50, bf16[1,2048,768]{2,1,0:T(8,128)(2,1)S(1)} %copy-done.24), kind=kOutput, calls=%fused_computation.8 | convolution fusion | flops 8063549440 | bytes 38535168 | tf_op jit(solution)/shard_map/dot_general | solution.py:28
  652.8 123.3 %all_to_all.75 = bf16[8,320,2048]{2,1,0:T(8,128)(2,1)} all-to-all(bf16[8,320,2048]{2,1,0:T(8,128)(2,1)} %bitcast.170), channel_id=1, replica_groups=mesh['z'=4,'x'=2,'w'=4] {'x','w'}, dimensions={0} | all-to-all | bytes 20971520 | tf_op jit(solution)/shard_map/all_to_all | solution.py:356
  802.7 67.6 %reduce-scatter.14.cloned.1.call-done = bf16[256,2048]{1,0:T(8,128)(2,1)} async-done(((bf16[1024,2048]{1,0:T(8,128)(2,1)}), bf16[256,2048]{1,0:T(8,128)(2,1)}) %reduce-scatter.14.cloned.1.call-update) | async-done | bytes 1048592 | tf_op jit(solution)/shard_map/reduce_scatter | solution.py:362
  876.7 35.2 %all-gather.10.cloned.1.call-done.grad_ref = bf16[1024,2048]{1,0:T(8,128)(2,1)} async-done(((bf16[256,2048]{1,0:T(8,128)(2,1)}), bf16[1024,2048]{1,0:T(8,128)(2,1)}) %all-gather.10.cloned.1.call-update) | async-done | bytes 4194320 | tf_op jit(solution)/shard_map/all_gather | solution.py:427
  911.9 73.2 %shard_map.263 = (bf16[1024,2048]{1,0:T(8,128)(2,1)}, bf16[2048,1024]{1,0:T(8,128)(2,1)}, bf16[2048,256]{1,0:T(8,128)(2,1)}, bf16[1024,2048]{1,0:T(8,128)(2,1)}, f32[8,128]{1,0:T(8,128)}, /*index=5*/f32[8,128]{1,0:T(8,128)}) custom-call(bf16[1024,2048]{1,0:T(8,128)(2,1)} %all-gather.10.cloned.1.call-done.grad_ref, bf16[1024,2048]{1,0:T(8,128)(2,1)} %wo_ref.3, ...), custom_call_target="tpu_custom_call" | custom-call | flops 35000000512 | bytes 60000000 | tf_op jit(solution)/shard_map/pallas_call | solution.py:252
  985.3 18.9 %fusion.3 = (bf16[2560,2048]{1,0:T(8,128)(2,1)}, bf16[2560,2048]{1,0:T(8,128)(2,1)}) fusion(bf16[8,320,2048]{2,1,0:T(8,128)(2,1)} %all-to-all-done.5, f32[2560]{0:T(1024)S(1)} %mul.194, bf16[2560,2048]{1,0:T(8,128)(2,1)} %get-tuple-element.71), kind=kLoop, calls=%fused_computation.7 | loop fusion | flops 31457280 | bytes 41953280 | tf_op jit(solution)/shard_map/convert_element_type | solution.py:401
  1010.3 128.2 %all-to-all-done.4 = bf16[8,320,2048]{2,1,0:T(8,128)(2,1)} async-done(((bf16[8,320,2048]{2,1,0:T(8,128)(2,1)}), bf16[8,320,2048]{2,1,0:T(8,128)(2,1)}, u32[]{:S(2)}, u32[]{:S(2)}) %all-to-all-start.4) | async-done | bytes 10485792 | tf_op jit(solution)/shard_map/all_to_all | solution.py:356
  1164.4 14.1 convolution_bitcast_fusion
  1191.9 13.5 convolution_bitcast_fusion.2
  1218.1 74.1 %reduce-scatter.12.cloned.1.call-done = bf16[256,2048]{1,0:T(8,128)(2,1)} async-done(((bf16[1024,2048]{1,0:T(8,128)(2,1)}), bf16[256,2048]{1,0:T(8,128)(2,1)}) %reduce-scatter.12.cloned.1.call-update) | async-done | bytes 1048592 | tf_op jit(solution)/shard_map/reduce_scatter | solution.py:362
  1300.0 47.9 %psum.7 = f32[260]{0:T(512)S(1)} all-reduce(f32[260]{0:T(512)S(1)} %concatenate.27), channel_id=1, replica_groups=mesh['z'=4,'x'=2,'w'=4] {'z','x','w'}, use_global_device_ids=true, to_apply=%region_24.25 | all-reduce | flops 260 | bytes 2080 | tf_op jit(solution)/shard_map/psum | solution.py:455
  1347.9 56.9 %reduce-scatter.18.cloned.1.call-done = bf16[256,1280]{1,0:T(8,128)(2,1)} async-done(((bf16[2048,1280]{1,0:T(8,128)(2,1)}), bf16[256,1280]{1,0:T(8,128)(2,1)}) %reduce-scatter.18.cloned.1.call-update) | async-done | bytes 655376 | tf_op jit(solution)/shard_map/reduce_scatter | solution.py:439
  1413.2 124.5 %reduce-scatter.22.cloned.1.call-done = f32[64,34]{1,0:T(8,128)} async-done(((f32[2048,34]{1,0:T(8,128)}), f32[64,34]{1,0:T(8,128)}) %reduce-scatter.22.cloned.1.call-update) | async-done | bytes 8720
  (170 shorter events, 253.5 us)
Async XLA Ops:
  7.2 545.1 %copy-start = (bf16[1,768,2048]{2,1,0:T(8,128)(2,1)S(1)}, bf16[1,768,2048]{2,1,0:T(8,128)(2,1)}, u32[]{:S(2)}) copy-start(bf16[1,768,2048]{2,1,0:T(8,128)(2,1)} %param.28) | copy-start | bytes 9437188
  7.2 99.7 %all-gather.8.cloned.1.call-start = ((), (), s32[]{:S(2)}) async-start(), calls=%async_computation.17 | async-start | bytes 5242880 | tf_op jit(solution)/shard_map/all_gather | solution.py:325
  14.0 92.9 %all-to-all-start = ((bf16[512,4,1280]{2,0,1:T(8,128)(2,1)}), bf16[512,4,1280]{2,0,1:T(8,128)(2,1)}, u32[]{:S(2)}, u32[]{:S(2)}) async-start(bf16[512,4,1280]{2,0,1:T(8,128)(2,1)} %pad_maximum_fusion), calls=%async_computation | async-start | bytes 10485760 | tf_op jit(solution)/shard_map/all_to_all | solution.py:327
  19.3 186.0 %reduce-scatter.10.cloned.1.call-start = ((), (), s32[]{:S(2)}) async-start(), calls=%async_computation.18 | async-start | bytes 5242880 | tf_op jit(solution)/shard_map/reduce_scatter | solution.py:370
  106.9 100.3 %copy-start.13 = (f32[2048,1]{0,1:T(1,128)}, f32[2048,1]{0,1:T(1,128)S(1)}, u32[]{:S(2)}) copy-start(f32[2048,1]{0,1:T(1,128)S(1)} %get-tuple-element.58) | copy-start | bytes 24580
  161.1 130.1 %all-gather.12.cloned.1.call-start = ((), (), s32[]{:S(2)}) async-start(), calls=%async_computation.25 | async-start | bytes 5242880 | tf_op jit(solution)/shard_map/all_gather | solution.py:376
  207.2 93.2 %copy-start.18 = (f32[256]{0:T(256)}, f32[256]{0:T(256)S(1)}, u32[]{:S(2)}) copy-start(f32[256]{0:T(256)S(1)} %add_rsqrt_fusion.1) | copy-start | bytes 3076
  310.7 120.6 %all-to-all-start.3 = ((bf16[8,320,2048]{2,1,0:T(8,128)(2,1)}), bf16[8,320,2048]{2,1,0:T(8,128)(2,1)}, u32[]{:S(2)}, u32[]{:S(2)}) async-start(bf16[8,320,2048]{2,1,0:T(8,128)(2,1)} %bitcast.164), calls=%async_computation.4 | async-start | bytes 20971520 | tf_op jit(solution)/shard_map/all_to_all | solution.py:350
  316.4 81.3 %all-gather.14.cloned.1.call-start = ((), (), s32[]{:S(2)}) async-start(), calls=%async_computation.26 | async-start | bytes 5242880 | tf_op jit(solution)/shard_map/all_gather | solution.py:364
  431.3 121.0 %all-to-all-start.5 = ((bf16[8,320,2048]{2,1,0:T(8,128)(2,1)}), bf16[8,320,2048]{2,1,0:T(8,128)(2,1)}, u32[]{:S(2)}, u32[]{:S(2)}) async-start(bf16[8,320,2048]{2,1,0:T(8,128)(2,1)} %bitcast.165), calls=%async_computation.7 | async-start | bytes 20971520 | tf_op jit(solution)/shard_map/all_to_all | solution.py:350
  567.9 8.1 all-to-all-start.7
  576.0 7.7 all-to-all-start.1
  579.3 291.0 %reduce-scatter.14.cloned.1.call-start = ((), (), s32[]{:S(2)}) async-start(), calls=%async_computation.20 | async-start | bytes 5242880 | tf_op jit(solution)/shard_map/reduce_scatter | solution.py:362
  795.4 116.5 %all-gather.10.cloned.1.call-start = ((), (), s32[]{:S(2)}) async-start(), calls=%async_computation.21 | async-start | bytes 5242880 | tf_op jit(solution)/shard_map/all_gather | solution.py:427
  876.6 331.3 %reduce-scatter.16.cloned.1.call-start = ((), (), s32[]{:S(2)}) async-start(), calls=%async_computation.22 | async-start | bytes 5242880 | tf_op jit(solution)/shard_map/reduce_scatter | solution.py:432
  1004.1 134.4 %all-to-all-start.4 = ((bf16[8,320,2048]{2,1,0:T(8,128)(2,1)}), bf16[8,320,2048]{2,1,0:T(8,128)(2,1)}, u32[]{:S(2)}, u32[]{:S(2)}) async-start(bf16[8,320,2048]{2,1,0:T(8,128)(2,1)} %bitcast.167), calls=%async_computation.5 | async-start | bytes 20971520 | tf_op jit(solution)/shard_map/all_to_all | solution.py:356
  1009.5 202.9 %reduce-scatter.20.cloned.1.call-start = ((), (), s32[]{:S(2)}) async-start(), calls=%async_computation.24 | async-start | bytes 4718592 | tf_op jit(solution)/shard_map/reduce_scatter | solution.py:436
  1010.2 282.0 %reduce-scatter.12.cloned.1.call-start = ((), (), s32[]{:S(2)}) async-start(), calls=%async_computation.19 | async-start | bytes 5242880 | tf_op jit(solution)/shard_map/reduce_scatter | solution.py:362
  1158.1 246.7 %reduce-scatter.18.cloned.1.call-start = ((), (), s32[]{:S(2)}) async-start(), calls=%async_computation.23 | async-start | bytes 5898240 | tf_op jit(solution)/shard_map/reduce_scatter | solution.py:439
  1164.4 373.3 %reduce-scatter.22.cloned.1.call-start = ((), (), s32[]{:S(2)}) async-start(), calls=%async_computation.27 | async-start | bytes 1081344
  1206.4 85.8 %copy-start.6 = (bf16[256,2048]{1,0:T(8,128)(2,1)S(1)}, bf16[256,2048]{1,0:T(8,128)(2,1)}, u32[]{:S(2)}) copy-start(bf16[256,2048]{1,0:T(8,128)(2,1)} %param.29) | copy-start | bytes 3145732
  1212.4 198.4 %collective-permute-start = (bf16[128,2048]{1,0:T(8,128)(2,1)}, bf16[128,2048]{1,0:T(8,128)(2,1)}, u32[]{:S(2)}, u32[]{:S(2)}) collective-permute-start(bf16[128,2048]{1,0:T(8,128)(2,1)} %reduce-scatter.20.cloned.1.call-done), channel_id=1, source_target_pairs={{0,0},{1,8},{2,16},{3,24},{4,1},{5,9},{6,17},{7,25},{8,2},{9,10},{... | collective-permute-start | bytes 1572872 | tf_op jit(solution)/shard_map/ppermute | solution.py:438
  1404.8 136.4 %all-to-all-start.9 = ((bf16[4,64,1280]{2,1,0:T(8,128)(2,1)}), bf16[4,64,1280]{2,1,0:T(8,128)(2,1)}, u32[]{:S(2)}, u32[]{:S(2)}) async-start(bf16[4,64,1280]{2,1,0:T(8,128)(2,1)} %bitcast.179), calls=%async_computation.14 | async-start | bytes 1310720 | tf_op jit(solution)/shard_map/all_to_all | solution.py:443
  1410.3 134.7 %copy-start.1 = (bf16[1,768,2048]{2,1,0:T(8,128)(2,1)S(1)}, bf16[1,768,2048]{2,1,0:T(8,128)(2,1)}, u32[]{:S(2)}) copy-start(bf16[1,768,2048]{2,1,0:T(8,128)(2,1)} %param.28) | copy-start | bytes 9437188
  (23 other events, 581.4 us)
Sparse Core Ops, SparseCore 0:
  9.6 59.1 all-gather.7
  161.2 44.0 reduce-scatter.9
  210.3 80.8 all-gather.11
  318.6 79.1 all-gather.13
  795.5 74.7 reduce-scatter.13
  876.7 35.0 all-gather.9
  985.3 115.8 reduce-scatter.15
  1105.2 91.8 reduce-scatter.19
  1199.4 92.7 reduce-scatter.11
  1296.1 108.6 reduce-scatter.17
  1407.7 129.8 reduce-scatter.21

commit v2 on v1

v2 whole, which is shorter than its diff:
```python
import functools

import jax
import jax.numpy as jnp
from jax import lax
from jax.experimental import pallas as pl
from jax.experimental.pallas import tpu as pltpu
from jax.sharding import Mesh
from jax.sharding import PartitionSpec as P

BLOCK = 256
EPS = 1e-06
ROPE_BASE = 1000000.0
F32 = jnp.float32
BF16 = jnp.bfloat16
VMEM_LIMIT = 60 * 1024 * 1024


def dot(left, right):
    return jnp.dot(left, right, preferred_element_type=F32)


def dot_tn(left, right):
    return lax.dot_general(left, right, (((0,), (0,)), ((), ())), preferred_element_type=F32)


def dot_nt(left, right):
    return lax.dot_general(left, right, (((1,), (1,)), ((), ())), preferred_element_type=F32)


def rope_tables(seq_length, head_size):
    indices = jnp.arange(head_size // 2, dtype=F32)
    frequency = ROPE_BASE ** (-2.0 * indices / head_size)
    angles = jnp.arange(seq_length, dtype=F32)[:, None] * frequency[None, :]
    cosine, sine = jnp.cos(angles), jnp.sin(angles)
    return jnp.concatenate([cosine, cosine], axis=1), jnp.concatenate([-sine, sine], axis=1)


def norm_forward(values):
    scaling = lax.rsqrt(jnp.mean(values * values, axis=-1, keepdims=True) + EPS)
    return values * scaling, scaling


def norm_backward(grad_normed, normed, scaling):
    return scaling * (grad_normed - normed * jnp.mean(grad_normed * normed, axis=-1, keepdims=True))


def half_turn(values):
    return pltpu.roll(values, values.shape[-1] // 2, 1)


def rotate(values, cosine, signed_sine):
    return values * cosine + half_turn(values) * signed_sine


def unrotate(grads, cosine, signed_sine):
    return grads * cosine - half_turn(grads) * signed_sine


MESH = pl.DeviceIdType.MESH


def remote(source, target, send, recv, device):
    return pltpu.make_async_remote_copy(
        src_ref=source, dst_ref=target, send_sem=send, recv_sem=recv, device_id=device, device_id_type=MESH
    )


def wait_bytes(ref, sem):
    pltpu.make_async_copy(ref, ref, sem).wait()


def line_order(z, planes, step):
    low = jnp.minimum(z, planes - 1 - z)
    paired = (step <= 2 * low).astype(jnp.int32)
    hop = paired * ((step + 1) // 2) + (1 - paired) * (step - low)
    longer = (z > planes - 1 - z).astype(jnp.int32)
    below = paired * (step % 2) + (1 - paired) * longer
    return z + hop - 2 * below * hop, hop, below


def greet_plane_and_line(planes, across, shards):
    z, x, w = lax.axis_index("z"), lax.axis_index("x"), lax.axis_index("w")
    in_plane = across * shards
    me = x * shards + w
    barrier = pltpu.get_barrier_semaphore()

    @pl.loop(1, in_plane)
    def _(offset):
        index = (me + offset) % in_plane
        pl.semaphore_signal(barrier, inc=1, device_id=(z, index // shards, index % shards), device_id_type=MESH)

    @pl.loop(1, planes)
    def _(offset):
        pl.semaphore_signal(barrier, inc=1, device_id=((z + offset) % planes, x, w), device_id_type=MESH)

    pl.semaphore_wait(barrier, in_plane + planes - 2)


def attention_forward(
    heads_a_step, hidden_ref, gain_ref, wq_ref, wkv_ref, query_gain_ref, key_gain_ref, cosine_ref, sine_ref, wo_ref,
    input_ref, query_raw_ref, key_raw_ref, value_ref, attended_ref, branch_ref, total_ref, key_rot_ref,
):
    step = pl.program_id(0)
    head_size = cosine_ref.shape[1]
    seq_length = cosine_ref.shape[0]
    blocks = seq_length // BLOCK
    factor = head_size ** (-0.5)

    @pl.when(step == 0)
    def _():
        for block in range(blocks):
            rows = pl.ds(block * BLOCK, BLOCK)
            normed, _ = norm_forward(hidden_ref[rows, :].astype(F32))
            first_input = (normed * gain_ref[...]).astype(BF16)
            input_ref[rows, :] = first_input
            key_value = dot(first_input, wkv_ref[...])
            key_raw = key_value[:, :head_size]
            key_raw_ref[rows, :] = key_raw
            value_ref[rows, :] = key_value[:, head_size:].astype(BF16)
            key_normed, _ = norm_forward(key_raw)
            key_rot_ref[rows, :] = rotate(
                key_normed * key_gain_ref[...], cosine_ref[rows, :], sine_ref[rows, :]
            ).astype(BF16)

    for block in range(blocks):
        rows = pl.ds(block * BLOCK, BLOCK)
        seen = pl.ds(0, (block + 1) * BLOCK)
        query_raw = dot(input_ref[rows, :], wq_ref[...])
        query_raw_ref[rows, :] = query_raw
        for head in range(heads_a_step):
            columns = slice(head * head_size, (head + 1) * head_size)
            query_normed, _ = norm_forward(query_raw[:, columns])
            query_rot = rotate(
                query_normed * query_gain_ref[...], cosine_ref[rows, :], sine_ref[rows, :]
            ).astype(BF16)
            scores = dot_nt(query_rot, key_rot_ref[seen, :]) * factor
            exponent = jnp.exp(scores - jnp.max(scores, axis=-1, keepdims=True))
            probs = (exponent / jnp.sum(exponent, axis=-1, keepdims=True)).astype(BF16)
            attended_ref[rows, columns] = dot(probs, value_ref[seen, :]).astype(BF16)
        partial = dot(attended_ref[rows, :], wo_ref[...])

        @pl.when(step == 0)
        def _():
            total_ref[rows, :] = partial

        @pl.when(step > 0)
        def _():
            total_ref[rows, :] += partial

    @pl.when(step == pl.num_programs(0) - 1)
    def _():
        branch_ref[...] = total_ref[...].astype(BF16)


def attention_backward(
    planes, across, shards, capacity, heads_a_step,
    own_grad_ref, wo_ref, attended_ref, query_raw_ref, key_raw_ref, value_ref, input_ref, wq_ref,
    query_gain_ref, key_gain_ref, cosine_ref, sine_ref, slots_ref, weighted_hbm,
    wo_grad_ref, wq_grad_ref, first_grad_ref, query_gain_grad_ref, key_gain_grad_ref, returned_hbm, expert_sum_ref,
    total_ref, key_rot_ref, key_grad_ref, value_grad_ref, query_grad_ref, turned_ref, grad_ref,
    rows, chosen, partial_out, partial_in,
    gather_send, gather_recv, back_send, back_recv, sum_send, sum_recv, load_sem,
):
    step = pl.program_id(0)
    last = pl.num_programs(0) - 1
    head_size = cosine_ref.shape[1]
    seq_length = cosine_ref.shape[0]
    blocks = seq_length // BLOCK
    factor = head_size ** (-0.5)
    z, x, w = lax.axis_index("z"), lax.axis_index("x"), lax.axis_index("w")
    in_plane = across * shards
    me = x * shards + w
    tokens, width = own_grad_ref.shape
    count = in_plane * capacity
    chunk = 512
    pair, core = w // 2, w % 2
    sibling, opposite, other = pair * 2 + 1 - core, (1 - pair) * 2 + core, (1 - pair) * 2 + 1 - core

    def slice_of(index):
        return pl.ds(pl.multiple_of(index * capacity, 16), capacity)

    def tokens_of(index):
        return pl.ds(pl.multiple_of(index * tokens, tokens), tokens)

    def gather_copy(kind, owner, target):
        return remote(
            grad_ref.at[tokens_of(owner)], grad_ref.at[tokens_of(owner)], gather_send.at[kind], gather_recv.at[kind],
            (z, x, target),
        )

    def back_copy(block, index):
        return remote(
            weighted_hbm.at[block, slice_of(index)], returned_hbm.at[block, slice_of(me)],
            back_send.at[block], back_recv.at[block], (z, index // shards, index % shards),
        )

    def start_back(near):
        @pl.loop(0, planes)
        def _(turn):
            block, _, _ = line_order(z, planes, planes - 1 - turn)

            @pl.loop(1, in_plane)
            def _(offset):
                index = (me + offset) % in_plane

                @pl.when((index % shards) // 2 == pair if near else (index % shards) // 2 != pair)
                def _():
                    back_copy(block, index).start()

    def sum_copy(block):
        return remote(partial_out.at[block], partial_in.at[z], sum_send.at[block], sum_recv.at[z], (block, x, w))

    @pl.when(step == 0)
    def _():
        greet_plane_and_line(planes, across, shards)
        grad_ref[tokens_of(w), :] = own_grad_ref[...]
        gather_copy(1, w, opposite).start()
        gather_copy(0, w, sibling).start()
        start_back(True)

        @pl.loop(0, planes)
        def _(block):
            pltpu.make_async_copy(
                weighted_hbm.at[block, slice_of(me)], returned_hbm.at[block, slice_of(me)], back_recv.at[block]
            ).start()

        key_normed, _ = norm_forward(key_raw_ref[...])
        key_rot_ref[...] = rotate(key_normed * key_gain_ref[...], cosine_ref[...], sine_ref[...]).astype(BF16)
        key_grad_ref[...] = jnp.zeros_like(key_grad_ref)
        value_grad_ref[...] = jnp.zeros_like(value_grad_ref)
        query_gain_grad_ref[...] = jnp.zeros_like(query_gain_grad_ref)
        for block in range(blocks):
            rows_here = pl.ds(block * BLOCK, BLOCK)
            turned_ref[:, rows_here] = input_ref[rows_here, :].T
        wait_bytes(grad_ref.at[tokens_of(opposite)], gather_recv.at[1])
        gather_copy(2, opposite, sibling).start()
        start_back(False)
        wait_bytes(grad_ref.at[tokens_of(sibling)], gather_recv.at[0])
        wait_bytes(grad_ref.at[tokens_of(other)], gather_recv.at[2])

    @pl.when(step < last)
    def _():
        wo_grad_ref[...] = dot_tn(attended_ref[...], grad_ref[...]).astype(BF16)
        for block in range(blocks):
            rows_here = pl.ds(block * BLOCK, BLOCK)
            seen = pl.ds(0, (block + 1) * BLOCK)
            attended_grad = dot_nt(grad_ref[rows_here, :], wo_ref[...]).astype(BF16)
            for head in range(heads_a_step):
                columns = slice(head * head_size, (head + 1) * head_size)
                query_normed, query_scale = norm_forward(query_raw_ref[rows_here, columns])
                cosine, sine = cosine_ref[rows_here, :], sine_ref[rows_here, :]
                query_rot = rotate(query_normed * query_gain_ref[...], cosine, sine).astype(BF16)
                head_grad = attended_grad[:, columns]
                keys, values = key_rot_ref[seen, :], value_ref[seen, :]
                scores = dot_nt(query_rot, keys) * factor
                exponent = jnp.exp(scores - jnp.max(scores, axis=-1, keepdims=True))
                probs = exponent / jnp.sum(exponent, axis=-1, keepdims=True)
                prob_grad = dot_nt(head_grad, values)
                value_grad_ref[seen, :] += dot_tn(probs.astype(BF16), head_grad)
                center = jnp.sum(probs * prob_grad, axis=-1, keepdims=True)
                score_grad = (probs * (prob_grad - center)).astype(BF16)
                key_grad_ref[seen, :] += dot_tn(score_grad, query_rot) * factor
                query_rot_grad = dot(score_grad, keys) * factor
                unrotated = unrotate(query_rot_grad, cosine, sine)
                query_gain_grad_ref[0:1, :] += jnp.sum(unrotated * query_normed, axis=0, keepdims=True)
                query_grad_ref[rows_here, columns] = norm_backward(
                    unrotated * query_gain_ref[...], query_normed, query_scale
                ).astype(BF16)
            partial = dot_nt(query_grad_ref[rows_here, :], wq_ref[...])

            @pl.when(step == 0)
            def _():
                total_ref[rows_here, :] = partial

            @pl.when(step > 0)
            def _():
                total_ref[rows_here, :] += partial

    @pl.when(step == last)
    def _():
        key_normed, key_scale = norm_forward(key_raw_ref[...])
        unrotated = unrotate(key_grad_ref[...], cosine_ref[...], sine_ref[...])
        key_gain_grad_ref[...] = jnp.zeros_like(key_gain_grad_ref)
        key_gain_grad_ref[0:1, :] = jnp.sum(unrotated * key_normed, axis=0, keepdims=True)
        key_grad = norm_backward(unrotated * key_gain_ref[...], key_normed, key_scale)
        query_grad_ref[:, :head_size] = key_grad.astype(BF16)
        query_grad_ref[:, head_size : 2 * head_size] = value_grad_ref[...].astype(BF16)
        for block in range(blocks):
            rows_here = pl.ds(block * BLOCK, BLOCK)
            first_grad_ref[rows_here, :] = (
                total_ref[rows_here, :] + dot_nt(query_grad_ref[rows_here, :], wq_ref[...])
            ).astype(BF16)

    wq_grad_ref[...] = dot(turned_ref[...], query_grad_ref[...]).astype(BF16)

    @pl.when(step >= last - planes + 1)
    def _():
        place = last - step
        block, _, _ = line_order(z, planes, place)
        wait_bytes(returned_hbm.at[block], back_recv.at[block])
        load = pltpu.make_async_copy(returned_hbm.at[block], rows, load_sem)
        load.start()
        slot_ids = lax.broadcasted_iota(jnp.int32, (capacity, tokens), 0)

        @pl.loop(0, in_plane)
        def _(index):
            slots = slots_ref[block * in_plane + index]
            chosen[slice_of(index), :] = (slot_ids == slots).astype(F32).astype(BF16)

        load.wait()

        @pl.loop(0, width // chunk)
        def _(part):
            wide = pl.ds(pl.multiple_of(part * chunk, chunk), chunk)
            summed = dot_tn(chosen[...], rows[:, wide])
            partial_out[block, :, wide] = summed.astype(BF16)

            @pl.when(place == 0)
            def _():
                expert_sum_ref[:, wide] = summed

        @pl.when(place > 0)
        def _():
            sum_copy(block).start()

    @pl.when(step == last)
    def _():
        @pl.loop(1, planes)
        def _(offset):
            source = (z + offset) % planes
            wait_bytes(partial_in.at[source], sum_recv.at[source])

            @pl.loop(0, width // chunk)
            def _(part):
                wide = pl.ds(pl.multiple_of(part * chunk, chunk), chunk)
                expert_sum_ref[:, wide] += partial_in[source, :, wide].astype(F32)

            wait_bytes(partial_out.at[source], sum_send.at[source])

        @pl.loop(0, planes)
        def _(block):
            wait_bytes(weighted_hbm.at[block, pl.ds(0, count - capacity)], back_send.at[block])

        wait_bytes(grad_ref.at[tokens_of(w)], gather_send.at[0])
        wait_bytes(grad_ref.at[tokens_of(w)], gather_send.at[1])
        wait_bytes(grad_ref.at[tokens_of(w)], gather_send.at[2])


def whole(shape):
    return pl.BlockSpec(shape, lambda step: (0,) * len(shape), pipeline_mode=pl.Buffered(1))


def run_forward(hidden_all, gain, weights, wo, query_gain, key_gain, cosine, sine):
    seq_length, width = hidden_all.shape
    head_size = query_gain.shape[1]
    heads_here = wo.shape[0] // head_size
    pair = 2
    wide = pair * head_size
    steps = heads_here // pair
    return pl.pallas_call(
        functools.partial(attention_forward, pair),
        grid=(steps,),
        in_specs=[
            whole((seq_length, width)),
            whole((1, width)),
            pl.BlockSpec((width, wide), lambda step: (0, step)),
            pl.BlockSpec((width, wide), lambda step: (0, steps), pipeline_mode=pl.Buffered(1)),
            whole((1, head_size)),
            whole((1, head_size)),
            whole((seq_length, head_size)),
            whole((seq_length, head_size)),
            pl.BlockSpec((wide, width), lambda step: (step, 0)),
        ],
        out_specs=[
            whole((seq_length, width)),
            pl.BlockSpec((seq_length, wide), lambda step: (0, step)),
            whole((seq_length, head_size)),
            whole((seq_length, head_size)),
            pl.BlockSpec((seq_length, wide), lambda step: (0, step)),
            whole((seq_length, width)),
        ],
        out_shape=[
            jax.ShapeDtypeStruct((seq_length, width), BF16),
            jax.ShapeDtypeStruct((seq_length, heads_here * head_size), F32),
            jax.ShapeDtypeStruct((seq_length, head_size), F32),
            jax.ShapeDtypeStruct((seq_length, head_size), BF16),
            jax.ShapeDtypeStruct((seq_length, heads_here * head_size), BF16),
            jax.ShapeDtypeStruct((seq_length, width), BF16),
        ],
        scratch_shapes=[
            pltpu.VMEM((seq_length, width), F32),
            pltpu.VMEM((seq_length, head_size), BF16),
        ],
        compiler_params=pltpu.CompilerParams(vmem_limit_bytes=VMEM_LIMIT),
        cost_estimate=pl.CostEstimate(flops=16 * 10**9, bytes_accessed=40 * 10**6, transcendentals=6 * 10**6),
    )(hidden_all, gain, weights, weights, query_gain, key_gain, cosine, sine, wo)


def run_backward(
    planes, across, shards, capacity, own_grad, wo, attended, query_raw, key_raw, value, first_input, weights, query_gain,
    key_gain, cosine, sine, slots, weighted,
):
    tokens, width = own_grad.shape
    seq_length = attended.shape[0]
    head_size = query_gain.shape[1]
    heads_here = wo.shape[0] // head_size
    pair = 2
    wide = pair * head_size
    steps = heads_here // pair
    count = across * shards * capacity
    hbm = pl.BlockSpec(memory_space=pl.ANY)
    dma = pltpu.SemaphoreType.DMA

    def held(step):
        return jnp.minimum(step, steps - 1)

    return pl.pallas_call(
        functools.partial(attention_backward, planes, across, shards, capacity, pair),
        grid=(steps + 1,),
        in_specs=[
            whole((tokens, width)),
            pl.BlockSpec((wide, width), lambda step: (held(step), 0)),
            pl.BlockSpec((seq_length, wide), lambda step: (0, held(step))),
            pl.BlockSpec((seq_length, wide), lambda step: (0, held(step))),
            whole((seq_length, head_size)),
            whole((seq_length, head_size)),
            whole((seq_length, width)),
            pl.BlockSpec((width, wide), lambda step: (0, step)),
            whole((1, head_size)),
            whole((1, head_size)),
            whole((seq_length, head_size)),
            whole((seq_length, head_size)),
            whole(slots.shape),
            hbm,
        ],
        out_specs=[
            pl.BlockSpec((wide, width), lambda step: (held(step), 0)),
            pl.BlockSpec((width, wide), lambda step: (0, step)),
            whole((seq_length, width)),
            whole((8, head_size)),
            whole((8, head_size)),
            hbm,
            whole((tokens, width)),
        ],
        out_shape=[
            jax.ShapeDtypeStruct((heads_here * head_size, width), BF16),
            jax.ShapeDtypeStruct((width, (steps + 1) * wide), BF16),
            jax.ShapeDtypeStruct((seq_length, width), BF16),
            jax.ShapeDtypeStruct((8, head_size), F32),
            jax.ShapeDtypeStruct((8, head_size), F32),
            jax.ShapeDtypeStruct(weighted.shape, BF16),
            jax.ShapeDtypeStruct((tokens, width), F32),
        ],
        scratch_shapes=[
            pltpu.VMEM((seq_length, width), F32),
            pltpu.VMEM((seq_length, head_size), BF16),
            pltpu.VMEM((seq_length, head_size), F32),
            pltpu.VMEM((seq_length, head_size), F32),
            pltpu.VMEM((seq_length, wide), BF16),
            pltpu.VMEM((width, seq_length), BF16),
            pltpu.VMEM((seq_length, width), BF16),
            pltpu.VMEM((count, width), BF16),
            pltpu.VMEM((count, tokens), BF16),
            pltpu.VMEM((planes, tokens, width), BF16),
            pltpu.VMEM((planes, tokens, width), BF16),
            dma((3,)), dma((3,)), dma((planes,)), dma((planes,)), dma((planes,)), dma((planes,)), dma,
        ],
        compiler_params=pltpu.CompilerParams(vmem_limit_bytes=VMEM_LIMIT, collective_id=2, has_side_effects=True),
        cost_estimate=pl.CostEstimate(flops=70 * 10**9, bytes_accessed=60 * 10**6, transcendentals=6 * 10**6),
    )(
        own_grad, wo, attended, query_raw, key_raw, value, first_input, weights, query_gain, key_gain, cosine, sine, slots,
        weighted,
    )


def reduce_kernel(
    planes, across, shards,
    wq_hbm, wo_hbm, first_hbm,
    query_ref, key_ref, value_ref, output_ref, first_ref,
    wq_parts, wo_parts, wq_out, wo_out, wq_in, wo_in, wq_total, wo_total, wq_final, wo_final, wq_home, wo_home, first_in,
    across_send, across_recv, line_send, line_recv, home_send, home_recv, swap_send, swap_recv, first_send, first_recv,
):
    z, x, w = lax.axis_index("z"), lax.axis_index("x"), lax.axis_index("w")
    rings = planes * across
    ring = z * across + x
    everyone = rings * shards
    wq_rows, wo_rows = wq_total.shape[0], wo_total.shape[0]
    mine = wq_rows // shards
    tokens = first_ref.shape[0]
    query_columns = query_ref.shape[1] // shards
    key_columns = key_ref.shape[1] // shards
    linear = ring * shards + w
    barrier = pltpu.get_barrier_semaphore()

    @pl.loop(1, everyone)
    def _(offset):
        other = (linear + offset) % everyone
        pl.semaphore_signal(
            barrier, inc=1, device_id=(other // shards // across, other // shards % across, other % shards),
            device_id_type=MESH,
        )

    pl.semaphore_wait(barrier, everyone - 1)

    def rows_of(index, size):
        return pl.ds(pl.multiple_of(index * size, 16), size)

    def across_copies(plane, column):
        target = plane * across + column
        return [
            remote(
                wq_hbm.at[rows_of(target, wq_rows)], wq_parts.at[plane, x],
                across_send.at[0, plane], across_recv.at[0, plane], (z, column, w),
            ),
            remote(
                wo_hbm.at[rows_of(target, wo_rows)], wo_parts.at[plane, x],
                across_send.at[1, plane], across_recv.at[1, plane], (z, column, w),
            ),
        ]

    def first_copy(offset):
        target = (w + offset) % shards
        return remote(
            first_hbm.at[rows_of(target, tokens)], first_in.at[offset], first_send.at[offset], first_recv.at[offset],
            (z, x, target),
        )

    @pl.loop(1, shards)
    def _(offset):
        first_copy(offset).start()

    pltpu.make_async_copy(first_hbm.at[rows_of(w, tokens)], first_in.at[0], first_recv.at[0]).start()

    @pl.loop(0, planes)
    def _(turn):
        plane, _, _ = line_order(z, planes, planes - 1 - turn)

        @pl.loop(1, across)
        def _(offset):
            for copy in across_copies(plane, (x + offset) % across):
                copy.start()

        target = plane * across + x
        pltpu.make_async_copy(
            wq_hbm.at[rows_of(target, wq_rows)], wq_parts.at[plane, x], across_recv.at[0, plane]
        ).start()
        pltpu.make_async_copy(
            wo_hbm.at[rows_of(target, wo_rows)], wo_parts.at[plane, x], across_recv.at[1, plane]
        ).start()

    def wq_line_copy(plane):
        return remote(wq_out.at[plane], wq_in.at[z], line_send.at[0, plane], line_recv.at[0, z], (plane, x, w))

    def wo_line_copy(plane):
        return remote(wo_out.at[plane], wo_in.at[z], line_send.at[1, plane], line_recv.at[1, z], (plane, x, w))

    @pl.loop(0, shards)
    def _(offset):
        wait_bytes(first_in.at[offset], first_recv.at[offset])

    first_ref[...] = first_in[0].astype(F32)

    @pl.loop(1, shards)
    def _(offset):
        first_ref[...] += first_in[offset].astype(F32)

    @pl.loop(0, planes)
    def _(turn):
        plane, _, _ = line_order(z, planes, planes - 1 - turn)
        wait_bytes(wq_parts.at[plane], across_recv.at[0, plane])
        wq_total[...] = wq_parts[plane, 0].astype(F32)

        @pl.loop(1, across)
        def _(column):
            wq_total[...] += wq_parts[plane, column].astype(F32)

        @pl.when(turn < planes - 1)
        def _():
            wq_out[plane] = wq_total[...].astype(BF16)
            wq_line_copy(plane).start()

        wait_bytes(wo_parts.at[plane], across_recv.at[1, plane])
        wo_total[...] = wo_parts[plane, 0].astype(F32)

        @pl.loop(1, across)
        def _(column):
            wo_total[...] += wo_parts[plane, column].astype(F32)

        @pl.when(turn < planes - 1)
        def _():
            wo_out[plane] = wo_total[...].astype(BF16)
            wo_line_copy(plane).start()

    @pl.loop(1, planes)
    def _(turn):
        plane, _, _ = line_order(z, planes, turn)
        wait_bytes(wq_in.at[plane], line_recv.at[0, plane])
        wq_total[...] += wq_in[plane].astype(F32)

    wq_final[...] = wq_total[...].astype(BF16)

    def home_copy(offset):
        target = (w + offset) % shards
        return remote(
            wq_final.at[rows_of(target, mine)], wq_home.at[w], home_send.at[offset], home_recv.at[w], (z, x, target)
        )

    @pl.loop(1, shards)
    def _(offset):
        home_copy(offset).start()

    pltpu.make_async_copy(wq_final.at[rows_of(w, mine)], wq_home.at[w], home_recv.at[w]).start()

    @pl.loop(1, planes)
    def _(turn):
        plane, _, _ = line_order(z, planes, turn)
        wait_bytes(wo_in.at[plane], line_recv.at[1, plane])
        wo_total[...] += wo_in[plane].astype(F32)

    wo_final[...] = wo_total[...].astype(BF16)
    goal = w * rings + ring
    stays = goal == linear
    swap = remote(
        wo_final, wo_home, swap_send, swap_recv, (goal // shards // across, goal // shards % across, goal % shards)
    )

    @pl.when(jnp.logical_not(stays))
    def _():
        swap.start()

    @pl.when(stays)
    def _():
        pltpu.make_async_copy(wo_final, wo_home, swap_recv).start()

    for part in range(shards):
        wait_bytes(wq_home.at[part], home_recv.at[part])
        rows = wq_home[part].astype(F32)
        query_ref[:, part * query_columns : (part + 1) * query_columns] = rows[:, :query_columns]
        key_ref[:, part * key_columns : (part + 1) * key_columns] = rows[:, query_columns : query_columns + key_columns]
        value_ref[:, part * key_columns : (part + 1) * key_columns] = rows[:, query_columns + key_columns :]

    wait_bytes(wo_home, swap_recv)
    output_ref[...] = wo_home[...].astype(F32)

    @pl.when(jnp.logical_not(stays))
    def _():
        wait_bytes(wo_final, swap_send)

    @pl.loop(1, shards)
    def _(offset):
        wait_bytes(wq_home.at[0], home_send.at[offset])
        wait_bytes(first_in.at[0], first_send.at[offset])

    if across > 1:

        @pl.loop(0, planes)
        def _(plane):
            wait_bytes(wq_parts.at[plane, pl.ds(0, across - 1)], across_send.at[0, plane])
            wait_bytes(wo_parts.at[plane, pl.ds(0, across - 1)], across_send.at[1, plane])

    @pl.loop(1, planes)
    def _(offset):
        plane = (z + offset) % planes
        wait_bytes(wq_out.at[plane], line_send.at[0, plane])
        wait_bytes(wo_out.at[plane], line_send.at[1, plane])


def run_reduce(planes, across, shards, wq_grad, wo_grad, first_part, query_columns, key_columns):
    rings = planes * across
    everyone = rings * shards
    width = wq_grad.shape[0]
    wq_wide = wq_grad.shape[1]
    wq_rows, wo_rows = width // rings, wo_grad.shape[0] // rings
    tokens = first_part.shape[0] // shards
    mine = wq_rows // shards
    hbm = pl.BlockSpec(memory_space=pl.ANY)
    vmem = pl.BlockSpec(memory_space=pltpu.VMEM)
    dma = pltpu.SemaphoreType.DMA
    return pl.pallas_call(
        functools.partial(reduce_kernel, planes, across, shards),
        in_specs=[hbm] * 3,
        out_specs=[vmem] * 5,
        out_shape=[
            jax.ShapeDtypeStruct((mine, query_columns), F32),
            jax.ShapeDtypeStruct((mine, key_columns), F32),
            jax.ShapeDtypeStruct((mine, key_columns), F32),
            jax.ShapeDtypeStruct((wo_rows, width), F32),
            jax.ShapeDtypeStruct((tokens, width), F32),
        ],
        scratch_shapes=[
            pltpu.VMEM((planes, across, wq_rows, wq_wide), BF16),
            pltpu.VMEM((planes, across, wo_rows, width), BF16),
            pltpu.VMEM((planes, wq_rows, wq_wide), BF16),
            pltpu.VMEM((planes, wo_rows, width), BF16),
            pltpu.VMEM((planes, wq_rows, wq_wide), BF16),
            pltpu.VMEM((planes, wo_rows, width), BF16),
            pltpu.VMEM((wq_rows, wq_wide), F32),
            pltpu.VMEM((wo_rows, width), F32),
            pltpu.VMEM((wq_rows, wq_wide), BF16),
            pltpu.VMEM((wo_rows, width), BF16),
            pltpu.VMEM((shards, mine, wq_wide), BF16),
            pltpu.VMEM((wo_rows, width), BF16),
            pltpu.VMEM((shards, tokens, width), BF16),
            dma((2, planes)), dma((2, planes)), dma((2, planes)), dma((2, planes)), dma((shards,)), dma((shards,)),
            dma, dma, dma((shards,)), dma((shards,)),
        ],
        compiler_params=pltpu.CompilerParams(vmem_limit_bytes=VMEM_LIMIT, collective_id=3, has_side_effects=True),
        cost_estimate=pl.CostEstimate(flops=70 * 10**9, bytes_accessed=40 * 10**6, transcendentals=0),
    )(wq_grad, wo_grad, first_part)


def total_kernel(planes, across, shards, parts_ref, total_ref, parts_in, send, recv):
    z, x, w = lax.axis_index("z"), lax.axis_index("x"), lax.axis_index("w")
    everyone = planes * across * shards
    linear = (z * across + x) * shards + w
    barrier = pltpu.get_barrier_semaphore()

    def place(index):
        return (index // shards // across, index // shards % across, index % shards)

    @pl.loop(1, everyone)
    def _(offset):
        pl.semaphore_signal(barrier, inc=1, device_id=place((linear + offset) % everyone), device_id_type=MESH)

    pl.semaphore_wait(barrier, everyone - 1)

    @pl.loop(1, everyone)
    def _(offset):
        other = (linear + offset) % everyone
        remote(parts_ref.at[other], parts_in.at[linear], send, recv, place(other)).start()

    parts_in[linear] = parts_ref[linear]
    wait_bytes(parts_ref.at[pl.ds(0, everyone - 1)], recv)
    total_ref[...] = jnp.sum(parts_in[...], axis=0)
    wait_bytes(parts_ref.at[pl.ds(0, everyone - 1)], send)


def run_total(planes, across, shards, parts):
    everyone, rows, lanes = parts.shape
    return pl.pallas_call(
        functools.partial(total_kernel, planes, across, shards),
        in_specs=[pl.BlockSpec(memory_space=pltpu.VMEM)],
        out_specs=pl.BlockSpec(memory_space=pltpu.VMEM),
        out_shape=jax.ShapeDtypeStruct((rows, lanes), F32),
        scratch_shapes=[
            pltpu.VMEM((everyone, rows, lanes), F32), pltpu.SemaphoreType.DMA, pltpu.SemaphoreType.DMA,
        ],
        compiler_params=pltpu.CompilerParams(vmem_limit_bytes=VMEM_LIMIT, collective_id=4, has_side_effects=True),
    )(parts)


def expert_kernel(
    planes, across, shards, capacity,
    own_ref, share_ref, slots_ref, my_slots_ref, gate_ref, up_ref, down_ref, top_hbm,
    rows_hbm, back_hbm, weighted_hbm, units_hbm, gate_grad_hbm, up_grad_hbm, pair_grad_hbm, row_grad_ref, share_grad_ref,
    plane_rows, plane_shares, share_in, share_back, share_home, stage, chosen, rows, top, units,
    gate_grad, up_grad, columns, partial_in,
    line_send, line_recv, plane_share_send, plane_share_recv, out_send, out_recv, out_share_send, out_share_recv,
    back_send, back_recv, back_share_send, back_share_recv, sum_send, sum_recv, sum_share_send, sum_share_recv,
    load_sem, top_sem, store_sem,
):
    z, x, w = lax.axis_index("z"), lax.axis_index("x"), lax.axis_index("w")
    in_plane = across * shards
    me = x * shards + w
    tokens, width = own_ref.shape
    count = in_plane * capacity
    half = count // 2
    per_half = in_plane // 2
    chunk = 512

    def place(index):
        return (z, index // shards, index % shards)

    def order(step):
        return line_order(z, planes, step)

    greet_plane_and_line(planes, across, shards)

    def line_up(block, hop):
        return remote(
            plane_rows.at[block], plane_rows.at[block], line_send.at[0, hop], line_recv.at[0, hop], (z + 1, x, w)
        )

    def line_down(block, hop):
        return remote(
            plane_rows.at[block], plane_rows.at[block], line_send.at[1, hop], line_recv.at[1, hop], (z - 1, x, w)
        )

    plane_rows[z] = own_ref[...]

    @pl.when(z + 1 < planes)
    def _():
        line_up(z, 1).start()

    @pl.when(z > 0)
    def _():
        line_down(z, 1).start()

    def plane_share_copy(other):
        return remote(
            share_ref.at[pl.ds(other * in_plane, in_plane)], plane_shares.at[z],
            plane_share_send.at[other], plane_share_recv.at[z], (other, x, w),
        )

    @pl.loop(1, planes)
    def _(offset):
        plane_share_copy((z + offset) % planes).start()

    plane_shares[z] = share_ref[pl.ds(z * in_plane, in_plane)]

    def slice_of(index):
        return pl.ds(pl.multiple_of(index * capacity, 16), capacity)

    def out_copy(step, block, index):
        return remote(
            stage.at[step, slice_of(index)], rows_hbm.at[block, slice_of(me)],
            out_send.at[step], out_recv.at[step], place(index),
        )

    def out_share_copy(step, block, index):
        return remote(
            plane_shares.at[block, index], share_in.at[block, me],
            out_share_send.at[step], out_share_recv.at[step], place(index),
        )

    def back_copy(step, block, index):
        return remote(
            stage.at[step, slice_of(index)], back_hbm.at[block, slice_of(me)],
            back_send.at[step], back_recv.at[step], place(index),
        )

    def back_share_copy(step, block, index):
        return remote(
            share_back.at[block, index], share_home.at[block, me],
            back_share_send.at[step], back_share_recv.at[step], place(index),
        )

    def start_back(step, block):
        @pl.loop(1, in_plane)
        def _(offset):
            index = (me + offset) % in_plane
            back_copy(step, block, index).start()
            back_share_copy(step, block, index).start()

        pltpu.make_async_copy(stage.at[step, slice_of(me)], back_hbm.at[block, slice_of(me)], back_recv.at[step]).start()
        pltpu.make_async_copy(share_back.at[block, me], share_home.at[block, me], back_share_recv.at[step]).start()

    slot_ids = lax.broadcasted_iota(jnp.int32, (capacity, tokens), 0)

    def send_step(step):
        block, hop, below = order(step)

        @pl.when(step > 0)
        def _():
            wait_bytes(plane_rows.at[block], line_recv.at[1 - below, hop])
            wait_bytes(plane_shares.at[block], plane_share_recv.at[block])

            @pl.when((below == 1) & (z + 1 < planes))
            def _():
                line_up(block, hop + 1).start()

            @pl.when((below == 0) & (z > 0))
            def _():
                line_down(block, hop + 1).start()

        @pl.loop(0, in_plane)
        def _(index):
            slots = slots_ref[block * in_plane + index]
            chosen[step, slice_of(index), :] = (slot_ids == slots).astype(F32).astype(BF16)

        @pl.loop(0, width // chunk)
        def _(part):
            wide = pl.ds(pl.multiple_of(part * chunk, chunk), chunk)
            stage[step, :, wide] = dot(chosen[step], plane_rows[block, :, wide]).astype(BF16)

        @pl.loop(1, in_plane)
        def _(offset):
            index = (me + offset) % in_plane
            out_copy(step, block, index).start()
            out_share_copy(step, block, index).start()

        pltpu.make_async_copy(stage.at[step, slice_of(me)], rows_hbm.at[block, slice_of(me)], out_recv.at[step]).start()
        pltpu.make_async_copy(plane_shares.at[block, me], share_in.at[block, me], out_share_recv.at[step]).start()

    def top_copy(block, index):
        return pltpu.make_async_copy(top_hbm.at[index, block], top.at[slice_of(index)], top_sem)

    def expert_step(step):
        block, _, _ = order(step)

        @pl.loop(0, in_plane)
        def _(index):
            top_copy(block, index).start()

        wait_bytes(rows_hbm.at[block], out_recv.at[step])
        load = pltpu.make_async_copy(rows_hbm.at[block], rows, load_sem)
        load.start()
        wait_bytes(share_in.at[block], out_share_recv.at[step])
        wait_bytes(stage.at[step, pl.ds(0, count - capacity)], out_send.at[step])
        wait_bytes(plane_shares.at[block, pl.ds(0, in_plane - 1)], out_share_send.at[step])

        @pl.loop(0, in_plane)
        def _(index):
            mine = slot_ids == my_slots_ref[block * in_plane + index]
            columns[slice_of(index), :] = jnp.broadcast_to(
                jnp.sum(jnp.where(mine, share_in[block, index], 0.0), axis=1, keepdims=True), (capacity, 128)
            )

        load.wait()
        wait_bytes(top, top_sem)

        @pl.loop(0, 2)
        def _(part):
            here = pl.ds(pl.multiple_of(part * half, 16), half)
            gate = dot(rows[here, :], gate_ref[...])
            up = dot(rows[here, :], up_ref[...])
            sigmoid = 1.0 / (1.0 + jnp.exp(-gate))
            active = gate * sigmoid
            hidden = (active * up).astype(BF16)
            units[here, :] = hidden
            share = columns[here, 0:1]
            total = jnp.zeros((half, 1), F32)
            for piece in range(width // chunk):
                wide = pl.ds(piece * chunk, chunk)
                pair_out = dot(hidden, down_ref[:, wide]).astype(BF16).astype(F32)
                top_rows = top[here, wide].astype(F32)
                total += jnp.sum(pair_out * top_rows, axis=1, keepdims=True)
                rows[here, wide] = (share * pair_out).astype(BF16)
                top[here, wide] = (share * top_rows).astype(BF16)
            columns[here, :] = jnp.broadcast_to(total, (half, 128))
            hidden_grad = dot_nt(top[here, :], down_ref[...])
            gate_low = (hidden_grad * up * sigmoid * (1.0 + gate * (1.0 - sigmoid))).astype(BF16)
            up_low = (hidden_grad * active).astype(BF16)
            gate_grad[here, :] = gate_low
            up_grad[here, :] = up_low
            for piece in range(width // chunk):
                wide = pl.ds(piece * chunk, chunk)
                stage[step, here, wide] = (dot_nt(gate_low, gate_ref[wide, :]) + dot_nt(up_low, up_ref[wide, :])).astype(BF16)

        @pl.loop(0, in_plane)
        def _(index):
            mine = slot_ids == my_slots_ref[block * in_plane + index]
            values = columns[slice_of(index), 0:1]
            share_back[block, index] = jnp.sum(jnp.where(mine, values, 0.0), axis=0, keepdims=True)

        @pl.when(step > 0)
        def _():
            start_back(step, block)

        stores = [
            pltpu.make_async_copy(units, units_hbm.at[block], store_sem.at[0]),
            pltpu.make_async_copy(gate_grad, gate_grad_hbm.at[block], store_sem.at[1]),
            pltpu.make_async_copy(up_grad, up_grad_hbm.at[block], store_sem.at[2]),
            pltpu.make_async_copy(top, pair_grad_hbm.at[block], store_sem.at[3]),
            pltpu.make_async_copy(rows, weighted_hbm.at[block], store_sem.at[4]),
        ]
        for store in stores:
            store.start()

        for store in stores:
            store.wait()

    @pl.loop(0, planes + 1)
    def _(step):
        @pl.when(step < planes)
        def _():
            send_step(step)

        @pl.when(step > 0)
        def _():
            expert_step(step - 1)

    start_back(0, z)

    for hop in range(1, planes):

        @pl.when((z - (hop - 1) >= 0) & (z + 1 < planes))
        def _():
            wait_bytes(plane_rows.at[0], line_send.at[0, hop])

        @pl.when((z + (hop - 1) < planes) & (z > 0))
        def _():
            wait_bytes(plane_rows.at[0], line_send.at[1, hop])

    @pl.loop(1, planes)
    def _(offset):
        wait_bytes(plane_shares.at[0], plane_share_send.at[(z + offset) % planes])

    def sum_copy(block):
        return remote(plane_rows.at[block], partial_in.at[z], sum_send.at[block], sum_recv.at[z], (block, x, w))

    def sum_share_copy(block):
        return remote(
            share_home.at[block], share_grad_ref.at[pl.ds(z * in_plane, in_plane)],
            sum_share_send.at[block], sum_share_recv.at[z], (block, x, w),
        )

    @pl.loop(0, planes)
    def _(turn):
        step = (turn + 1) % planes
        block, _, _ = order(step)
        wait_bytes(back_hbm.at[block], back_recv.at[step])
        load = pltpu.make_async_copy(back_hbm.at[block], rows, load_sem)
        load.start()
        wait_bytes(share_home.at[block], back_share_recv.at[step])
        load.wait()

        @pl.when(step > 0)
        def _():
            sum_share_copy(block).start()

            @pl.loop(0, width // chunk)
            def _(part):
                wide = pl.ds(pl.multiple_of(part * chunk, chunk), chunk)
                plane_rows[block, :, wide] = dot_tn(chosen[step], rows[:, wide]).astype(BF16)

            sum_copy(block).start()

        @pl.when(step == 0)
        def _():
            share_grad_ref[pl.ds(z * in_plane, in_plane)] = share_home[z]

            @pl.loop(0, width // chunk)
            def _(part):
                wide = pl.ds(pl.multiple_of(part * chunk, chunk), chunk)
                row_grad_ref[:, wide] = dot_tn(chosen[0], rows[:, wide])

    @pl.loop(1, planes)
    def _(offset):
        other = (z + offset) % planes
        wait_bytes(partial_in.at[other], sum_recv.at[other])
        wait_bytes(share_home.at[other], sum_share_recv.at[other])

        @pl.loop(0, width // chunk)
        def _(part):
            wide = pl.ds(pl.multiple_of(part * chunk, chunk), chunk)
            row_grad_ref[:, wide] += partial_in[other, :, wide].astype(F32)

    @pl.loop(1, planes)
    def _(offset):
        other = (z + offset) % planes
        wait_bytes(plane_rows.at[other], sum_send.at[other])
        wait_bytes(share_home.at[other], sum_share_send.at[other])

    @pl.loop(0, planes)
    def _(step):
        wait_bytes(stage.at[step, pl.ds(0, count - capacity)], back_send.at[step])
        wait_bytes(share_back.at[step, pl.ds(0, in_plane - 1)], back_share_send.at[step])


def run_experts(planes, across, shards, capacity, own, shares, slots, my_slots, w_gate, w_up, w_down, top_rows):
    tokens, width = own.shape
    in_plane = across * shards
    count = in_plane * capacity
    units = w_gate.shape[1]
    experts = planes * in_plane
    hbm = pl.BlockSpec(memory_space=pl.ANY)
    vmem = pl.BlockSpec(memory_space=pltpu.VMEM)
    dma = pltpu.SemaphoreType.DMA
    flops = 12 * planes * count * width * units
    return pl.pallas_call(
        functools.partial(expert_kernel, planes, across, shards, capacity),
        in_specs=[vmem] * 7 + [hbm],
        out_specs=[hbm] * 7 + [vmem] * 2,
        out_shape=[
            jax.ShapeDtypeStruct((planes, count, width), BF16),
            jax.ShapeDtypeStruct((planes, count, width), BF16),
            jax.ShapeDtypeStruct((planes, count, width), BF16),
            jax.ShapeDtypeStruct((planes, count, units), BF16),
            jax.ShapeDtypeStruct((planes, count, units), BF16),
            jax.ShapeDtypeStruct((planes, count, units), BF16),
            jax.ShapeDtypeStruct((planes, count, width), BF16),
            jax.ShapeDtypeStruct((tokens, width), F32),
            jax.ShapeDtypeStruct((experts, 1, tokens), F32),
        ],
        scratch_shapes=[
            pltpu.VMEM((planes, tokens, width), BF16),
            pltpu.VMEM((planes, in_plane, 1, tokens), F32),
            pltpu.VMEM((planes, in_plane, 1, tokens), F32),
            pltpu.VMEM((planes, in_plane, 1, tokens), F32),
            pltpu.VMEM((planes, in_plane, 1, tokens), F32),
            pltpu.VMEM((planes, count, width), BF16),
            pltpu.VMEM((planes, count, tokens), BF16),
            pltpu.VMEM((count, width), BF16),
            pltpu.VMEM((count, width), BF16),
            pltpu.VMEM((count, units), BF16),
            pltpu.VMEM((count, units), BF16),
            pltpu.VMEM((count, units), BF16),
            pltpu.VMEM((count, 128), F32),
            pltpu.VMEM((planes, tokens, width), BF16),
            dma((2, planes + 1)), dma((2, planes + 1)), dma((planes,)), dma((planes,)),
            dma((planes,)), dma((planes,)), dma((planes,)), dma((planes,)),
            dma((planes,)), dma((planes,)), dma((planes,)), dma((planes,)),
            dma((planes,)), dma((planes,)), dma((planes,)), dma((planes,)),
            dma, dma, dma((5,)),
        ],
        compiler_params=pltpu.CompilerParams(vmem_limit_bytes=VMEM_LIMIT, collective_id=1, has_side_effects=True),
        cost_estimate=pl.CostEstimate(flops=4 * flops, bytes_accessed=100 * 10**6, transcendentals=2 * 10**6),
    )(own, shares, slots, my_slots, w_gate, w_up, w_down, top_rows)


def local(
    hidden_in, attn_gain, w_query, key_projection, value_projection, query_gain, key_gain, w_output, ffn_gain, w_router,
    routes, w_gate, w_up, w_down, cotangent,
):
    tokens_here, width = hidden_in.shape
    head_size = query_gain.shape[0]
    top_count = routes.shape[1]
    planes, across, shards = lax.axis_size("z"), lax.axis_size("x"), lax.axis_size("w")
    rings = planes * across
    device_count = rings * shards
    in_plane = across * shards
    experts = device_count
    capacity = 5 * tokens_here * top_count // (4 * experts)
    seq_length = tokens_here * shards
    plane, column, shard = lax.axis_index("z"), lax.axis_index("x"), lax.axis_index("w")

    small = jnp.concatenate([w_router, attn_gain[:, None], ffn_gain[:, None]], axis=1)
    depth = w_query.shape[0]
    merged = jnp.concatenate(
        [
            w_query.reshape(depth, shards, -1),
            key_projection.reshape(depth, shards, -1),
            value_projection.reshape(depth, shards, -1),
        ],
        axis=2,
    ).reshape(depth, -1)
    hidden_all = lax.all_gather(hidden_in, "w", axis=0, tiled=True)
    small_all = lax.all_gather(small, "w", axis=0, tiled=True)
    weights = lax.all_to_all(merged, "w", split_axis=1, concat_axis=0, tiled=True)
    router_full = small_all[:, :experts]
    attn_scale = small_all[:, experts].astype(F32)[None, :]
    ffn_scale = small_all[:, experts + 1].astype(F32)[None, :]
    cosine, sine = rope_tables(seq_length, head_size)
    query_gain_row, key_gain_row = query_gain[None, :], key_gain[None, :]

    capacity = -(-capacity // 16) * 16
    routes_all = lax.all_gather(routes, ("z", "x", "w"), axis=0, tiled=True)
    routes_all = routes_all.reshape(planes, in_plane, tokens_here, top_count)
    me = column * shards + shard
    earlier = (
        jnp.arange(tokens_here)[:, None] < jnp.arange(tokens_here)[None, :]
    ).astype(BF16)

    def slots_of(hits):
        ranks = jnp.einsum("zps,st->zpt", hits.astype(BF16), earlier, preferred_element_type=F32).astype(jnp.int32)
        return jnp.where(hits, ranks, -1)

    routes_z = lax.dynamic_index_in_dim(routes_all, me, 1, keepdims=True)
    plane_experts = plane * in_plane + jnp.arange(in_plane, dtype=jnp.int32)
    slots = slots_of(jnp.any(routes_z == plane_experts[None, :, None, None], axis=3))
    my_slots = slots_of(jnp.any(routes_all == plane * in_plane + me, axis=3))
    slots_flat = slots.reshape(-1, 1, tokens_here)
    chosen = slots[:, :, None, :] == jnp.arange(capacity, dtype=jnp.int32)[None, None, :, None]
    chosen_flat = chosen.reshape(planes, in_plane * capacity, tokens_here).astype(BF16)

    def send_out(rows_z):
        packed = jnp.einsum("zst,ztd->zsd", chosen_flat, rows_z, preferred_element_type=F32).astype(BF16)
        packed = packed.reshape(planes, in_plane, capacity, width).transpose(1, 0, 2, 3)
        got = lax.all_to_all(
            packed.reshape(in_plane, planes * capacity, width), ("x", "w"), split_axis=0, concat_axis=0, tiled=True
        )
        return got.reshape(in_plane * planes * capacity, width)

    cotangent_z = lax.all_gather(cotangent, "z", axis=0, tiled=False)
    grads_in = send_out(cotangent_z)

    first_input, query_raw, key_raw, value, attended, branch_part = run_forward(
        hidden_all, attn_scale, weights, w_output, query_gain_row, key_gain_row, cosine, sine
    )
    branch = lax.psum_scatter(branch_part, "w", scatter_dimension=0, tiled=True).astype(F32)
    source = hidden_in.astype(F32)
    first_normed, first_scale = norm_forward(source)
    middle = source + branch
    second_normed, second_scale = norm_forward(middle)
    second_input = (second_normed * ffn_scale).astype(BF16)
    logits = lax.dot_general(router_full, second_input, (((0,), (1,)), ((), ())), preferred_element_type=F32)
    expert_ids = jnp.arange(experts, dtype=jnp.int32)
    routed = jnp.any(routes.T[None, :, :] == expert_ids[:, None, None], axis=1)
    peaks = jnp.max(jnp.where(routed, logits, -jnp.inf), axis=0, keepdims=True)
    shifted = jnp.where(routed, jnp.exp(jnp.where(routed, logits - peaks, 0.0)), 0.0)
    shares = shifted / jnp.sum(shifted, axis=0, keepdims=True)

    rows_in, _, weighted, hidden_units, gate_grad, up_grad, pair_grad, row_grad_sum, share_grad = run_experts(
        planes, across, shards, capacity, second_input, shares[:, None, :], slots_flat,
        my_slots.reshape(-1, 1, tokens_here), w_gate[0], w_up[0], w_down[0],
        grads_in.reshape(in_plane, planes, capacity, width),
    )
    share_grad = share_grad[:, 0, :]
    rows_in, pair_grad = rows_in.reshape(-1, width), pair_grad.reshape(-1, width)
    units = w_gate.shape[2]
    grad_down = dot_tn(hidden_units.reshape(-1, units), pair_grad)[None]
    grad_gate = dot_tn(rows_in, gate_grad.reshape(-1, units))[None]
    grad_up = dot_tn(rows_in, up_grad.reshape(-1, units))[None]
    grad_top = cotangent.astype(F32)
    share_center = jnp.sum(shares * share_grad, axis=0, keepdims=True)
    logit_grad = (shares * (share_grad - share_center)).astype(BF16)
    router_grad = dot_tn(second_input, logit_grad.T)
    second_grad = row_grad_sum + dot_nt(logit_grad.T, router_full)
    ffn_gain_grad = jnp.sum(second_grad * second_normed, axis=0)
    middle_grad = grad_top + norm_backward(second_grad * ffn_scale, second_normed, second_scale)
    wo_grad, wq_grad, first_part, query_gain_grad, key_gain_grad, _, expert_sum = run_backward(
        planes, across, shards, capacity, middle_grad.astype(BF16), w_output, attended, query_raw, key_raw, value,
        first_input, weights, query_gain_row, key_gain_row, cosine, sine, slots_flat, weighted,
    )
    hidden_out = (middle + expert_sum).astype(BF16)
    sum_query, sum_key, sum_value, sum_output, first_grad = run_reduce(
        planes, across, shards, wq_grad, wo_grad, first_part, w_query.shape[1], key_projection.shape[1]
    )
    attn_gain_grad = jnp.sum(first_grad * first_normed, axis=0)
    grad_in = middle_grad + norm_backward(first_grad * attn_scale, first_normed, first_scale)

    squares = jnp.stack(
        [jnp.sum(source * source), jnp.sum(branch * branch), jnp.sum(expert_sum * expert_sum), jnp.sum(grad_in * grad_in)]
    )
    mine = width // device_count
    shared = jnp.concatenate([query_gain_grad[0], key_gain_grad[0], squares])
    parts = jnp.concatenate(
        [
            router_grad.reshape(device_count, mine * experts),
            ffn_gain_grad.reshape(device_count, mine),
            attn_gain_grad.reshape(device_count, mine),
            jnp.broadcast_to(shared[None, :], (device_count, shared.shape[0])),
        ],
        axis=1,
    )
    length = parts.shape[1]
    padded = -(-length // 1024) * 1024
    parts = jnp.pad(parts, ((0, 0), (0, padded - length))).reshape(device_count, padded // 128, 128)
    summed = run_total(planes, across, shards, parts).reshape(-1)
    sum_router = summed[: mine * experts].reshape(mine, experts)
    sum_ffn = summed[mine * experts : mine * (experts + 1)]
    sum_attn = summed[mine * (experts + 1) : mine * (experts + 2)]
    totals = summed[mine * (experts + 2) : length]
    root_mean_squares = jnp.sqrt(totals[2 * head_size :] / (tokens_here * device_count * width))
    return (
        hidden_out,
        grad_in,
        sum_attn,
        sum_query,
        sum_key,
        sum_value,
        totals[:head_size],
        totals[head_size : 2 * head_size],
        sum_output,
        sum_ffn,
        sum_router,
        grad_gate,
        grad_up,
        grad_down,
        root_mean_squares,
    )


def solution(mesh):
    rings, shards = mesh.shape["ep"], mesh.shape["ws"]
    planes = 4 if rings % 4 == 0 else 1
    fine = Mesh(mesh.devices.reshape(planes, rings // planes, shards), ("z", "x", "w"))
    every = ("z", "x", "w")
    rows, deep = P(every, None), P(every, None, None)
    return jax.shard_map(
        local,
        mesh=fine,
        in_specs=(
            rows, P("w"), P("w", None), P("w", None), P("w", None), P(), P(), P("w", None), P("w"), P("w", None),
            rows, deep, deep, deep, rows,
        ),
        out_specs=(
            rows, rows, P(every), rows, rows, rows, P(), P(), rows, P(every), rows, deep, deep, deep, P(),
        ),
        check_vma=False,
    )
```

time: 1560 us -> 1080 us (0.69)
  waiting for transfers between devices: 786 us -> 124 us
  Pallas kernels: 127 us -> 690 us
  blocking collectives: 281 us -> 126 us
  matrix products: 174 us -> 58 us
  other arithmetic: 64.1 us -> 22.8 us
  local copies, waits for them, and re-layouts: 62.6 us -> 30 us
  starting transfers between devices: 41.9 us -> 10.7 us
    pallas_call x1 -> x4, Pallas kernels: 73.2 us -> 636 us  [the longest x1 272 us: run_experts(): pl.pallas_call(functools.partial(expert_kernel, planes, across, shards, c...]
    reduce_scatter x5 -> x0, waiting for transfers between devices: 199 us -> none  [the longest x2 142 us: send_back(): lax.psum_scatter(summed.reshape(planes * tokens_here, width), 'z', scatte...]
    all_to_all x3 -> x0, blocking collectives: 139 us -> none  [the longest x1 123 us: send_back(): lax.all_to_all(rows.reshape(in_plane, planes * capacity, width), ('x', 'w...]
    all_to_all x4 -> x0, waiting for transfers between devices: 136 us -> none  [the longest x1 128 us: send_back(): lax.all_to_all(rows.reshape(in_plane, planes * capacity, width), ('x', 'w...]
    unnamed x12 -> x3, waiting for transfers between devices: 127 us -> 1.39 us
    all_gather x2 -> x0, waiting for transfers between devices: 104 us -> none  [the longest x1 68.9 us: local(): rows_z = lax.all_gather(second_input, 'z', axis=0, tiled=False)]
    all_gather x1, waiting for transfers between devices: 80.8 us -> 0.02 us  [local(): cotangent_z = lax.all_gather(cotangent, 'z', axis=0, tiled=False)]
    all_to_all x2 -> x1, waiting for transfers between devices: 97.2 us -> 34.9 us  [send_out(): lax.all_to_all(packed.reshape(in_plane, planes * capacity, width), ('x',...]
  transfers between devices with their start and end apart: 19 -> 5, of which waited for: 13 -> 2; matrix products, arithmetic and copies ran while one was open for 11% -> 3% of each run, Pallas kernels for 0% -> 5%
where the time goes in v2:
time: 1080 us
  Pallas kernels  690 us (64%)
  blocking collectives  126 us (12%)
  waiting for transfers between devices  124 us (11%)
  matrix products  58 us (5%)
  local copies, waits for them, and re-layouts  30 us (3%)
  other arithmetic  22.8 us (2%)
  between operations  14.6 us (1%)
    pallas_call x1, Pallas kernels, run_experts(): pl.pallas_call(functools.partial(expert_kernel, planes, across, shards, c...  272 us
    pallas_call x1, Pallas kernels, run_backward(): pl.pallas_call(functools.partial(attention_backward, planes, across, shar...  181 us
    pallas_call x1, Pallas kernels, run_reduce(): pl.pallas_call(functools.partial(reduce_kernel, planes, across, shards),...  140 us
    reduce_scatter x1, waiting for transfers between devices, local(): lax.psum_scatter(branch_part, 'w', scatter_dimension=0, tiled=True)  88 us
    all_gather x1, blocking collectives, local(): small_all = lax.all_gather(small, 'w', axis=0, tiled=True)  82.9 us
    pallas_call x1, Pallas kernels, run_forward(): pl.pallas_call(functools.partial(attention_forward, pair), grid=(steps,),...  54.1 us
    dot_general x4, matrix products, dot_tn(): lax.dot_general(left, right, (((0,), (0,)), ((), ())), preferred_element_...  44.4 us
    all_gather x1, blocking collectives, local(): routes_all = lax.all_gather(routes, ('z', 'x', 'w'), axis=0, tiled=True)  42.8 us
  transfers between devices with their start and end apart: 5, of which 2 were waited for; matrix products, arithmetic and copies ran while one was open for 3% of the time, Pallas kernels for 5%

profile of v2, /device:TPU:1, one launch (start us, length us, event | category | flops | bytes accessed | tf_op | source)
XLA Modules:
  0.0 1075.8 jit_solution(4185743846360745582)
XLA Ops:
  8.7 2.8 copy.71
  11.7 2.9 pad_maximum_fusion
  14.6 5.2 all-to-all-start
  20.1 82.9 %all_gather.16 = bf16[2048,34]{0,1:T(8,128)(2,1)S(1)} all-gather(bf16[512,34]{0,1:T(8,128)(2,1)S(1)} %pad_maximum_fusion.3), channel_id=1, replica_groups=mesh['z'=4,'x'=2,'w'=4] {'w'}, dimensions={0}, use_global_device_ids=true | all-gather | bytes 174080 | tf_op jit(solution)/shard_map/all_gather | solution.py:1130
  103.0 42.8 %all_gather.17 = s32[8192,8]{0,1:T(8,128)S(1)} all-gather(s32[256,8]{0,1:T(8,128)S(1)} %copy-done.20), channel_id=1, replica_groups=mesh['z'=4,'x'=2,'w'=4] {'z','x','w'}, dimensions={0}, use_global_device_ids=true | all-gather | bytes 270336 | tf_op jit(solution)/shard_map/all_gather | solution.py:1139
  146.0 2.0 fusion.20
  149.9 54.1 %shard_map.262 = (bf16[1024,2048]{1,0:T(8,128)(2,1)}, f32[1024,1024]{1,0:T(8,128)}, f32[1024,128]{1,0:T(8,128)}, bf16[1024,128]{1,0:T(8,128)(2,1)}, bf16[1024,10...) custom-call(bf16[1024,2048]{1,0:T(8,128)(2,1)} %all-gather.4.cloned.1.call-done.hidden_ref, ...), custom_call_target="tpu_custom_call" | custom-call | flops 16000000000 | bytes 40000000 | tf_op jit(solution)/shard_map/pallas_call | solution.py:361
  204.6 9.3 convolution_convert_fusion
  213.9 10.7 copy.51
  224.6 5.4 all-to-all-start.1
  231.6 88.0 %reduce-scatter.2.cloned.1.call-done = bf16[256,2048]{1,0:T(8,128)(2,1)} async-done(((bf16[1024,2048]{1,0:T(8,128)(2,1)}), bf16[256,2048]{1,0:T(8,128)(2,1)}) %reduce-scatter.2.cloned.1.call-update) | async-done | bytes 1048592 | tf_op jit(solution)/shard_map/reduce_scatter | solution.py:1172
  323.0 34.9 %all-to-all-done.1 = bf16[8,320,2048]{2,1,0:T(8,128)(2,1)} async-done(((bf16[8,320,2048]{2,1,0:T(8,128)(2,1)}), bf16[8,320,2048]{2,1,0:T(8,128)(2,1)}, u32[]{:S(2)}, u32[]{:S(2)}) %all-to-all-start.1) | async-done | bytes 10485792 | tf_op jit(solution)/shard_map/all_to_all | solution.py:1161
  357.9 272.0 %shard_map.263 = (bf16[4,640,2048]{2,1,0:T(8,128)(2,1)}, bf16[4,640,2048]{2,1,0:T(8,128)(2,1)}, bf16[4,640,2048]{2,1,0:T(8,128)(2,1)}, bf16[4,640,768]{2,1,0:T(8...) custom-call(bf16[256,2048]{1,0:T(8,128)(2,1)} %copy-done.7, ...), custom_call_target="tpu_custom_call" | custom-call | flops 193273528320 | bytes 100000000 | tf_op jit(solution)/shard_map/pallas_call | solution.py:1062
  631.7 2.7 fusion.34
  634.5 3.5 multiply_reduce_fusion.2
  639.9 181.3 %shard_map.264 = (bf16[1024,2048]{1,0:T(8,128)(2,1)}, bf16[2048,1280]{1,0:T(8,128)(2,1)}, bf16[1024,2048]{1,0:T(8,128)(2,1)}, f32[8,128]{1,0:T(8,128)}, f32[8,12...) custom-call(bf16[256,2048]{1,0:T(8,128)(2,1)} %fusion.31.own_grad_ref, bf16[1024,2048]{1,0:T(8,128)(2,1)} %wo_ref.3, ...), custom_call_target="tpu_custom_call" | custom-call | flops 70000001024 | bytes 60000000 | tf_op jit(solution)/shard_map/pallas_call | solution.py:418
  821.2 139.9 %shard_map.265 = (f32[64,4096]{1,0:T(8,128)}, f32[64,512]{1,0:T(8,128)}, f32[64,512]{1,0:T(8,128)}, f32[128,2048]{1,0:T(8,128)}, f32[256,2048]{1,0:T(8,128)}) custom-call(bf16[2048,1280]{1,0:T(8,128)(2,1)} %get-tuple-element.50.wq_hbm, bf16[1024,2048]{1,0:T(8,128)(2,1)} %get-tuple-element.51.wo_hbm, bf16[1024,2048]{1,0:T(8,128)(2,1)} %get-tuple-element.52.first_hbm), custom_call_target="tpu_custom_call" | custom-call | flops 70000001024 | bytes 40000000 | tf_op jit(solution)/shard_map/pallas_call | solution.py:680
  961.2 2.3 fusion.10
  966.6 5.9 multiply_reduce_fusion.1
  972.5 2.7 concatenate.22
  976.2 42.4 %shard_map.266 = f32[24,128]{1,0:T(8,128)} custom-call(f32[32,24,128]{2,1,0:T(8,128)} %bitcast.95), custom_call_target="tpu_custom_call" | custom-call | tf_op jit(solution)/shard_map/pallas_call | solution.py:741
  1023.1 14.3 %convolution_bitcast_fusion.1 = f32[1,2048,768]{2,1,0:T(8,128)} fusion(bf16[4,640,2048]{2,1,0:T(8,128)(2,1)} %get-tuple-element.60, bf16[4,640,768]{2,1,0:T(8,128)(2,1)} %get-tuple-element.62), kind=kOutput, calls=%fused_computation.4 | convolution fusion | flops 8053063680 | bytes 20709376 | tf_op jit(solution)/shard_map/dot_general | solution.py:24
  1037.4 13.2 %convolution_bitcast_fusion.2 = f32[1,2048,768]{2,1,0:T(8,128)} fusion(bf16[4,640,2048]{2,1,0:T(8,128)(2,1)} %get-tuple-element.60, bf16[4,640,768]{2,1,0:T(8,128)(2,1)S(1)} %copy-done.26), kind=kOutput, calls=%fused_computation.5 | convolution fusion | flops 8053063680 | bytes 20709376 | tf_op jit(solution)/shard_map/dot_general | solution.py:24
  1051.3 14.2 %convolution_bitcast_fusion = f32[1,768,2048]{2,1,0:T(8,128)} fusion(bf16[4,640,768]{2,1,0:T(8,128)(2,1)} %get-tuple-element.63, bf16[4,640,2048]{2,1,0:T(8,128)(2,1)} %get-tuple-element.64), kind=kOutput, calls=%fused_computation.3 | convolution fusion | flops 8053063680 | bytes 20709376 | tf_op jit(solution)/shard_map/dot_general | solution.py:24
  (115 shorter events, 25.8 us)
Async XLA Ops:
  7.2 4.4 copy-start
  7.2 142.7 %all-gather.4.cloned.1.call-start = ((), (), s32[]{:S(2)}) async-start(), calls=%async_computation.3 | async-start | bytes 5242880 | tf_op jit(solution)/shard_map/all_gather | solution.py:1129
  7.9 196.7 %all-gather.6.cloned.1.call-start = ((), (), s32[]{:S(2)}) async-start(), calls=%async_computation.5 | async-start | bytes 5242880 | tf_op jit(solution)/shard_map/all_gather | solution.py:1166
  14.6 5.3 copy-start.24
  14.6 5.3 copy-start.25
  14.6 5.4 copy-start.21
  14.6 88.4 %copy-start.20 = (s32[256,8]{0,1:T(8,128)S(1)}, s32[256,8]{0,1:T(8,128)}, u32[]{:S(2)}) copy-start(s32[256,8]{0,1:T(8,128)} %param.25) | copy-start | bytes 24580
  14.6 135.2 %all-to-all-start = ((bf16[512,4,1280]{2,0,1:T(8,128)(2,1)}), bf16[512,4,1280]{2,0,1:T(8,128)(2,1)}, u32[]{:S(2)}, u32[]{:S(2)}) async-start(bf16[512,4,1280]{2,0,1:T(8,128)(2,1)} %pad_maximum_fusion), calls=%async_computation | async-start | bytes 10485760 | tf_op jit(solution)/shard_map/all_to_all | solution.py:1131
  19.9 299.7 %reduce-scatter.2.cloned.1.call-start = ((), (), s32[]{:S(2)}) async-start(), calls=%async_computation.4 | async-start | bytes 5242880 | tf_op jit(solution)/shard_map/reduce_scatter | solution.py:1172
  103.0 218.9 %copy-start.11 = (bf16[2048,34]{0,1:T(8,128)(2,1)}, bf16[2048,34]{0,1:T(8,128)(2,1)S(1)}, u32[]{:S(2)}) copy-start(bf16[2048,34]{0,1:T(8,128)(2,1)S(1)} %all_gather.16) | copy-start | bytes 417796
  149.9 171.5 %copy-start.15 = (f32[2048,1]{0,1:T(1,128)}, f32[2048,1]{0,1:T(1,128)S(1)}, u32[]{:S(2)}) copy-start(f32[2048,1]{0,1:T(1,128)S(1)} %get-tuple-element.125) | copy-start | bytes 24580
  224.6 95.0 %copy-start.2 = (bf16[256,2048]{1,0:T(8,128)(2,1)S(1)}, bf16[256,2048]{1,0:T(8,128)(2,1)}, u32[]{:S(2)}) copy-start(bf16[256,2048]{1,0:T(8,128)(2,1)} %param.15) | copy-start | bytes 3145732
  224.6 133.3 %all-to-all-start.1 = ((bf16[8,320,2048]{2,1,0:T(8,128)(2,1)}), bf16[8,320,2048]{2,1,0:T(8,128)(2,1)}, u32[]{:S(2)}, u32[]{:S(2)}) async-start(bf16[8,320,2048]{2,1,0:T(8,128)(2,1)} %bitcast.91), calls=%async_computation.2 | async-start | bytes 20971520 | tf_op jit(solution)/shard_map/all_to_all | solution.py:1161
  321.8 36.1 %copy-start.7 = (bf16[256,2048]{1,0:T(8,128)(2,1)}, bf16[256,2048]{1,0:T(8,128)(2,1)S(1)}, u32[]{:S(2)}) copy-start(bf16[256,2048]{1,0:T(8,128)(2,1)S(1)} %multiply_convert_fusion.own_ref) | copy-start | bytes 3145732
  322.4 35.6 %copy-start.13 = (f32[32,256]{1,0:T(8,128)}, f32[32,256]{1,0:T(8,128)S(1)}, u32[]{:S(2)}) copy-start(f32[32,256]{1,0:T(8,128)S(1)} %fusion.27) | copy-start | bytes 98308
  630.0 4.5 copy-start.3
  630.0 4.4 copy-start.5
  630.0 4.4 copy-start.12
  630.0 4.4 copy-start.23
  634.4 3.6 copy-start.6
  634.4 3.6 copy-start.16
  821.2 139.9 %copy-start.19 = (f32[2048,1]{0,1:T(1,128)S(1)}, f32[2048,1]{0,1:T(1,128)}, u32[]{:S(2)}) copy-start(f32[2048,1]{0,1:T(1,128)} %get-tuple-element.123) | copy-start | bytes 24580
  1023.1 14.3 %copy-start.26 = (bf16[4,640,768]{2,1,0:T(8,128)(2,1)S(1)}, bf16[4,640,768]{2,1,0:T(8,128)(2,1)}, u32[]{:S(2)}) copy-start(bf16[4,640,768]{2,1,0:T(8,128)(2,1)} %get-tuple-element.61) | copy-start | bytes 11796484
  1051.3 14.3 %copy-start.10 = (f32[64,4096]{1,0:T(8,128)S(1)}, f32[64,4096]{1,0:T(8,128)}, u32[]{:S(2)}) copy-start(f32[64,4096]{1,0:T(8,128)} %get-tuple-element.158) | copy-start | bytes 3145732
  (8 other events, 15.8 us)
Sparse Core Ops, SparseCore 0:
  9.6 58.4 all-gather.3
  69.7 80.5 all-gather.5
  204.1 115.4 reduce-scatter.1

commit v3 on v2

--- a/solution.py
+++ b/solution.py
@@ -13,7 +13,7 @@
 ROPE_BASE = 1000000.0
 F32 = jnp.float32
 BF16 = jnp.bfloat16
-VMEM_LIMIT = 60 * 1024 * 1024
+VMEM_LIMIT = 62 * 1024 * 1024
 
 
 def dot(left, right):
@@ -98,23 +98,237 @@
 
 
 def attention_forward(
-    heads_a_step, hidden_ref, gain_ref, wq_ref, wkv_ref, query_gain_ref, key_gain_ref, cosine_ref, sine_ref, wo_ref,
-    input_ref, query_raw_ref, key_raw_ref, value_ref, attended_ref, branch_ref, total_ref, key_rot_ref,
+    planes, across, shards, capacity, heads_a_step,
+    own_ref, small_ref, routes_ref, top_ref, wq_hbm, wk_hbm, wv_hbm, query_gain_ref, key_gain_ref, cosine_ref, sine_ref, wo_ref,
+    input_ref, query_raw_ref, key_raw_ref, value_ref, attended_ref, branch_ref, slots_ref, my_slots_ref, small_hbm,
+    weights_hbm, top_rows_hbm,
+    hidden, small_in, weights, key_rot_ref, routes_in, far_slots, plane_rows, stage, chosen, pair_out, far_out,
+    gather_send, gather_recv, gain_send, gain_recv, weight_send, weight_recv, route_send, route_recv, plane_route_send,
+    plane_route_recv, far_send, far_recv,
+    line_send, line_recv, top_send, top_recv, pair_send, pair_recv, store_sem, small_sem,
 ):
     step = pl.program_id(0)
     head_size = cosine_ref.shape[1]
+    last = wo_ref.shape[0] // (heads_a_step * head_size)
     seq_length = cosine_ref.shape[0]
     blocks = seq_length // BLOCK
     factor = head_size ** (-0.5)
+    z, x, w = lax.axis_index("z"), lax.axis_index("x"), lax.axis_index("w")
+    in_plane = across * shards
+    tokens, width = own_ref.shape
+    me = x * shards + w
+    depth = width // shards
+    experts = planes * in_plane
+    wide = heads_a_step * head_size
+    chunk = 512
+    targets = in_plane // 2
+    pair, core = w // 2, w % 2
+    sibling, opposite, other = pair * 2 + 1 - core, (1 - pair) * 2 + core, (1 - pair) * 2 + 1 - core
+
+    def slice_of(index):
+        return pl.ds(pl.multiple_of(index * capacity, 16), capacity)
+
+    def tokens_of(index):
+        return pl.ds(pl.multiple_of(index * tokens, tokens), tokens)
+
+    def gather_copy(kind, owner, target):
+        return remote(
+            hidden.at[tokens_of(owner)], hidden.at[tokens_of(owner)], gather_send.at[kind], gather_recv.at[kind],
+            (z, x, target),
+        )
+
+    def gain_copy(offset):
+        return remote(small_ref, small_in.at[w], gain_send.at[offset], gain_recv.at[w], (z, x, (w + offset) % shards))
+
+    def columns_at(start, size):
+        return pl.ds(pl.multiple_of(start, 128), size)
+
+    my_depth = pl.ds(pl.multiple_of(w * depth, 16), depth)
+    query_wide = last * wide
+
+    def weight_pieces(piece, target):
+        if piece is None:
+            key_at, value_at = columns_at(target * head_size, head_size), columns_at(target * head_size, head_size)
+            return [
+                (wk_hbm.at[:, key_at], weights.at[my_depth, columns_at(last * wide, head_size)], last),
+                (wv_hbm.at[:, value_at], weights.at[my_depth, columns_at(last * wide + head_size, head_size)], last),
+            ]
+        return [
+            (
+                wq_hbm.at[:, columns_at(target * query_wide + piece * wide, wide)],
+                weights.at[my_depth, columns_at(piece * wide, wide)], piece,
+            )
+        ]
+
+    def start_weights(piece):
+        @pl.loop(1, shards)
+        def _(offset):
+            for source, goal, sem in weight_pieces(piece, (w + offset) % shards):
+                remote(source, goal, weight_send.at[sem], weight_recv.at[sem], (z, x, (w + offset) % shards)).start()
+
+        for source, goal, sem in weight_pieces(piece, w):
+            pltpu.make_async_copy(source, goal, weight_recv.at[sem]).start()
+
+    def wait_weights(piece):
+        whole_piece = weights.at[:, columns_at(piece * wide, wide)]
+        wait_bytes(whole_piece, weight_recv.at[piece])
+
+    def line_copy(column, block, hop, direction):
+        rows = plane_rows.at[column, block]
+        return remote(
+            rows, rows, line_send.at[column, direction, hop], line_recv.at[column, direction, hop],
+            (z + 1 - 2 * direction, x, w),
+        )
+
+    def start_line(column, block, hop, upward, downward):
+        @pl.when(upward & (z + 1 < planes))
+        def _():
+            line_copy(column, block, hop, 0).start()
+
+        @pl.when(downward & (z > 0))
+        def _():
+            line_copy(column, block, hop, 1).start()
+
+    def relay(column, turn):
+        block, hop, below = line_order(z, planes, turn)
+        wait_bytes(plane_rows.at[column, block], line_recv.at[column, 1 - below, hop])
+        start_line(column, block, hop + 1, below == 1, below == 0)
+
+    expert_of = z * in_plane + lax.broadcasted_iota(jnp.int32, (in_plane, tokens), 0)
+    earlier = (
+        lax.broadcasted_iota(jnp.int32, (tokens, tokens), 0) < lax.broadcasted_iota(jnp.int32, (tokens, tokens), 1)
+    ).astype(F32).astype(BF16)
+    slot_ids = lax.broadcasted_iota(jnp.int32, (capacity, tokens), 0)
+
+    def fill_slots(column, table):
+        @pl.loop(0, planes)
+        def _(block):
+            hits = jnp.zeros((in_plane, tokens), F32)
+            for k in range(routes_ref.shape[0]):
+                hits += (routes_in[column, block, k : k + 1, :] == expert_of).astype(F32)
+            ranks = dot(hits.astype(BF16), earlier).astype(jnp.int32)
+            slots = jnp.where(hits > 0.0, ranks, -1)
+            for index in range(in_plane):
+                table[block * in_plane + index] = slots[index : index + 1, :]
+
+    def pack(column, turn, table):
+        block, _, _ = line_order(z, planes, turn)
+
+        def index_of(target):
+            return (target // 2) * shards + pair * 2 + target % 2
+
+        for target in range(targets):
+            slots = table[block * in_plane + index_of(target)]
+            chosen[target * capacity : (target + 1) * capacity, :] = (slot_ids == slots).astype(F32).astype(BF16)
+
+        @pl.loop(0, width // chunk)
+        def _(part):
+            here = pl.ds(pl.multiple_of(part * chunk, chunk), chunk)
+            stage[column, turn, :, here] = dot(chosen[...], plane_rows[column, block, :, here]).astype(BF16)
+
+        source = x * shards + (w if column == 0 else opposite)
+        mine = x * 2 + core
+
+        @pl.loop(1, targets)
+        def _(offset):
+            target = (mine + offset) % targets
+            remote(
+                stage.at[column, turn, slice_of(target)], top_rows_hbm.at[block, slice_of(source)],
+                top_send.at[column, turn], top_recv.at[block], (z, target // 2, pair * 2 + target % 2),
+            ).start()
+
+        pltpu.make_async_copy(
+            stage.at[column, turn, slice_of(mine)], top_rows_hbm.at[block, slice_of(source)], top_recv.at[block]
+        ).start()
+
+    def route_copy(offset):
+        return remote(
+            routes_ref, routes_in.at[me, z], route_send.at[offset], route_recv.at[z], ((z + offset) % planes, x, w)
+        )
+
+    far_top = remote(top_ref, plane_rows.at[1, z], far_send, far_recv, (z, x, opposite))
+    opposite_me = x * shards + opposite
+
+    def plane_route_copy(index):
+        return remote(
+            routes_in.at[me], routes_in.at[me], plane_route_send, plane_route_recv.at[me],
+            (z, index // shards, index % shards),
+        )
+
+    def fill_my_slots():
+        my_expert = z * in_plane + me
+
+        @pl.loop(0, planes)
+        def _(block):
+            hits = jnp.concatenate(
+                [
+                    jnp.max((routes_in[index, block] == my_expert).astype(F32), axis=0, keepdims=True)
+                    for index in range(in_plane)
+                ],
+                axis=0,
+            )
+            ranks = dot(hits.astype(BF16), earlier).astype(jnp.int32)
+            slots = jnp.where(hits > 0.0, ranks, -1)
+            for index in range(in_plane):
+                my_slots_ref[block * in_plane + index] = slots[index : index + 1, :]
 
     @pl.when(step == 0)
     def _():
+        greet_plane_and_line(planes, across, shards)
+        hidden[tokens_of(w), :] = own_ref[...]
+        gather_copy(1, w, opposite).start()
+
+        @pl.loop(1, shards)
+        def _(offset):
+            gain_copy(offset).start()
+
+        @pl.loop(1, planes)
+        def _(offset):
+            route_copy(offset).start()
+
+        plane_rows[0, z] = top_ref[...]
+        start_line(0, z, 1, True, True)
+        gather_copy(0, w, sibling).start()
+        start_weights(None)
+        start_weights(0)
+        small_in[w] = small_ref[...]
+        routes_in[me, z] = routes_ref[...]
+
+        @pl.loop(1, planes)
+        def _(offset):
+            source = (z + offset) % planes
+            wait_bytes(routes_in.at[me, source], route_recv.at[source])
+
+        @pl.loop(1, in_plane)
+        def _(offset):
+            plane_route_copy((me + offset) % in_plane).start()
+
+        fill_slots(me, slots_ref)
+        pack(0, 0, slots_ref)
+        wait_bytes(hidden.at[tokens_of(opposite)], gather_recv.at[1])
+        gather_copy(2, opposite, sibling).start()
+        far_top.start()
+        start_weights(1)
+        relay(0, 1)
+        wait_bytes(hidden.at[tokens_of(sibling)], gather_recv.at[0])
+        wait_bytes(hidden.at[tokens_of(other)], gather_recv.at[2])
+
+        @pl.loop(1, shards)
+        def _(offset):
+            source = (w + offset) % shards
+            wait_bytes(small_in.at[source], gain_recv.at[source])
+
         for block in range(blocks):
             rows = pl.ds(block * BLOCK, BLOCK)
-            normed, _ = norm_forward(hidden_ref[rows, :].astype(F32))
-            first_input = (normed * gain_ref[...]).astype(BF16)
-            input_ref[rows, :] = first_input
-            key_value = dot(first_input, wkv_ref[...])
+            normed, _ = norm_forward(hidden[rows, :].astype(F32))
+            for part in range(shards):
+                here = slice(part * depth, (part + 1) * depth)
+                input_ref[rows, here] = (normed[:, here] * small_in[part, experts + 1 : experts + 2, :]).astype(BF16)
+        pack(0, 1, slots_ref)
+        wait_weights(last)
+        for block in range(blocks):
+            rows = pl.ds(block * BLOCK, BLOCK)
+            key_value = dot(input_ref[rows, :], weights[:, columns_at(last * wide, wide)])
             key_raw = key_value[:, :head_size]
             key_raw_ref[rows, :] = key_raw
             value_ref[rows, :] = key_value[:, head_size:].astype(BF16)
@@ -122,35 +336,153 @@
             key_rot_ref[rows, :] = rotate(
                 key_normed * key_gain_ref[...], cosine_ref[rows, :], sine_ref[rows, :]
             ).astype(BF16)
-
-    for block in range(blocks):
-        rows = pl.ds(block * BLOCK, BLOCK)
-        seen = pl.ds(0, (block + 1) * BLOCK)
-        query_raw = dot(input_ref[rows, :], wq_ref[...])
-        query_raw_ref[rows, :] = query_raw
-        for head in range(heads_a_step):
-            columns = slice(head * head_size, (head + 1) * head_size)
-            query_normed, _ = norm_forward(query_raw[:, columns])
-            query_rot = rotate(
-                query_normed * query_gain_ref[...], cosine_ref[rows, :], sine_ref[rows, :]
-            ).astype(BF16)
-            scores = dot_nt(query_rot, key_rot_ref[seen, :]) * factor
-            exponent = jnp.exp(scores - jnp.max(scores, axis=-1, keepdims=True))
-            probs = (exponent / jnp.sum(exponent, axis=-1, keepdims=True)).astype(BF16)
-            attended_ref[rows, columns] = dot(probs, value_ref[seen, :]).astype(BF16)
-        partial = dot(attended_ref[rows, :], wo_ref[...])
-
-        @pl.when(step == 0)
-        def _():
-            total_ref[rows, :] = partial
-
-        @pl.when(step > 0)
-        def _():
-            total_ref[rows, :] += partial
-
-    @pl.when(step == pl.num_programs(0) - 1)
-    def _():
-        branch_ref[...] = total_ref[...].astype(BF16)
+        relay(0, 2)
+
+    for piece in range(2, last):
+
+        @pl.when(step == piece - 2)
+        def _():
+            wait_weights(piece - 2)
+            if piece == last - 1:
+                for kind in range(3):
+                    wait_bytes(hidden.at[tokens_of(w)], gather_send.at[kind])
+            start_weights(piece)
+
+    @pl.when((step >= last - 2) & (step < last))
+    def _():
+        wait_weights(step)
+
+    @pl.when(step < last)
+    def _():
+        here = columns_at(step * wide, wide)
+        for block in range(blocks):
+            rows = pl.ds(block * BLOCK, BLOCK)
+            seen = pl.ds(0, (block + 1) * BLOCK)
+            query_raw = dot(input_ref[rows, :], weights[:, here])
+            query_raw_ref[rows, :] = query_raw
+            parts = []
+            for head in range(heads_a_step):
+                columns = slice(head * head_size, (head + 1) * head_size)
+                query_normed, _ = norm_forward(query_raw[:, columns])
+                query_rot = rotate(
+                    query_normed * query_gain_ref[...], cosine_ref[rows, :], sine_ref[rows, :]
+                ).astype(BF16)
+                scores = dot_nt(query_rot, key_rot_ref[seen, :]) * factor
+                exponent = jnp.exp(scores - jnp.max(scores, axis=-1, keepdims=True))
+                probs = (exponent / jnp.sum(exponent, axis=-1, keepdims=True)).astype(BF16)
+                parts.append(dot(probs, value_ref[seen, :]).astype(BF16))
+            attended_ref[rows, here] = jnp.concatenate(parts, axis=1)
+
+    @pl.when(step == 0)
+    def _():
+        pack(0, 2, slots_ref)
+        wait_bytes(routes_in.at[opposite_me], plane_route_recv.at[opposite_me])
+        fill_slots(opposite_me, far_slots)
+        wait_bytes(plane_rows.at[1, z], far_recv)
+        start_line(1, z, 1, True, True)
+        relay(0, 3)
+        pack(1, 0, far_slots)
+
+    @pl.when(step == 1)
+    def _():
+        pack(0, 3, slots_ref)
+        relay(1, 1)
+
+    @pl.when(step == 2)
+    def _():
+        pack(1, 1, far_slots)
+
+    @pl.when(step == 3)
+    def _():
+        relay(1, 2)
+
+    def project(owner, goal, added):
+        rows = tokens_of(owner)
+
+        @pl.loop(0, width // chunk)
+        def _(part):
+            here = pl.ds(pl.multiple_of(part * chunk, chunk), chunk)
+            value = dot(attended_ref[rows, :], wo_ref[:, here])
+            if added is not None:
+                value += hidden[added, here].astype(F32)
+            goal[:, here] = value.astype(goal.dtype)
+
+    def pair_copy(kind):
+        at = pl.ds(kind * tokens, tokens)
+        return remote(pair_out.at[kind], hidden.at[at], pair_send.at[kind], pair_recv.at[kind], (z, x, sibling))
+
+    far_at = pl.ds(2 * tokens, tokens)
+    far_copy = remote(far_out, hidden.at[far_at], pair_send.at[2], pair_recv.at[2], (z, x, opposite))
+
+    @pl.when(step == last)
+    def _():
+        store = pltpu.make_async_copy(weights, weights_hbm, store_sem)
+        store.start()
+        small_store = pltpu.make_async_copy(small_in, small_hbm, small_sem)
+        small_store.start()
+        project(other, pair_out.at[0], None)
+        pair_copy(0).start()
+        project(sibling, pair_out.at[1], None)
+        pair_copy(1).start()
+        wait_bytes(hidden.at[pl.ds(0, tokens)], pair_recv.at[0])
+        project(opposite, far_out, pl.ds(0, tokens))
+        far_copy.start()
+        wait_bytes(hidden.at[pl.ds(tokens, tokens)], pair_recv.at[1])
+        project(w, branch_ref, pl.ds(tokens, tokens))
+        pack(1, 2, far_slots)
+
+        @pl.loop(1, in_plane)
+        def _(offset):
+            index = (me + offset) % in_plane
+
+            @pl.when(index != opposite_me)
+            def _():
+                wait_bytes(routes_in.at[index], plane_route_recv.at[index])
+
+        fill_my_slots()
+        relay(1, 3)
+        pack(1, 3, far_slots)
+        wait_bytes(hidden.at[far_at], pair_recv.at[2])
+        branch_ref[...] += hidden[far_at, :].astype(F32)
+
+        @pl.loop(0, planes)
+        def _(block):
+            wait_bytes(top_rows_hbm.at[block], top_recv.at[block])
+            if targets > 1:
+                for column in range(2):
+                    wait_bytes(stage.at[column, 0, pl.ds(0, (targets - 1) * capacity)], top_send.at[column, block])
+
+        for kind in range(3):
+            wait_bytes(far_out, pair_send.at[kind])
+
+        @pl.loop(1, shards)
+        def _(offset):
+            wait_bytes(small_in.at[w], gain_send.at[offset])
+
+        @pl.loop(1, planes)
+        def _(offset):
+            wait_bytes(routes_in.at[0, 0], route_send.at[offset])
+
+        wait_bytes(routes_in.at[pl.ds(0, in_plane - 1)], plane_route_send)
+        wait_bytes(plane_rows.at[1, 0], far_send)
+
+        @pl.loop(0, last + 1)
+        def _(piece):
+            wait_bytes(weights.at[pl.ds(0, (shards - 1) * depth), pl.ds(0, wide)], weight_send.at[piece])
+
+        for column in range(2):
+            for hop in range(1, planes):
+
+                @pl.when((z - (hop - 1) >= 0) & (z + 1 < planes))
+                def _():
+                    wait_bytes(plane_rows.at[0, 0], line_send.at[column, 0, hop])
+
+                @pl.when((z + (hop - 1) < planes) & (z > 0))
+                def _():
+                    wait_bytes(plane_rows.at[0, 0], line_send.at[column, 1, hop])
+
+        store.wait()
+        small_store.wait()
 
 
 def attention_backward(
@@ -195,18 +527,23 @@
             back_send.at[block], back_recv.at[block], (z, index // shards, index % shards),
         )
 
-    def start_back(near):
-        @pl.loop(0, planes)
-        def _(turn):
-            block, _, _ = line_order(z, planes, planes - 1 - turn)
-
-            @pl.loop(1, in_plane)
-            def _(offset):
-                index = (me + offset) % in_plane
-
-                @pl.when((index % shards) // 2 == pair if near else (index % shards) // 2 != pair)
-                def _():
-                    back_copy(block, index).start()
+    def start_back(turn, near, far):
+        block, _, _ = line_order(z, planes, planes - 1 - turn)
+
+        @pl.loop(1, in_plane)
+        def _(offset):
+            index = (me + offset) % in_plane
+            beside = (index % shards) // 2 == pair
+
+            @pl.when((beside & near) | (jnp.logical_not(beside) & far))
+            def _():
+                back_copy(block, index).start()
+
+        @pl.when(near)
+        def _():
+            pltpu.make_async_copy(
+                weighted_hbm.at[block, slice_of(me)], returned_hbm.at[block, slice_of(me)], back_recv.at[block]
+            ).start()
 
     def sum_copy(block):
         return remote(partial_out.at[block], partial_in.at[z], sum_send.at[block], sum_recv.at[z], (block, x, w))
@@ -217,14 +554,7 @@
         grad_ref[tokens_of(w), :] = own_grad_ref[...]
         gather_copy(1, w, opposite).start()
         gather_copy(0, w, sibling).start()
-        start_back(True)
-
-        @pl.loop(0, planes)
-        def _(block):
-            pltpu.make_async_copy(
-                weighted_hbm.at[block, slice_of(me)], returned_hbm.at[block, slice_of(me)], back_recv.at[block]
-            ).start()
-
+        start_back(0, step == 0, step != 0)
         key_normed, _ = norm_forward(key_raw_ref[...])
         key_rot_ref[...] = rotate(key_normed * key_gain_ref[...], cosine_ref[...], sine_ref[...]).astype(BF16)
         key_grad_ref[...] = jnp.zeros_like(key_grad_ref)
@@ -235,9 +565,13 @@
             turned_ref[:, rows_here] = input_ref[rows_here, :].T
         wait_bytes(grad_ref.at[tokens_of(opposite)], gather_recv.at[1])
         gather_copy(2, opposite, sibling).start()
-        start_back(False)
+        start_back(0, step != 0, step == 0)
         wait_bytes(grad_ref.at[tokens_of(sibling)], gather_recv.at[0])
         wait_bytes(grad_ref.at[tokens_of(other)], gather_recv.at[2])
+
+    @pl.when((step > 0) & (step < planes))
+    def _():
+        start_back(step, step > 0, step > 0)
 
     @pl.when(step < last)
     def _():
@@ -351,34 +685,50 @@
     return pl.BlockSpec(shape, lambda step: (0,) * len(shape), pipeline_mode=pl.Buffered(1))
 
 
-def run_forward(hidden_all, gain, weights, wo, query_gain, key_gain, cosine, sine):
-    seq_length, width = hidden_all.shape
+def run_forward(
+    planes, across, shards, capacity, own, small, routes, top, w_query, w_key, w_value, query_gain, key_gain, cosine, sine, wo
+):
+    tokens, width = own.shape
+    seq_length = tokens * shards
     head_size = query_gain.shape[1]
     heads_here = wo.shape[0] // head_size
     pair = 2
     wide = pair * head_size
     steps = heads_here // pair
+    in_plane = across * shards
+    count = in_plane * capacity
+    hbm = pl.BlockSpec(memory_space=pl.ANY)
+    dma = pltpu.SemaphoreType.DMA
+    slots_shape = (planes * in_plane, 1, tokens)
     return pl.pallas_call(
-        functools.partial(attention_forward, pair),
-        grid=(steps,),
+        functools.partial(attention_forward, planes, across, shards, capacity, pair),
+        grid=(steps + 1,),
         in_specs=[
-            whole((seq_length, width)),
-            whole((1, width)),
-            pl.BlockSpec((width, wide), lambda step: (0, step)),
-            pl.BlockSpec((width, wide), lambda step: (0, steps), pipeline_mode=pl.Buffered(1)),
+            whole((tokens, width)),
+            whole(small.shape),
+            whole(routes.shape),
+            whole((tokens, width)),
+            hbm,
+            hbm,
+            hbm,
             whole((1, head_size)),
             whole((1, head_size)),
             whole((seq_length, head_size)),
             whole((seq_length, head_size)),
-            pl.BlockSpec((wide, width), lambda step: (step, 0)),
+            whole(wo.shape),
         ],
         out_specs=[
             whole((seq_length, width)),
-            pl.BlockSpec((seq_length, wide), lambda step: (0, step)),
+            pl.BlockSpec((seq_length, wide), lambda step: (0, jnp.minimum(step, steps - 1))),
             whole((seq_length, head_size)),
             whole((seq_length, head_size)),
-            pl.BlockSpec((seq_length, wide), lambda step: (0, step)),
-            whole((seq_length, width)),
+            whole((seq_length, heads_here * head_size)),
+            whole((tokens, width)),
+            whole(slots_shape),
+            whole(slots_shape),
+            hbm,
+            hbm,
+            hbm,
         ],
         out_shape=[
             jax.ShapeDtypeStruct((seq_length, width), BF16),
@@ -386,15 +736,32 @@
             jax.ShapeDtypeStruct((seq_length, head_size), F32),
             jax.ShapeDtypeStruct((seq_length, head_size), BF16),
             jax.ShapeDtypeStruct((seq_length, heads_here * head_size), BF16),
-            jax.ShapeDtypeStruct((seq_length, width), BF16),
+            jax.ShapeDtypeStruct((tokens, width), F32),
+            jax.ShapeDtypeStruct(slots_shape, jnp.int32),
+            jax.ShapeDtypeStruct(slots_shape, jnp.int32),
+            jax.ShapeDtypeStruct((shards,) + small.shape, F32),
+            jax.ShapeDtypeStruct((width, (steps + 1) * wide), BF16),
+            jax.ShapeDtypeStruct((planes, count, width), BF16),
         ],
         scratch_shapes=[
-            pltpu.VMEM((seq_length, width), F32),
+            pltpu.VMEM((seq_length, width), BF16),
+            pltpu.VMEM((shards,) + small.shape, F32),
+            pltpu.VMEM((width, (steps + 1) * wide), BF16),
             pltpu.VMEM((seq_length, head_size), BF16),
+            pltpu.VMEM((in_plane, planes) + routes.shape, jnp.int32),
+            pltpu.VMEM(slots_shape, jnp.int32),
+            pltpu.VMEM((2, planes, tokens, width), BF16),
+            pltpu.VMEM((2, planes, count // 2, width), BF16),
+            pltpu.VMEM((count // 2, tokens), BF16),
+            pltpu.VMEM((2, tokens, width), BF16),
+            pltpu.VMEM((tokens, width), BF16),
+            dma((3,)), dma((3,)), dma((shards,)), dma((shards,)), dma((steps + 1,)), dma((steps + 1,)),
+            dma((planes,)), dma((planes,)), dma, dma((in_plane,)), dma, dma,
+            dma((2, 2, planes + 1)), dma((2, 2, planes + 1)), dma((2, planes)), dma((planes,)), dma((3,)), dma((3,)), dma, dma,
         ],
-        compiler_params=pltpu.CompilerParams(vmem_limit_bytes=VMEM_LIMIT),
-        cost_estimate=pl.CostEstimate(flops=16 * 10**9, bytes_accessed=40 * 10**6, transcendentals=6 * 10**6),
-    )(hidden_all, gain, weights, weights, query_gain, key_gain, cosine, sine, wo)
+        compiler_params=pltpu.CompilerParams(vmem_limit_bytes=VMEM_LIMIT, collective_id=5, has_side_effects=True),
+        cost_estimate=pl.CostEstimate(flops=70 * 10**9, bytes_accessed=40 * 10**6, transcendentals=6 * 10**6),
+    )(own, small, routes, top, w_query, w_key, w_value, query_gain, key_gain, cosine, sine, wo)
 
 
 def run_backward(
@@ -506,18 +873,14 @@
     def rows_of(index, size):
         return pl.ds(pl.multiple_of(index * size, 16), size)
 
-    def across_copies(plane, column):
-        target = plane * across + column
-        return [
-            remote(
-                wq_hbm.at[rows_of(target, wq_rows)], wq_parts.at[plane, x],
-                across_send.at[0, plane], across_recv.at[0, plane], (z, column, w),
-            ),
-            remote(
-                wo_hbm.at[rows_of(target, wo_rows)], wo_parts.at[plane, x],
-                across_send.at[1, plane], across_recv.at[1, plane], (z, column, w),
-            ),
-        ]
+    sources = [(wq_hbm, wq_rows, wq_parts), (wo_hbm, wo_rows, wo_parts)]
+
+    def across_copy(kind, plane, column):
+        source, rows, goal = sources[kind]
+        return remote(
+            source.at[rows_of(plane * across + column, rows)], goal.at[plane, x],
+            across_send.at[kind, plane], across_recv.at[kind, plane], (z, column, w),
+        )
 
     def first_copy(offset):
         target = (w + offset) % shards
@@ -532,43 +895,36 @@
 
     pltpu.make_async_copy(first_hbm.at[rows_of(w, tokens)], first_in.at[0], first_recv.at[0]).start()
 
-    @pl.loop(0, planes)
-    def _(turn):
+    def start_across(kind, turn):
         plane, _, _ = line_order(z, planes, planes - 1 - turn)
 
         @pl.loop(1, across)
         def _(offset):
-            for copy in across_copies(plane, (x + offset) % across):
-                copy.start()
-
-        target = plane * across + x
+            across_copy(kind, plane, (x + offset) % across).start()
+
+        source, rows, goal = sources[kind]
         pltpu.make_async_copy(
-            wq_hbm.at[rows_of(target, wq_rows)], wq_parts.at[plane, x], across_recv.at[0, plane]
+            source.at[rows_of(plane * across + x, rows)], goal.at[plane, x], across_recv.at[kind, plane]
         ).start()
-        pltpu.make_async_copy(
-            wo_hbm.at[rows_of(target, wo_rows)], wo_parts.at[plane, x], across_recv.at[1, plane]
-        ).start()
+
+    start_across(0, 0)
+    start_across(1, 0)
 
     def wq_line_copy(plane):
         return remote(wq_out.at[plane], wq_in.at[z], line_send.at[0, plane], line_recv.at[0, z], (plane, x, w))
 
     def wo_line_copy(plane):
         return remote(wo_out.at[plane], wo_in.at[z], line_send.at[1, plane], line_recv.at[1, z], (plane, x, w))
-
-    @pl.loop(0, shards)
-    def _(offset):
-        wait_bytes(first_in.at[offset], first_recv.at[offset])
-
-    first_ref[...] = first_in[0].astype(F32)
-
-    @pl.loop(1, shards)
-    def _(offset):
-        first_ref[...] += first_in[offset].astype(F32)
 
     @pl.loop(0, planes)
     def _(turn):
         plane, _, _ = line_order(z, planes, planes - 1 - turn)
         wait_bytes(wq_parts.at[plane], across_recv.at[0, plane])
+
+        @pl.when(turn < planes - 1)
+        def _():
+            start_across(0, turn + 1)
+
         wq_total[...] = wq_parts[plane, 0].astype(F32)
 
         @pl.loop(1, across)
@@ -581,6 +937,11 @@
             wq_line_copy(plane).start()
 
         wait_bytes(wo_parts.at[plane], across_recv.at[1, plane])
+
+        @pl.when(turn < planes - 1)
+        def _():
+            start_across(1, turn + 1)
+
         wo_total[...] = wo_parts[plane, 0].astype(F32)
 
         @pl.loop(1, across)
@@ -591,6 +952,16 @@
         def _():
             wo_out[plane] = wo_total[...].astype(BF16)
             wo_line_copy(plane).start()
+
+    @pl.loop(0, shards)
+    def _(offset):
+        wait_bytes(first_in.at[offset], first_recv.at[offset])
+
+    first_ref[...] = first_in[0].astype(F32)
+
+    @pl.loop(1, shards)
+    def _(offset):
+        first_ref[...] += first_in[offset].astype(F32)
 
     @pl.loop(1, planes)
     def _(turn):
@@ -883,16 +1254,10 @@
         pltpu.make_async_copy(stage.at[step, slice_of(me)], rows_hbm.at[block, slice_of(me)], out_recv.at[step]).start()
         pltpu.make_async_copy(plane_shares.at[block, me], share_in.at[block, me], out_share_recv.at[step]).start()
 
-    def top_copy(block, index):
-        return pltpu.make_async_copy(top_hbm.at[index, block], top.at[slice_of(index)], top_sem)
-
     def expert_step(step):
         block, _, _ = order(step)
 
-        @pl.loop(0, in_plane)
-        def _(index):
-            top_copy(block, index).start()
-
+        pltpu.make_async_copy(top_hbm.at[block], top, top_sem).start()
         wait_bytes(rows_hbm.at[block], out_recv.at[step])
         load = pltpu.make_async_copy(rows_hbm.at[block], rows, load_sem)
         load.start()
@@ -1114,68 +1479,28 @@
     experts = device_count
     capacity = 5 * tokens_here * top_count // (4 * experts)
     seq_length = tokens_here * shards
-    plane, column, shard = lax.axis_index("z"), lax.axis_index("x"), lax.axis_index("w")
-
-    small = jnp.concatenate([w_router, attn_gain[:, None], ffn_gain[:, None]], axis=1)
-    depth = w_query.shape[0]
-    merged = jnp.concatenate(
-        [
-            w_query.reshape(depth, shards, -1),
-            key_projection.reshape(depth, shards, -1),
-            value_projection.reshape(depth, shards, -1),
-        ],
-        axis=2,
-    ).reshape(depth, -1)
-    hidden_all = lax.all_gather(hidden_in, "w", axis=0, tiled=True)
-    small_all = lax.all_gather(small, "w", axis=0, tiled=True)
-    weights = lax.all_to_all(merged, "w", split_axis=1, concat_axis=0, tiled=True)
-    router_full = small_all[:, :experts]
-    attn_scale = small_all[:, experts].astype(F32)[None, :]
-    ffn_scale = small_all[:, experts + 1].astype(F32)[None, :]
+
     cosine, sine = rope_tables(seq_length, head_size)
     query_gain_row, key_gain_row = query_gain[None, :], key_gain[None, :]
 
     capacity = -(-capacity // 16) * 16
-    routes_all = lax.all_gather(routes, ("z", "x", "w"), axis=0, tiled=True)
-    routes_all = routes_all.reshape(planes, in_plane, tokens_here, top_count)
-    me = column * shards + shard
-    earlier = (
-        jnp.arange(tokens_here)[:, None] < jnp.arange(tokens_here)[None, :]
-    ).astype(BF16)
-
-    def slots_of(hits):
-        ranks = jnp.einsum("zps,st->zpt", hits.astype(BF16), earlier, preferred_element_type=F32).astype(jnp.int32)
-        return jnp.where(hits, ranks, -1)
-
-    routes_z = lax.dynamic_index_in_dim(routes_all, me, 1, keepdims=True)
-    plane_experts = plane * in_plane + jnp.arange(in_plane, dtype=jnp.int32)
-    slots = slots_of(jnp.any(routes_z == plane_experts[None, :, None, None], axis=3))
-    my_slots = slots_of(jnp.any(routes_all == plane * in_plane + me, axis=3))
-    slots_flat = slots.reshape(-1, 1, tokens_here)
-    chosen = slots[:, :, None, :] == jnp.arange(capacity, dtype=jnp.int32)[None, None, :, None]
-    chosen_flat = chosen.reshape(planes, in_plane * capacity, tokens_here).astype(BF16)
-
-    def send_out(rows_z):
-        packed = jnp.einsum("zst,ztd->zsd", chosen_flat, rows_z, preferred_element_type=F32).astype(BF16)
-        packed = packed.reshape(planes, in_plane, capacity, width).transpose(1, 0, 2, 3)
-        got = lax.all_to_all(
-            packed.reshape(in_plane, planes * capacity, width), ("x", "w"), split_axis=0, concat_axis=0, tiled=True
-        )
-        return got.reshape(in_plane * planes * capacity, width)
-
-    cotangent_z = lax.all_gather(cotangent, "z", axis=0, tiled=False)
-    grads_in = send_out(cotangent_z)
-
-    first_input, query_raw, key_raw, value, attended, branch_part = run_forward(
-        hidden_all, attn_scale, weights, w_output, query_gain_row, key_gain_row, cosine, sine
+    small = jnp.concatenate([w_router.T, ffn_gain[None, :], attn_gain[None, :]], axis=0).astype(F32)
+    small = jnp.pad(small, ((0, -small.shape[0] % 8), (0, 0)))
+    first_input, query_raw, key_raw, value, attended, branch, slots_flat, my_slots, small_all, weights, top_rows = (
+        run_forward(
+        planes, across, shards, capacity, hidden_in, small, routes.T, cotangent, w_query,
+        key_projection, value_projection, query_gain_row, key_gain_row, cosine, sine, w_output,
+        )
     )
-    branch = lax.psum_scatter(branch_part, "w", scatter_dimension=0, tiled=True).astype(F32)
+    small_all = small_all.transpose(1, 0, 2).reshape(small.shape[0], width)
+    router_full = small_all[:experts].astype(BF16)
+    ffn_scale, attn_scale = small_all[experts : experts + 1], small_all[experts + 1 : experts + 2]
     source = hidden_in.astype(F32)
     first_normed, first_scale = norm_forward(source)
     middle = source + branch
     second_normed, second_scale = norm_forward(middle)
     second_input = (second_normed * ffn_scale).astype(BF16)
-    logits = lax.dot_general(router_full, second_input, (((0,), (1,)), ((), ())), preferred_element_type=F32)
+    logits = dot_nt(router_full, second_input)
     expert_ids = jnp.arange(experts, dtype=jnp.int32)
     routed = jnp.any(routes.T[None, :, :] == expert_ids[:, None, None], axis=1)
     peaks = jnp.max(jnp.where(routed, logits, -jnp.inf), axis=0, keepdims=True)
@@ -1184,8 +1509,8 @@
 
     rows_in, _, weighted, hidden_units, gate_grad, up_grad, pair_grad, row_grad_sum, share_grad = run_experts(
         planes, across, shards, capacity, second_input, shares[:, None, :], slots_flat,
-        my_slots.reshape(-1, 1, tokens_here), w_gate[0], w_up[0], w_down[0],
-        grads_in.reshape(in_plane, planes, capacity, width),
+        my_slots, w_gate[0], w_up[0], w_down[0],
+        top_rows,
     )
     share_grad = share_grad[:, 0, :]
     rows_in, pair_grad = rows_in.reshape(-1, width), pair_grad.reshape(-1, width)
@@ -1197,7 +1522,7 @@
     share_center = jnp.sum(shares * share_grad, axis=0, keepdims=True)
     logit_grad = (shares * (share_grad - share_center)).astype(BF16)
     router_grad = dot_tn(second_input, logit_grad.T)
-    second_grad = row_grad_sum + dot_nt(logit_grad.T, router_full)
+    second_grad = row_grad_sum + dot(logit_grad.T, router_full)
     ffn_gain_grad = jnp.sum(second_grad * second_normed, axis=0)
     middle_grad = grad_top + norm_backward(second_grad * ffn_scale, second_normed, second_scale)
     wo_grad, wq_grad, first_part, query_gain_grad, key_gain_grad, _, expert_sum = run_backward(

time: 1080 us -> 899 us (0.83)
  blocking collectives: 126 us -> 0 us
  Pallas kernels: 690 us -> 815 us
  waiting for transfers between devices: 124 us -> 0 us
  matrix products: 58 us -> 38.5 us
  between operations: 14.6 us -> 1.28 us
  local copies, waits for them, and re-layouts: 30 us -> 18.5 us
    pallas_call x1, Pallas kernels: 54.1 us -> 206 us  [run_forward(): pl.pallas_call(functools.partial(attention_forward, planes, across, shard...]
    all_gather x2 -> x0, blocking collectives: 126 us -> none  [the longest x1 82.9 us: local(): small_all = lax.all_gather(small, 'w', axis=0, tiled=True)]
    reduce_scatter x1 -> x0, waiting for transfers between devices: 88 us -> none  [local(): lax.psum_scatter(branch_part, 'w', scatter_dimension=0, tiled=True)]
    all_to_all x2 -> x0, waiting for transfers between devices: 34.9 us -> none  [the longest x1 34.9 us: send_out(): lax.all_to_all(packed.reshape(in_plane, planes * capacity, width), ('x',...]
    pallas_call x1, Pallas kernels: 42.4 us -> 26.5 us  [run_total(): pl.pallas_call(functools.partial(total_kernel, planes, across, shards), i...]
  transfers between devices with their start and end apart: 5 -> 0, of which waited for: 2 -> 0; matrix products, arithmetic and copies ran while one was open for 3% -> 0% of each run, Pallas kernels for 5% -> 0%
where the time goes in v3:
time: 899 us; the launch traced here: 892 us
  Pallas kernels  815 us (91%)
  matrix products  38.5 us (4%)
  other arithmetic  19.3 us (2%)
  local copies, waits for them, and re-layouts  18.5 us (2%)
    pallas_call x1, Pallas kernels, run_experts(): pl.pallas_call(functools.partial(expert_kernel, planes, across, shards, c...  270 us
    pallas_call x1, Pallas kernels, run_forward(): pl.pallas_call(functools.partial(attention_forward, planes, across, shard...  206 us
    pallas_call x1, Pallas kernels, run_backward(): pl.pallas_call(functools.partial(attention_backward, planes, across, shar...  177 us
    pallas_call x1, Pallas kernels, run_reduce(): pl.pallas_call(functools.partial(reduce_kernel, planes, across, shards),...  136 us
    dot_general x4, matrix products, dot_tn(): lax.dot_general(left, right, (((0,), (0,)), ((), ())), preferred_element_...  36.7 us
    pallas_call x1, Pallas kernels, run_total(): pl.pallas_call(functools.partial(total_kernel, planes, across, shards), i...  26.5 us

profile of v3, /device:TPU:1, one launch (start us, length us, event | category | flops | bytes accessed | tf_op | source)
XLA Modules:
  0.0 892.2 jit_solution(13850085437883835100)
XLA Ops:
  0.7 2.0 fusion.13
  2.7 1.3 pad_maximum_fusion
  4.7 205.5 %shard_map.262 = (bf16[1024,2048]{1,0:T(8,128)(2,1)}, f32[1024,1024]{1,0:T(8,128)}, f32[1024,128]{1,0:T(8,128)}, bf16[1024,128]{1,0:T(8,128)(2,1)}, bf16[1024,10...) custom-call(bf16[256,2048]{1,0:T(8,128)(2,1)} %own_ref.1, ...), custom_call_target="tpu_custom_call" | custom-call | flops 70000001024 | bytes 40000000 | tf_op jit(solution)/shard_map/pallas_call | solution.py:703
  210.2 3.2 multiply_reduce_fusion.5
  213.4 1.6 fusion.29
  215.3 1.2 fusion.14
  218.4 270.0 %shard_map.263 = (bf16[4,640,2048]{2,1,0:T(8,128)(2,1)}, bf16[4,640,2048]{2,1,0:T(8,128)(2,1)}, bf16[4,640,2048]{2,1,0:T(8,128)(2,1)}, bf16[4,640,768]{2,1,0:T(8...) custom-call(bf16[256,2048]{1,0:T(8,128)(2,1)} %copy-done.6, ...), custom_call_target="tpu_custom_call" | custom-call | flops 193273528320 | bytes 100000000 | tf_op jit(solution)/shard_map/pallas_call | solution.py:1427
  488.5 14.3 %convolution_bitcast_fusion = f32[1,768,2048]{2,1,0:T(8,128)} fusion(bf16[4,640,768]{2,1,0:T(8,128)(2,1)} %get-tuple-element.73, bf16[4,640,2048]{2,1,0:T(8,128)(2,1)} %get-tuple-element.74), kind=kOutput, calls=%fused_computation | convolution fusion | flops 8053063680 | bytes 20709376 | tf_op jit(solution)/shard_map/dot_general | solution.py:24
  502.7 11.0 %convolution_bitcast_fusion.1 = f32[1,2048,768]{2,1,0:T(8,128)} fusion(bf16[4,640,2048]{2,1,0:T(8,128)(2,1)S(1)} %copy-done.32, bf16[4,640,768]{2,1,0:T(8,128)(2,1)S(1)} %copy-done.34), kind=kOutput, calls=%fused_computation.1 | convolution fusion | flops 8053063680 | bytes 20709376 | tf_op jit(solution)/shard_map/dot_general | solution.py:24
  513.8 11.0 %convolution_bitcast_fusion.2 = f32[1,2048,768]{2,1,0:T(8,128)} fusion(bf16[4,640,2048]{2,1,0:T(8,128)(2,1)S(1)} %copy-done.32, bf16[4,640,768]{2,1,0:T(8,128)(2,1)S(1)} %copy-done.33), kind=kOutput, calls=%fused_computation.2 | convolution fusion | flops 8053063680 | bytes 20709376 | tf_op jit(solution)/shard_map/dot_general | solution.py:24
  524.9 1.4 multiply_reduce_fusion.3
  526.3 1.7 fusion.27.own_grad_ref
  527.9 176.9 %shard_map.264 = (bf16[1024,2048]{1,0:T(8,128)(2,1)}, bf16[2048,1280]{1,0:T(8,128)(2,1)}, bf16[1024,2048]{1,0:T(8,128)(2,1)}, f32[8,128]{1,0:T(8,128)}, f32[8,12...) custom-call(bf16[256,2048]{1,0:T(8,128)(2,1)} %fusion.27.own_grad_ref, bf16[1024,2048]{1,0:T(8,128)(2,1)} %wo_ref.3, ...), custom_call_target="tpu_custom_call" | custom-call | flops 70000001024 | bytes 60000000 | tf_op jit(solution)/shard_map/pallas_call | solution.py:785
  704.8 135.8 %shard_map.265 = (f32[64,4096]{1,0:T(8,128)}, f32[64,512]{1,0:T(8,128)}, f32[64,512]{1,0:T(8,128)}, f32[128,2048]{1,0:T(8,128)}, f32[256,2048]{1,0:T(8,128)}) custom-call(bf16[2048,1280]{1,0:T(8,128)(2,1)} %get-tuple-element.60.wq_hbm, bf16[1024,2048]{1,0:T(8,128)(2,1)} %get-tuple-element.61.wo_hbm, bf16[1024,2048]{1,0:T(8,128)(2,1)} %get-tuple-element.62.first_hbm), custom_call_target="tpu_custom_call" | custom-call | flops 70000001024 | bytes 40000000 | tf_op jit(solution)/shard_map/pallas_call | solution.py:1051
  840.7 3.3 fusion.9
  844.0 5.5 multiply_reduce_fusion.1
  851.0 2.7 concatenate.18
  854.9 0.8 copy.52
  855.7 26.5 %shard_map.266 = f32[24,128]{1,0:T(8,128)} custom-call(f32[32,24,128]{2,1,0:T(8,128)} %bitcast.59), custom_call_target="tpu_custom_call" | custom-call | tf_op jit(solution)/shard_map/pallas_call | solution.py:1112
  883.7 1.3 fusion.30
  885.0 1.3 slice_bitcast_fusion
  886.3 1.2 fusion.26
  887.5 2.3 copy.59
  891.0 1.0 copy.62
  (101 shorter events, 8.4 us)
Async XLA Ops:
  0.7 3.3 copy-start.30
  4.7 205.5 %copy-start.4 = (bf16[256,2048]{1,0:T(8,128)(2,1)S(1)}, bf16[256,2048]{1,0:T(8,128)(2,1)}, u32[]{:S(2)}) copy-start(bf16[256,2048]{1,0:T(8,128)(2,1)} %own_ref.1) | copy-start | bytes 3145732
  213.4 3.6 copy-start
  488.4 14.3 %copy-start.32 = (bf16[4,640,2048]{2,1,0:T(8,128)(2,1)S(1)}, bf16[4,640,2048]{2,1,0:T(8,128)(2,1)}, u32[]{:S(2)}) copy-start(bf16[4,640,2048]{2,1,0:T(8,128)(2,1)} %get-tuple-element.70) | copy-start | bytes 31457284
  488.4 14.3 %copy-start.34 = (bf16[4,640,768]{2,1,0:T(8,128)(2,1)S(1)}, bf16[4,640,768]{2,1,0:T(8,128)(2,1)}, u32[]{:S(2)}) copy-start(bf16[4,640,768]{2,1,0:T(8,128)(2,1)} %get-tuple-element.72) | copy-start | bytes 11796484
  502.7 11.0 %copy-start.33 = (bf16[4,640,768]{2,1,0:T(8,128)(2,1)S(1)}, bf16[4,640,768]{2,1,0:T(8,128)(2,1)}, u32[]{:S(2)}) copy-start(bf16[4,640,768]{2,1,0:T(8,128)(2,1)} %get-tuple-element.71) | copy-start | bytes 11796484
  513.7 11.0 %copy-start.15 = (f32[32,256]{1,0:T(8,128)S(1)}, f32[32,256]{1,0:T(8,128)}, u32[]{:S(2)}) copy-start(f32[32,256]{1,0:T(8,128)} %copy-done.14) | copy-start | bytes 98308
  513.7 11.0 %copy-start.22 = (f32[32,1,256]{2,1,0:T(1,128)S(1)}, f32[32,1,256]{2,1,0:T(1,128)}, u32[]{:S(2)}) copy-start(f32[32,1,256]{2,1,0:T(1,128)} %get-tuple-element.51) | copy-start | bytes 98308
  513.7 11.1 %copy-start.1 = (f32[256,2048]{1,0:T(8,128)S(1)}, f32[256,2048]{1,0:T(8,128)}, u32[]{:S(2)}) copy-start(f32[256,2048]{1,0:T(8,128)} %copy-done) | copy-start | bytes 6291460
  513.7 11.1 %copy-start.10 = (f32[256,2048]{1,0:T(8,128)S(1)}, f32[256,2048]{1,0:T(8,128)}, u32[]{:S(2)}) copy-start(f32[256,2048]{1,0:T(8,128)} %get-tuple-element.50) | copy-start | bytes 6291460
  513.7 11.1 %copy-start.12 = (bf16[4,4,8,512]{3,2,0,1:T(8,128)(2,1)S(1)}, bf16[4,4,8,512]{3,2,0,1:T(8,128)(2,1)}, u32[]{:S(2)}) copy-start(bf16[4,4,8,512]{3,2,0,1:T(8,128)(2,1)} %copy-done.11) | copy-start | bytes 393220
  513.7 11.1 %copy-start.17 = (f32[1,4,512]{2,0,1:T(1,128)S(1)}, f32[1,4,512]{2,0,1:T(1,128)}, u32[]{:S(2)}) copy-start(f32[1,4,512]{2,0,1:T(1,128)} %copy-done.16) | copy-start | bytes 24580
  513.8 11.1 %copy-start.27 = (f32[256]{0:T(256)S(1)}, f32[256]{0:T(256)}, u32[]{:S(2)}) copy-start(f32[256]{0:T(256)} %copy-done.26) | copy-start | bytes 3076
  704.8 135.8 %copy-start.29 = (f32[256]{0:T(256)S(1)}, f32[256]{0:T(256)}, u32[]{:S(2)}) copy-start(f32[256]{0:T(256)} %get-tuple-element.134) | copy-start | bytes 3076
  704.8 135.9 %copy-start.5 = (bf16[256,2048]{1,0:T(8,128)(2,1)S(1)}, bf16[256,2048]{1,0:T(8,128)(2,1)}, u32[]{:S(2)}) copy-start(bf16[256,2048]{1,0:T(8,128)(2,1)} %own_ref.1) | copy-start | bytes 3145732
  704.8 135.9 %copy-start.23 = (f32[1,4,512]{2,0,1:T(1,128)S(1)}, f32[1,4,512]{2,0,1:T(1,128)}, u32[]{:S(2)}) copy-start(f32[1,4,512]{2,0,1:T(1,128)} %get-tuple-element.135) | copy-start | bytes 24580
  840.6 3.4 copy-start.2
  840.6 3.4 copy-start.9
  844.0 9.6 %copy-start.7 = (bf16[256,2048]{1,0:T(8,128)(2,1)S(1)}, bf16[256,2048]{1,0:T(8,128)(2,1)}, u32[]{:S(2)}) copy-start(bf16[256,2048]{1,0:T(8,128)(2,1)} %copy-done.6) | copy-start | bytes 3145732
  844.0 9.6 %copy-start.19 = (bf16[32,256]{1,0:T(8,128)(2,1)S(1)}, bf16[32,256]{1,0:T(8,128)(2,1)}, u32[]{:S(2)}) copy-start(bf16[32,256]{1,0:T(8,128)(2,1)} %copy-done.18) | copy-start | bytes 49156
  849.6 5.1 copy-start.24
  854.9 34.9 %copy-start.21 = (f32[64,512]{1,0:T(8,128)S(1)}, f32[64,512]{1,0:T(8,128)}, u32[]{:S(2)}) copy-start(f32[64,512]{1,0:T(8,128)} %get-tuple-element.168) | copy-start | bytes 393220
  854.9 35.5 %copy-start.20 = (f32[64,512]{1,0:T(8,128)S(1)}, f32[64,512]{1,0:T(8,128)}, u32[]{:S(2)}) copy-start(f32[64,512]{1,0:T(8,128)} %get-tuple-element.169) | copy-start | bytes 393220
  854.9 36.2 %copy-start.13 = (f32[128,2048]{1,0:T(8,128)S(1)}, f32[128,2048]{1,0:T(8,128)}, u32[]{:S(2)}) copy-start(f32[128,2048]{1,0:T(8,128)} %get-tuple-element.172) | copy-start | bytes 3145732
  (11 other events, 23.8 us)

commit v4 on v3

--- a/solution.py
+++ b/solution.py
@@ -103,7 +103,7 @@
     input_ref, query_raw_ref, key_raw_ref, value_ref, attended_ref, branch_ref, slots_ref, my_slots_ref, small_hbm,
     weights_hbm, top_rows_hbm,
     hidden, small_in, weights, key_rot_ref, routes_in, far_slots, plane_rows, stage, chosen, pair_out, far_out,
-    gather_send, gather_recv, gain_send, gain_recv, weight_send, weight_recv, route_send, route_recv, plane_route_send,
+    gather_send, gather_recv, small_send, small_recv, weight_send, weight_recv, route_send, route_recv, plane_route_send,
     plane_route_recv, far_send, far_recv,
     line_send, line_recv, top_send, top_recv, pair_send, pair_recv, store_sem, small_sem,
 ):
@@ -137,8 +137,8 @@
             (z, x, target),
         )
 
-    def gain_copy(offset):
-        return remote(small_ref, small_in.at[w], gain_send.at[offset], gain_recv.at[w], (z, x, (w + offset) % shards))
+    def small_copy(offset):
+        return remote(small_ref, small_in.at[w], small_send.at[offset], small_recv.at[w], (z, x, (w + offset) % shards))
 
     def columns_at(start, size):
         return pl.ds(pl.multiple_of(start, 128), size)
@@ -189,10 +189,22 @@
         def _():
             line_copy(column, block, hop, 1).start()
 
-    def relay(column, turn):
-        block, hop, below = line_order(z, planes, turn)
-        wait_bytes(plane_rows.at[column, block], line_recv.at[column, 1 - below, hop])
-        start_line(column, block, hop + 1, below == 1, below == 0)
+    def relay(column, hop):
+        @pl.when(z - hop >= 0)
+        def _():
+            wait_bytes(plane_rows.at[column, 0], line_recv.at[column, 0, hop])
+
+            @pl.when(z + 1 < planes)
+            def _():
+                line_copy(column, z - hop, hop + 1, 0).start()
+
+        @pl.when(z + hop < planes)
+        def _():
+            wait_bytes(plane_rows.at[column, 0], line_recv.at[column, 1, hop])
+
+            @pl.when(z > 0)
+            def _():
+                line_copy(column, z + hop, hop + 1, 1).start()
 
     expert_of = z * in_plane + lax.broadcasted_iota(jnp.int32, (in_plane, tokens), 0)
     earlier = (
@@ -275,22 +287,20 @@
     @pl.when(step == 0)
     def _():
         greet_plane_and_line(planes, across, shards)
-        hidden[tokens_of(w), :] = own_ref[...]
-        gather_copy(1, w, opposite).start()
-
-        @pl.loop(1, shards)
-        def _(offset):
-            gain_copy(offset).start()
+        far_top.start()
 
         @pl.loop(1, planes)
         def _(offset):
             route_copy(offset).start()
 
+        @pl.loop(1, shards)
+        def _(offset):
+            small_copy(offset).start()
+
         plane_rows[0, z] = top_ref[...]
         start_line(0, z, 1, True, True)
+        hidden[tokens_of(w), :] = own_ref[...]
         gather_copy(0, w, sibling).start()
-        start_weights(None)
-        start_weights(0)
         small_in[w] = small_ref[...]
         routes_in[me, z] = routes_ref[...]
 
@@ -305,26 +315,35 @@
 
         fill_slots(me, slots_ref)
         pack(0, 0, slots_ref)
+        gather_copy(1, w, opposite).start()
+        relay(0, 1)
+        wait_bytes(plane_rows.at[1, z], far_recv)
+        start_line(1, z, 1, True, True)
+        start_weights(None)
+        wait_bytes(routes_in.at[opposite_me], plane_route_recv.at[opposite_me])
+        fill_slots(opposite_me, far_slots)
+        pack(1, 0, far_slots)
         wait_bytes(hidden.at[tokens_of(opposite)], gather_recv.at[1])
         gather_copy(2, opposite, sibling).start()
-        far_top.start()
-        start_weights(1)
-        relay(0, 1)
-        wait_bytes(hidden.at[tokens_of(sibling)], gather_recv.at[0])
-        wait_bytes(hidden.at[tokens_of(other)], gather_recv.at[2])
+        start_weights(0)
+        pack(0, 1, slots_ref)
 
         @pl.loop(1, shards)
         def _(offset):
             source = (w + offset) % shards
-            wait_bytes(small_in.at[source], gain_recv.at[source])
-
+            wait_bytes(small_in.at[source], small_recv.at[source])
+
+        wait_bytes(hidden.at[tokens_of(sibling)], gather_recv.at[0])
+        wait_bytes(hidden.at[tokens_of(other)], gather_recv.at[2])
         for block in range(blocks):
             rows = pl.ds(block * BLOCK, BLOCK)
             normed, _ = norm_forward(hidden[rows, :].astype(F32))
             for part in range(shards):
                 here = slice(part * depth, (part + 1) * depth)
                 input_ref[rows, here] = (normed[:, here] * small_in[part, experts + 1 : experts + 2, :]).astype(BF16)
-        pack(0, 1, slots_ref)
+        relay(0, 2)
+        start_weights(1)
+        pack(0, 2, slots_ref)
         wait_weights(last)
         for block in range(blocks):
             rows = pl.ds(block * BLOCK, BLOCK)
@@ -336,7 +355,8 @@
             key_rot_ref[rows, :] = rotate(
                 key_normed * key_gain_ref[...], cosine_ref[rows, :], sine_ref[rows, :]
             ).astype(BF16)
-        relay(0, 2)
+        relay(1, 1)
+        pack(1, 1, far_slots)
 
     for piece in range(2, last):
 
@@ -373,28 +393,15 @@
                 parts.append(dot(probs, value_ref[seen, :]).astype(BF16))
             attended_ref[rows, here] = jnp.concatenate(parts, axis=1)
 
-    @pl.when(step == 0)
-    def _():
-        pack(0, 2, slots_ref)
-        wait_bytes(routes_in.at[opposite_me], plane_route_recv.at[opposite_me])
-        fill_slots(opposite_me, far_slots)
-        wait_bytes(plane_rows.at[1, z], far_recv)
-        start_line(1, z, 1, True, True)
-        relay(0, 3)
-        pack(1, 0, far_slots)
-
     @pl.when(step == 1)
     def _():
+        relay(0, 3)
         pack(0, 3, slots_ref)
-        relay(1, 1)
 
     @pl.when(step == 2)
     def _():
-        pack(1, 1, far_slots)
-
-    @pl.when(step == 3)
-    def _():
         relay(1, 2)
+        pack(1, 2, far_slots)
 
     def project(owner, goal, added):
         rows = tokens_of(owner)
@@ -429,8 +436,6 @@
         far_copy.start()
         wait_bytes(hidden.at[pl.ds(tokens, tokens)], pair_recv.at[1])
         project(w, branch_ref, pl.ds(tokens, tokens))
-        pack(1, 2, far_slots)
-
         @pl.loop(1, in_plane)
         def _(offset):
             index = (me + offset) % in_plane
@@ -457,7 +462,7 @@
 
         @pl.loop(1, shards)
         def _(offset):
-            wait_bytes(small_in.at[w], gain_send.at[offset])
+            wait_bytes(small_in.at[w], small_send.at[offset])
 
         @pl.loop(1, planes)
         def _(offset):
@@ -527,6 +532,8 @@
             back_send.at[block], back_recv.at[block], (z, index // shards, index % shards),
         )
 
+    pace = [(1, 1), (2, 2), (3, 3)]
+
     def start_back(turn, near, far):
         block, _, _ = line_order(z, planes, planes - 1 - turn)
 
@@ -547,6 +554,35 @@
 
     def sum_copy(block):
         return remote(partial_out.at[block], partial_in.at[z], sum_send.at[block], sum_recv.at[z], (block, x, w))
+
+    def combine(turn):
+        place = planes - 1 - turn
+        block, _, _ = line_order(z, planes, place)
+        wait_bytes(returned_hbm.at[block], back_recv.at[block])
+        load = pltpu.make_async_copy(returned_hbm.at[block], rows, load_sem)
+        load.start()
+        if place > 0:
+            start_back(turn + 1, step >= 0, step >= 0)
+        slot_ids = lax.broadcasted_iota(jnp.int32, (capacity, tokens), 0)
+
+        @pl.loop(0, in_plane)
+        def _(index):
+            slots = slots_ref[block * in_plane + index]
+            chosen[slice_of(index), :] = (slot_ids == slots).astype(F32).astype(BF16)
+
+        load.wait()
+
+        @pl.loop(0, width // chunk)
+        def _(part):
+            wide = pl.ds(pl.multiple_of(part * chunk, chunk), chunk)
+            summed = dot_tn(chosen[...], rows[:, wide])
+            if place > 0:
+                partial_out[block, :, wide] = summed.astype(BF16)
+            else:
+                expert_sum_ref[:, wide] = summed
+
+        if place > 0:
+            sum_copy(block).start()
 
     @pl.when(step == 0)
     def _():
@@ -568,10 +604,6 @@
         start_back(0, step != 0, step == 0)
         wait_bytes(grad_ref.at[tokens_of(sibling)], gather_recv.at[0])
         wait_bytes(grad_ref.at[tokens_of(other)], gather_recv.at[2])
-
-    @pl.when((step > 0) & (step < planes))
-    def _():
-        start_back(step, step > 0, step > 0)
 
     @pl.when(step < last)
     def _():
@@ -611,6 +643,13 @@
             def _():
                 total_ref[rows_here, :] += partial
 
+            for turn, place in enumerate(pace):
+                if place[1] == block:
+
+                    @pl.when(step == place[0])
+                    def _():
+                        combine(turn)
+
     @pl.when(step == last)
     def _():
         key_normed, key_scale = norm_forward(key_raw_ref[...])
@@ -628,38 +667,11 @@
 
     wq_grad_ref[...] = dot(turned_ref[...], query_grad_ref[...]).astype(BF16)
 
-    @pl.when(step >= last - planes + 1)
-    def _():
-        place = last - step
-        block, _, _ = line_order(z, planes, place)
-        wait_bytes(returned_hbm.at[block], back_recv.at[block])
-        load = pltpu.make_async_copy(returned_hbm.at[block], rows, load_sem)
-        load.start()
-        slot_ids = lax.broadcasted_iota(jnp.int32, (capacity, tokens), 0)
-
-        @pl.loop(0, in_plane)
-        def _(index):
-            slots = slots_ref[block * in_plane + index]
-            chosen[slice_of(index), :] = (slot_ids == slots).astype(F32).astype(BF16)
-
-        load.wait()
-
-        @pl.loop(0, width // chunk)
-        def _(part):
-            wide = pl.ds(pl.multiple_of(part * chunk, chunk), chunk)
-            summed = dot_tn(chosen[...], rows[:, wide])
-            partial_out[block, :, wide] = summed.astype(BF16)
-
-            @pl.when(place == 0)
-            def _():
-                expert_sum_ref[:, wide] = summed
-
-        @pl.when(place > 0)
-        def _():
-            sum_copy(block).start()
-
     @pl.when(step == last)
     def _():
+        for turn in range(len(pace), planes):
+            combine(turn)
+
         @pl.loop(1, planes)
         def _(offset):
             source = (z + offset) % planes
@@ -910,48 +922,46 @@
     start_across(0, 0)
     start_across(1, 0)
 
-    def wq_line_copy(plane):
-        return remote(wq_out.at[plane], wq_in.at[z], line_send.at[0, plane], line_recv.at[0, z], (plane, x, w))
-
-    def wo_line_copy(plane):
-        return remote(wo_out.at[plane], wo_in.at[z], line_send.at[1, plane], line_recv.at[1, z], (plane, x, w))
+    outs, ins = [wq_out, wo_out], [wq_in, wo_in]
+    totals, parts = [wq_total, wo_total], [wq_parts, wo_parts]
+
+    def line_copy(kind, plane):
+        up = (plane > z).astype(jnp.int32)
+        ends = (plane == z + 2 * up - 1).astype(jnp.int32)
+        slot = plane + ends * (1 - up) * (planes - plane)
+        return remote(
+            outs[kind].at[plane], ins[kind].at[slot], line_send.at[kind, plane], line_recv.at[kind, slot],
+            (z + 2 * up - 1, x, w),
+        )
+
+    def take(kind, slot):
+        wait_bytes(ins[kind].at[slot], line_recv.at[kind, slot])
+        totals[kind][...] += ins[kind][slot].astype(F32)
 
     @pl.loop(0, planes)
     def _(turn):
         plane, _, _ = line_order(z, planes, planes - 1 - turn)
-        wait_bytes(wq_parts.at[plane], across_recv.at[0, plane])
-
-        @pl.when(turn < planes - 1)
-        def _():
-            start_across(0, turn + 1)
-
-        wq_total[...] = wq_parts[plane, 0].astype(F32)
-
-        @pl.loop(1, across)
-        def _(column):
-            wq_total[...] += wq_parts[plane, column].astype(F32)
-
-        @pl.when(turn < planes - 1)
-        def _():
-            wq_out[plane] = wq_total[...].astype(BF16)
-            wq_line_copy(plane).start()
-
-        wait_bytes(wo_parts.at[plane], across_recv.at[1, plane])
-
-        @pl.when(turn < planes - 1)
-        def _():
-            start_across(1, turn + 1)
-
-        wo_total[...] = wo_parts[plane, 0].astype(F32)
-
-        @pl.loop(1, across)
-        def _(column):
-            wo_total[...] += wo_parts[plane, column].astype(F32)
-
-        @pl.when(turn < planes - 1)
-        def _():
-            wo_out[plane] = wo_total[...].astype(BF16)
-            wo_line_copy(plane).start()
+        for kind in range(2):
+            wait_bytes(parts[kind].at[plane], across_recv.at[kind, plane])
+
+            @pl.when(turn < planes - 1)
+            def _():
+                start_across(kind, turn + 1)
+
+            totals[kind][...] = parts[kind][plane, 0].astype(F32)
+
+            @pl.loop(1, across)
+            def _(column):
+                totals[kind][...] += parts[kind][plane, column].astype(F32)
+
+            @pl.when(((plane > z) & (z > 0)) | ((plane < z) & (z < planes - 1)))
+            def _():
+                take(kind, plane)
+
+            @pl.when(plane != z)
+            def _():
+                outs[kind][plane] = totals[kind][...].astype(BF16)
+                line_copy(kind, plane).start()
 
     @pl.loop(0, shards)
     def _(offset):
@@ -963,12 +973,16 @@
     def _(offset):
         first_ref[...] += first_in[offset].astype(F32)
 
-    @pl.loop(1, planes)
-    def _(turn):
-        plane, _, _ = line_order(z, planes, turn)
-        wait_bytes(wq_in.at[plane], line_recv.at[0, plane])
-        wq_total[...] += wq_in[plane].astype(F32)
-
+    def finish(kind):
+        @pl.when(z > 0)
+        def _():
+            take(kind, z)
+
+        @pl.when(z < planes - 1)
+        def _():
+            take(kind, planes)
+
+    finish(0)
     wq_final[...] = wq_total[...].astype(BF16)
 
     def home_copy(offset):
@@ -983,12 +997,7 @@
 
     pltpu.make_async_copy(wq_final.at[rows_of(w, mine)], wq_home.at[w], home_recv.at[w]).start()
 
-    @pl.loop(1, planes)
-    def _(turn):
-        plane, _, _ = line_order(z, planes, turn)
-        wait_bytes(wo_in.at[plane], line_recv.at[1, plane])
-        wo_total[...] += wo_in[plane].astype(F32)
-
+    finish(1)
     wo_final[...] = wo_total[...].astype(BF16)
     goal = w * rings + ring
     stays = goal == linear
@@ -1064,8 +1073,8 @@
             pltpu.VMEM((planes, across, wo_rows, width), BF16),
             pltpu.VMEM((planes, wq_rows, wq_wide), BF16),
             pltpu.VMEM((planes, wo_rows, width), BF16),
-            pltpu.VMEM((planes, wq_rows, wq_wide), BF16),
-            pltpu.VMEM((planes, wo_rows, width), BF16),
+            pltpu.VMEM((planes + 1, wq_rows, wq_wide), BF16),
+            pltpu.VMEM((planes + 1, wo_rows, width), BF16),
             pltpu.VMEM((wq_rows, wq_wide), F32),
             pltpu.VMEM((wo_rows, width), F32),
             pltpu.VMEM((wq_rows, wq_wide), BF16),
@@ -1073,7 +1082,7 @@
             pltpu.VMEM((shards, mine, wq_wide), BF16),
             pltpu.VMEM((wo_rows, width), BF16),
             pltpu.VMEM((shards, tokens, width), BF16),
-            dma((2, planes)), dma((2, planes)), dma((2, planes)), dma((2, planes)), dma((shards,)), dma((shards,)),
+            dma((2, planes)), dma((2, planes)), dma((2, planes)), dma((2, planes + 1)), dma((shards,)), dma((shards,)),
             dma, dma, dma((shards,)), dma((shards,)),
         ],
         compiler_params=pltpu.CompilerParams(vmem_limit_bytes=VMEM_LIMIT, collective_id=3, has_side_effects=True),
@@ -1219,21 +1228,28 @@
 
     slot_ids = lax.broadcasted_iota(jnp.int32, (capacity, tokens), 0)
 
-    def send_step(step):
-        block, hop, below = order(step)
+    def pack_step(step):
+        block, _, _ = order(step)
 
         @pl.when(step > 0)
         def _():
-            wait_bytes(plane_rows.at[block], line_recv.at[1 - below, hop])
+            @pl.when(z - step >= 0)
+            def _():
+                wait_bytes(plane_rows.at[0], line_recv.at[0, step])
+
+                @pl.when(z + 1 < planes)
+                def _():
+                    line_up(z - step, step + 1).start()
+
+            @pl.when(z + step < planes)
+            def _():
+                wait_bytes(plane_rows.at[0], line_recv.at[1, step])
+
+                @pl.when(z > 0)
+                def _():
+                    line_down(z + step, step + 1).start()
+
             wait_bytes(plane_shares.at[block], plane_share_recv.at[block])
-
-            @pl.when((below == 1) & (z + 1 < planes))
-            def _():
-                line_up(block, hop + 1).start()
-
-            @pl.when((below == 0) & (z > 0))
-            def _():
-                line_down(block, hop + 1).start()
 
         @pl.loop(0, in_plane)
         def _(index):
@@ -1244,6 +1260,9 @@
         def _(part):
             wide = pl.ds(pl.multiple_of(part * chunk, chunk), chunk)
             stage[step, :, wide] = dot(chosen[step], plane_rows[block, :, wide]).astype(BF16)
+
+    def send_step(step):
+        block, _, _ = order(step)
 
         @pl.loop(1, in_plane)
         def _(offset):
@@ -1261,6 +1280,11 @@
         wait_bytes(rows_hbm.at[block], out_recv.at[step])
         load = pltpu.make_async_copy(rows_hbm.at[block], rows, load_sem)
         load.start()
+
+        @pl.when(step + 1 < planes)
+        def _():
+            send_step(step + 1)
+
         wait_bytes(share_in.at[block], out_share_recv.at[step])
         wait_bytes(stage.at[step, pl.ds(0, count - capacity)], out_send.at[step])
         wait_bytes(plane_shares.at[block, pl.ds(0, in_plane - 1)], out_share_send.at[step])
@@ -1309,7 +1333,7 @@
             values = columns[slice_of(index), 0:1]
             share_back[block, index] = jnp.sum(jnp.where(mine, values, 0.0), axis=0, keepdims=True)
 
-        @pl.when(step > 0)
+        @pl.when(step > 1)
         def _():
             start_back(step, block)
 
@@ -1330,13 +1354,15 @@
     def _(step):
         @pl.when(step < planes)
         def _():
+            pack_step(step)
+
+        @pl.when(step == 0)
+        def _():
             send_step(step)
 
         @pl.when(step > 0)
         def _():
             expert_step(step - 1)
-
-    start_back(0, z)
 
     for hop in range(1, planes):
 
@@ -1352,6 +1378,10 @@
     def _(offset):
         wait_bytes(plane_shares.at[0], plane_share_send.at[(z + offset) % planes])
 
+    def wait_back(step):
+        wait_bytes(stage.at[step, pl.ds(0, count - capacity)], back_send.at[step])
+        wait_bytes(share_back.at[0, pl.ds(0, in_plane - 1)], back_share_send.at[step])
+
     def sum_copy(block):
         return remote(plane_rows.at[block], partial_in.at[z], sum_send.at[block], sum_recv.at[z], (block, x, w))
 
@@ -1363,7 +1393,7 @@
 
     @pl.loop(0, planes)
     def _(turn):
-        step = (turn + 1) % planes
+        step = jnp.where(turn < planes - 2, turn + 2, planes - 1 - turn)
         block, _, _ = order(step)
         wait_bytes(back_hbm.at[block], back_recv.at[step])
         load = pltpu.make_async_copy(back_hbm.at[block], rows, load_sem)
@@ -1391,6 +1421,16 @@
                 wide = pl.ds(pl.multiple_of(part * chunk, chunk), chunk)
                 row_grad_ref[:, wide] = dot_tn(chosen[0], rows[:, wide])
 
+        @pl.when(turn == planes - 4)
+        def _():
+            wait_back(planes - 1)
+            start_back(1, order(1)[0])
+
+        @pl.when(turn == planes - 3)
+        def _():
+            wait_back(1)
+            start_back(0, z)
+
     @pl.loop(1, planes)
     def _(offset):
         other = (z + offset) % planes
@@ -1408,10 +1448,9 @@
         wait_bytes(plane_rows.at[other], sum_send.at[other])
         wait_bytes(share_home.at[other], sum_share_send.at[other])
 
-    @pl.loop(0, planes)
-    def _(step):
-        wait_bytes(stage.at[step, pl.ds(0, count - capacity)], back_send.at[step])
-        wait_bytes(share_back.at[step, pl.ds(0, in_plane - 1)], back_share_send.at[step])
+    wait_back(0)
+    for step in range(2, planes - 1):
+        wait_back(step)
 
 
 def run_experts(planes, across, shards, capacity, own, shares, slots, my_slots, w_gate, w_up, w_down, top_rows):

time: 899 us -> 820 us (0.912)
  Pallas kernels: 815 us -> 736 us
    pallas_call x1, Pallas kernels: 206 us -> 171 us  [run_forward(): pl.pallas_call(functools.partial(attention_forward, planes, across, shard...]
    pallas_call x1, Pallas kernels: 270 us -> 249 us  [run_experts(): pl.pallas_call(functools.partial(expert_kernel, planes, across, shards, c...]
    pallas_call x1, Pallas kernels: 177 us -> 168 us  [run_backward(): pl.pallas_call(functools.partial(attention_backward, planes, across, shar...]
    pallas_call x1, Pallas kernels: 26.5 us -> 17.5 us  [run_total(): pl.pallas_call(functools.partial(total_kernel, planes, across, shards), i...]
where the time goes in v4:
time: 820 us; the launch traced here: 813 us
  Pallas kernels  736 us (90%)
  matrix products  38.5 us (5%)
  other arithmetic  19.3 us (2%)
  local copies, waits for them, and re-layouts  18.5 us (2%)
    pallas_call x1, Pallas kernels, run_experts(): pl.pallas_call(functools.partial(expert_kernel, planes, across, shards, c...  249 us
    pallas_call x1, Pallas kernels, run_forward(): pl.pallas_call(functools.partial(attention_forward, planes, across, shard...  171 us
    pallas_call x1, Pallas kernels, run_backward(): pl.pallas_call(functools.partial(attention_backward, planes, across, shar...  168 us
    pallas_call x1, Pallas kernels, run_reduce(): pl.pallas_call(functools.partial(reduce_kernel, planes, across, shards),...  130 us
    dot_general x4, matrix products, dot_tn(): lax.dot_general(left, right, (((0,), (0,)), ((), ())), preferred_element_...  36.7 us
    pallas_call x1, Pallas kernels, run_total(): pl.pallas_call(functools.partial(total_kernel, planes, across, shards), i...  17.5 us

profile of v4, /device:TPU:1, one launch (start us, length us, event | category | flops | bytes accessed | tf_op | source)
XLA Modules:
  0.0 813.1 jit_solution(1937259494809683740)
XLA Ops:
  0.7 2.0 fusion.13
  2.7 1.3 pad_maximum_fusion
  4.7 171.1 %shard_map.262 = (bf16[1024,2048]{1,0:T(8,128)(2,1)}, f32[1024,1024]{1,0:T(8,128)}, f32[1024,128]{1,0:T(8,128)}, bf16[1024,128]{1,0:T(8,128)(2,1)}, bf16[1024,10...) custom-call(bf16[256,2048]{1,0:T(8,128)(2,1)} %own_ref.1, ...), custom_call_target="tpu_custom_call" | custom-call | flops 70000001024 | bytes 40000000 | tf_op jit(solution)/shard_map/pallas_call | solution.py:715
  175.7 3.2 multiply_reduce_fusion.5
  178.9 1.6 fusion.29
  180.8 1.2 fusion.14
  184.0 249.3 %shard_map.263 = (bf16[4,640,2048]{2,1,0:T(8,128)(2,1)}, bf16[4,640,2048]{2,1,0:T(8,128)(2,1)}, bf16[4,640,2048]{2,1,0:T(8,128)(2,1)}, bf16[4,640,768]{2,1,0:T(8...) custom-call(bf16[256,2048]{1,0:T(8,128)(2,1)} %copy-done.6, ...), custom_call_target="tpu_custom_call" | custom-call | flops 193273528320 | bytes 100000000 | tf_op jit(solution)/shard_map/pallas_call | solution.py:1466
  433.3 14.3 %convolution_bitcast_fusion = f32[1,768,2048]{2,1,0:T(8,128)} fusion(bf16[4,640,768]{2,1,0:T(8,128)(2,1)} %get-tuple-element.73, bf16[4,640,2048]{2,1,0:T(8,128)(2,1)} %get-tuple-element.74), kind=kOutput, calls=%fused_computation | convolution fusion | flops 8053063680 | bytes 20709376 | tf_op jit(solution)/shard_map/dot_general | solution.py:24
  447.6 11.0 %convolution_bitcast_fusion.1 = f32[1,2048,768]{2,1,0:T(8,128)} fusion(bf16[4,640,2048]{2,1,0:T(8,128)(2,1)S(1)} %copy-done.32, bf16[4,640,768]{2,1,0:T(8,128)(2,1)S(1)} %copy-done.34), kind=kOutput, calls=%fused_computation.1 | convolution fusion | flops 8053063680 | bytes 20709376 | tf_op jit(solution)/shard_map/dot_general | solution.py:24
  458.6 11.0 %convolution_bitcast_fusion.2 = f32[1,2048,768]{2,1,0:T(8,128)} fusion(bf16[4,640,2048]{2,1,0:T(8,128)(2,1)S(1)} %copy-done.32, bf16[4,640,768]{2,1,0:T(8,128)(2,1)S(1)} %copy-done.33), kind=kOutput, calls=%fused_computation.2 | convolution fusion | flops 8053063680 | bytes 20709376 | tf_op jit(solution)/shard_map/dot_general | solution.py:24
  469.7 1.4 multiply_reduce_fusion.3
  471.1 1.7 fusion.27.own_grad_ref
  472.8 167.7 %shard_map.264 = (bf16[1024,2048]{1,0:T(8,128)(2,1)}, bf16[2048,1280]{1,0:T(8,128)(2,1)}, bf16[1024,2048]{1,0:T(8,128)(2,1)}, f32[8,128]{1,0:T(8,128)}, f32[8,12...) custom-call(bf16[256,2048]{1,0:T(8,128)(2,1)} %fusion.27.own_grad_ref, bf16[1024,2048]{1,0:T(8,128)(2,1)} %wo_ref.3, ...), custom_call_target="tpu_custom_call" | custom-call | flops 70000001024 | bytes 60000000 | tf_op jit(solution)/shard_map/pallas_call | solution.py:797
  640.6 130.0 %shard_map.265 = (f32[64,4096]{1,0:T(8,128)}, f32[64,512]{1,0:T(8,128)}, f32[64,512]{1,0:T(8,128)}, f32[128,2048]{1,0:T(8,128)}, f32[256,2048]{1,0:T(8,128)}) custom-call(bf16[2048,1280]{1,0:T(8,128)(2,1)} %get-tuple-element.60.wq_hbm, bf16[1024,2048]{1,0:T(8,128)(2,1)} %get-tuple-element.61.wo_hbm, bf16[1024,2048]{1,0:T(8,128)(2,1)} %get-tuple-element.62.first_hbm), custom_call_target="tpu_custom_call" | custom-call | flops 70000001024 | bytes 40000000 | tf_op jit(solution)/shard_map/pallas_call | solution.py:1060
  770.7 3.3 fusion.9
  774.0 5.5 multiply_reduce_fusion.1
  780.9 2.7 concatenate.18
  784.9 0.8 copy.52
  785.7 17.5 %shard_map.266 = f32[24,128]{1,0:T(8,128)} custom-call(f32[32,24,128]{2,1,0:T(8,128)} %bitcast.59), custom_call_target="tpu_custom_call" | custom-call | tf_op jit(solution)/shard_map/pallas_call | solution.py:1121
  804.6 1.3 fusion.30
  805.9 1.3 slice_bitcast_fusion
  807.2 1.2 fusion.26
  808.4 2.3 copy.59
  812.0 1.0 copy.62
  (101 shorter events, 8.4 us)
Async XLA Ops:
  0.7 3.3 copy-start.30
  4.7 171.1 %copy-start.4 = (bf16[256,2048]{1,0:T(8,128)(2,1)S(1)}, bf16[256,2048]{1,0:T(8,128)(2,1)}, u32[]{:S(2)}) copy-start(bf16[256,2048]{1,0:T(8,128)(2,1)} %own_ref.1) | copy-start | bytes 3145732
  178.9 3.6 copy-start
  433.3 14.3 %copy-start.32 = (bf16[4,640,2048]{2,1,0:T(8,128)(2,1)S(1)}, bf16[4,640,2048]{2,1,0:T(8,128)(2,1)}, u32[]{:S(2)}) copy-start(bf16[4,640,2048]{2,1,0:T(8,128)(2,1)} %get-tuple-element.70) | copy-start | bytes 31457284
  433.3 14.3 %copy-start.34 = (bf16[4,640,768]{2,1,0:T(8,128)(2,1)S(1)}, bf16[4,640,768]{2,1,0:T(8,128)(2,1)}, u32[]{:S(2)}) copy-start(bf16[4,640,768]{2,1,0:T(8,128)(2,1)} %get-tuple-element.72) | copy-start | bytes 11796484
  447.6 11.0 %copy-start.33 = (bf16[4,640,768]{2,1,0:T(8,128)(2,1)S(1)}, bf16[4,640,768]{2,1,0:T(8,128)(2,1)}, u32[]{:S(2)}) copy-start(bf16[4,640,768]{2,1,0:T(8,128)(2,1)} %get-tuple-element.71) | copy-start | bytes 11796484
  458.6 11.0 %copy-start.15 = (f32[32,256]{1,0:T(8,128)S(1)}, f32[32,256]{1,0:T(8,128)}, u32[]{:S(2)}) copy-start(f32[32,256]{1,0:T(8,128)} %copy-done.14) | copy-start | bytes 98308
  458.6 11.0 %copy-start.22 = (f32[32,1,256]{2,1,0:T(1,128)S(1)}, f32[32,1,256]{2,1,0:T(1,128)}, u32[]{:S(2)}) copy-start(f32[32,1,256]{2,1,0:T(1,128)} %get-tuple-element.51) | copy-start | bytes 98308
  458.6 11.1 %copy-start.1 = (f32[256,2048]{1,0:T(8,128)S(1)}, f32[256,2048]{1,0:T(8,128)}, u32[]{:S(2)}) copy-start(f32[256,2048]{1,0:T(8,128)} %copy-done) | copy-start | bytes 6291460
  458.6 11.1 %copy-start.10 = (f32[256,2048]{1,0:T(8,128)S(1)}, f32[256,2048]{1,0:T(8,128)}, u32[]{:S(2)}) copy-start(f32[256,2048]{1,0:T(8,128)} %get-tuple-element.50) | copy-start | bytes 6291460
  458.6 11.1 %copy-start.12 = (bf16[4,4,8,512]{3,2,0,1:T(8,128)(2,1)S(1)}, bf16[4,4,8,512]{3,2,0,1:T(8,128)(2,1)}, u32[]{:S(2)}) copy-start(bf16[4,4,8,512]{3,2,0,1:T(8,128)(2,1)} %copy-done.11) | copy-start | bytes 393220
  458.6 11.1 %copy-start.17 = (f32[1,4,512]{2,0,1:T(1,128)S(1)}, f32[1,4,512]{2,0,1:T(1,128)}, u32[]{:S(2)}) copy-start(f32[1,4,512]{2,0,1:T(1,128)} %copy-done.16) | copy-start | bytes 24580
  458.6 11.1 %copy-start.27 = (f32[256]{0:T(256)S(1)}, f32[256]{0:T(256)}, u32[]{:S(2)}) copy-start(f32[256]{0:T(256)} %copy-done.26) | copy-start | bytes 3076
  640.6 130.1 %copy-start.29 = (f32[256]{0:T(256)S(1)}, f32[256]{0:T(256)}, u32[]{:S(2)}) copy-start(f32[256]{0:T(256)} %get-tuple-element.134) | copy-start | bytes 3076
  640.6 130.1 %copy-start.5 = (bf16[256,2048]{1,0:T(8,128)(2,1)S(1)}, bf16[256,2048]{1,0:T(8,128)(2,1)}, u32[]{:S(2)}) copy-start(bf16[256,2048]{1,0:T(8,128)(2,1)} %own_ref.1) | copy-start | bytes 3145732
  640.6 130.1 %copy-start.23 = (f32[1,4,512]{2,0,1:T(1,128)S(1)}, f32[1,4,512]{2,0,1:T(1,128)}, u32[]{:S(2)}) copy-start(f32[1,4,512]{2,0,1:T(1,128)} %get-tuple-element.135) | copy-start | bytes 24580
  770.6 3.4 copy-start.2
  770.6 3.4 copy-start.9
  774.0 9.6 %copy-start.7 = (bf16[256,2048]{1,0:T(8,128)(2,1)S(1)}, bf16[256,2048]{1,0:T(8,128)(2,1)}, u32[]{:S(2)}) copy-start(bf16[256,2048]{1,0:T(8,128)(2,1)} %copy-done.6) | copy-start | bytes 3145732
  774.0 9.6 %copy-start.19 = (bf16[32,256]{1,0:T(8,128)(2,1)S(1)}, bf16[32,256]{1,0:T(8,128)(2,1)}, u32[]{:S(2)}) copy-start(bf16[32,256]{1,0:T(8,128)(2,1)} %copy-done.18) | copy-start | bytes 49156
  779.6 5.1 copy-start.24
  784.8 25.9 %copy-start.21 = (f32[64,512]{1,0:T(8,128)S(1)}, f32[64,512]{1,0:T(8,128)}, u32[]{:S(2)}) copy-start(f32[64,512]{1,0:T(8,128)} %get-tuple-element.168) | copy-start | bytes 393220
  784.8 26.5 %copy-start.20 = (f32[64,512]{1,0:T(8,128)S(1)}, f32[64,512]{1,0:T(8,128)}, u32[]{:S(2)}) copy-start(f32[64,512]{1,0:T(8,128)} %get-tuple-element.169) | copy-start | bytes 393220
  784.9 27.1 %copy-start.13 = (f32[128,2048]{1,0:T(8,128)S(1)}, f32[128,2048]{1,0:T(8,128)}, u32[]{:S(2)}) copy-start(f32[128,2048]{1,0:T(8,128)} %get-tuple-element.172) | copy-start | bytes 3145732
  (11 other events, 23.8 us)

commit v5 on v4

--- a/solution.py
+++ b/solution.py
@@ -855,10 +855,14 @@
 
 def reduce_kernel(
     planes, across, shards,
-    wq_hbm, wo_hbm, first_hbm,
-    query_ref, key_ref, value_ref, output_ref, first_ref,
+    wq_hbm, wo_hbm, first_hbm, hidden_ref, middle_hbm, expert_sum_hbm, middle_grad_hbm, scale_ref, early_ref, shared_ref,
+    rows_hbm, gate_grad_hbm, up_grad_hbm, units_hbm, pair_grad_hbm,
+    query_ref, key_ref, value_ref, output_ref, hidden_out_ref, grad_in_ref, early_total_ref, late_total_ref,
+    gate_out_hbm, up_out_hbm, down_out_hbm,
     wq_parts, wo_parts, wq_out, wo_out, wq_in, wo_in, wq_total, wo_total, wq_final, wo_final, wq_home, wo_home, first_in,
+    early_in, late, late_in, held_a, held_b, side, turned, tiles, tall, flat,
     across_send, across_recv, line_send, line_recv, home_send, home_recv, swap_send, swap_recv, first_send, first_recv,
+    early_send, early_recv, late_send, late_recv, held_sem, side_sem, tile_sem, result_sem,
 ):
     z, x, w = lax.axis_index("z"), lax.axis_index("x"), lax.axis_index("w")
     rings = planes * across
@@ -866,19 +870,18 @@
     everyone = rings * shards
     wq_rows, wo_rows = wq_total.shape[0], wo_total.shape[0]
     mine = wq_rows // shards
-    tokens = first_ref.shape[0]
+    tokens, width = grad_in_ref.shape
     query_columns = query_ref.shape[1] // shards
     key_columns = key_ref.shape[1] // shards
     linear = ring * shards + w
     barrier = pltpu.get_barrier_semaphore()
 
+    def place(index):
+        return (index // shards // across, index // shards % across, index % shards)
+
     @pl.loop(1, everyone)
     def _(offset):
-        other = (linear + offset) % everyone
-        pl.semaphore_signal(
-            barrier, inc=1, device_id=(other // shards // across, other // shards % across, other % shards),
-            device_id_type=MESH,
-        )
+        pl.semaphore_signal(barrier, inc=1, device_id=place((linear + offset) % everyone), device_id_type=MESH)
 
     pl.semaphore_wait(barrier, everyone - 1)
 
@@ -906,6 +909,10 @@
         first_copy(offset).start()
 
     pltpu.make_async_copy(first_hbm.at[rows_of(w, tokens)], first_in.at[0], first_recv.at[0]).start()
+    hold_a = pltpu.make_async_copy(middle_hbm, held_a, held_sem.at[0])
+    hold_b = pltpu.make_async_copy(expert_sum_hbm, held_b, held_sem.at[1])
+    hold_a.start()
+    hold_b.start()
 
     def start_across(kind, turn):
         plane, _, _ = line_order(z, planes, planes - 1 - turn)
@@ -919,8 +926,132 @@
             source.at[rows_of(plane * across + x, rows)], goal.at[plane, x], across_recv.at[kind, plane]
         ).start()
 
-    start_across(0, 0)
     start_across(1, 0)
+    start_across(1, 1)
+
+    @pl.loop(1, everyone)
+    def _(offset):
+        other = (linear + offset) % everyone
+        remote(early_ref.at[other], early_in.at[linear], early_send, early_recv, place(other)).start()
+
+    early_in[linear] = early_ref[linear]
+    lanes = tiles.shape[2]
+    per_kind = width // lanes
+    depth = side.shape[0]
+    late_rows = width // 128
+    pick = (lax.broadcasted_iota(jnp.int32, (8, 128), 0) == 2).astype(F32)
+    lane = lax.broadcasted_iota(jnp.int32, (8, 128), 1)
+
+    def tile_copy(unit):
+        slot = unit % 2
+        here = pl.ds(pl.multiple_of((unit % per_kind) * lanes, lanes), lanes)
+
+        @pl.when(unit < 2 * per_kind)
+        def _():
+            pltpu.make_async_copy(rows_hbm.at[:, here], tiles.at[slot], tile_sem.at[slot]).start()
+
+        @pl.when(unit >= 2 * per_kind)
+        def _():
+            pltpu.make_async_copy(pair_grad_hbm.at[:, here], tiles.at[slot], tile_sem.at[slot]).start()
+
+    tile_copy(0)
+
+    def multiply(unit):
+        slot = unit % 2
+        here = pl.ds(pl.multiple_of((unit % per_kind) * lanes, lanes), lanes)
+        for kind, source in enumerate([gate_grad_hbm, up_grad_hbm, units_hbm]):
+
+            @pl.when(unit == kind * per_kind)
+            def _():
+                load = pltpu.make_async_copy(source, side, side_sem)
+                load.start()
+                load.wait()
+                if kind == 2:
+
+                    @pl.loop(0, depth // 128)
+                    def _(part):
+                        at = pl.ds(pl.multiple_of(part * 128, 128), 128)
+                        turned[:, at] = side[at, :].T
+
+        @pl.when(unit + 1 < 3 * per_kind)
+        def _():
+            tile_copy(unit + 1)
+
+        wait_bytes(tiles.at[slot], tile_sem.at[slot])
+
+        @pl.when(unit >= 2)
+        def _():
+            wait_bytes(tall.at[slot], result_sem.at[slot])
+
+        @pl.when(unit < 2 * per_kind)
+        def _():
+            tall[slot] = dot_tn(tiles[slot], side[...])
+
+        @pl.when(unit < per_kind)
+        def _():
+            pltpu.make_async_copy(tall.at[slot], gate_out_hbm.at[here], result_sem.at[slot]).start()
+
+        @pl.when((unit >= per_kind) & (unit < 2 * per_kind))
+        def _():
+            pltpu.make_async_copy(tall.at[slot], up_out_hbm.at[here], result_sem.at[slot]).start()
+
+        @pl.when(unit >= 2 * per_kind)
+        def _():
+            flat[slot] = dot(turned[...], tiles[slot])
+            pltpu.make_async_copy(flat.at[slot], down_out_hbm.at[:, here], result_sem.at[slot]).start()
+
+    def late_copy(other):
+        return remote(late, late_in.at[linear], late_send, late_recv, place(other))
+
+    def finish_rows():
+        hold_a.wait()
+        hold_b.wait()
+        pieces = tokens // 64
+
+        def add_rows(piece, carry):
+            at = pl.ds(pl.multiple_of(piece * 64, 64), 64)
+            extra = held_b[at, :]
+            hidden_out_ref[at, :] = (held_a[at, :] + extra).astype(BF16)
+            return carry + jnp.sum(jnp.sum(extra * extra, axis=1, keepdims=True), axis=0, keepdims=True)
+
+        expert_square = lax.fori_loop(0, pieces, add_rows, jnp.zeros((1, 1), F32))
+        load = pltpu.make_async_copy(middle_grad_hbm, held_a, held_sem.at[0])
+        load.start()
+
+        @pl.loop(0, shards)
+        def _(offset):
+            wait_bytes(first_in.at[offset], first_recv.at[offset])
+
+        load.wait()
+
+        def grad_rows(piece, carry):
+            square, gain_grad = carry
+            at = pl.ds(pl.multiple_of(piece * 64, 64), 64)
+            first = first_in[0, at, :].astype(F32)
+            for offset in range(1, shards):
+                first += first_in[offset, at, :].astype(F32)
+            normed, scaling = norm_forward(hidden_ref[at, :].astype(F32))
+            grad = held_a[at, :] + norm_backward(first * scale_ref[...], normed, scaling)
+            grad_in_ref[at, :] = grad
+            return (
+                square + jnp.sum(jnp.sum(grad * grad, axis=1, keepdims=True), axis=0, keepdims=True),
+                gain_grad + jnp.sum(first * normed, axis=0, keepdims=True),
+            )
+
+        square, gain_grad = lax.fori_loop(
+            0, pieces, grad_rows, (jnp.zeros((1, 1), F32), jnp.zeros((1, width), F32))
+        )
+        for row in range(late_rows):
+            late[row : row + 1, :] = gain_grad[:, row * 128 : (row + 1) * 128]
+        late[late_rows:, :] = shared_ref[...] + pick * (
+            jnp.where(lane == 2, expert_square, 0.0) + jnp.where(lane == 3, square, 0.0)
+        )
+
+        @pl.loop(1, everyone)
+        def _(offset):
+            late_copy((linear + offset) % everyone).start()
+
+        late_in[linear] = late[...]
 
     outs, ins = [wq_out, wo_out], [wq_in, wo_in]
     totals, parts = [wq_total, wo_total], [wq_parts, wo_parts]
@@ -934,19 +1065,32 @@
             (z + 2 * up - 1, x, w),
         )
 
+    per_turn = 3 * per_kind // (2 * planes)
+
     def take(kind, slot):
         wait_bytes(ins[kind].at[slot], line_recv.at[kind, slot])
         totals[kind][...] += ins[kind][slot].astype(F32)
 
-    @pl.loop(0, planes)
-    def _(turn):
-        plane, _, _ = line_order(z, planes, planes - 1 - turn)
-        for kind in range(2):
+    def collect(kind):
+        @pl.loop(0, planes)
+        def _(turn):
+            plane, _, _ = line_order(z, planes, planes - 1 - turn)
+
+            @pl.loop(0, per_turn)
+            def _(unit):
+                multiply((turn + (1 - kind) * planes) * per_turn + unit)
+
             wait_bytes(parts[kind].at[plane], across_recv.at[kind, plane])
 
-            @pl.when(turn < planes - 1)
+            @pl.when(turn < planes - 2)
             def _():
-                start_across(kind, turn + 1)
+                start_across(kind, turn + 2)
+
+            if kind == 1:
+
+                @pl.when(turn >= planes - 2)
+                def _():
+                    start_across(0, turn + 2 - planes)
 
             totals[kind][...] = parts[kind][plane, 0].astype(F32)
 
@@ -963,16 +1107,6 @@
                 outs[kind][plane] = totals[kind][...].astype(BF16)
                 line_copy(kind, plane).start()
 
-    @pl.loop(0, shards)
-    def _(offset):
-        wait_bytes(first_in.at[offset], first_recv.at[offset])
-
-    first_ref[...] = first_in[0].astype(F32)
-
-    @pl.loop(1, shards)
-    def _(offset):
-        first_ref[...] += first_in[offset].astype(F32)
-
     def finish(kind):
         @pl.when(z > 0)
         def _():
@@ -982,21 +1116,7 @@
         def _():
             take(kind, planes)
 
-    finish(0)
-    wq_final[...] = wq_total[...].astype(BF16)
-
-    def home_copy(offset):
-        target = (w + offset) % shards
-        return remote(
-            wq_final.at[rows_of(target, mine)], wq_home.at[w], home_send.at[offset], home_recv.at[w], (z, x, target)
-        )
-
-    @pl.loop(1, shards)
-    def _(offset):
-        home_copy(offset).start()
-
-    pltpu.make_async_copy(wq_final.at[rows_of(w, mine)], wq_home.at[w], home_recv.at[w]).start()
-
+    collect(1)
     finish(1)
     wo_final[...] = wo_total[...].astype(BF16)
     goal = w * rings + ring
@@ -1013,6 +1133,23 @@
     def _():
         pltpu.make_async_copy(wo_final, wo_home, swap_recv).start()
 
+    finish_rows()
+    collect(0)
+    finish(0)
+    wq_final[...] = wq_total[...].astype(BF16)
+
+    def home_copy(offset):
+        target = (w + offset) % shards
+        return remote(
+            wq_final.at[rows_of(target, mine)], wq_home.at[w], home_send.at[offset], home_recv.at[w], (z, x, target)
+        )
+
+    @pl.loop(1, shards)
+    def _(offset):
+        home_copy(offset).start()
+
+    pltpu.make_async_copy(wq_final.at[rows_of(w, mine)], wq_home.at[w], home_recv.at[w]).start()
+
     for part in range(shards):
         wait_bytes(wq_home.at[part], home_recv.at[part])
         rows = wq_home[part].astype(F32)
@@ -1020,6 +1157,14 @@
         key_ref[:, part * key_columns : (part + 1) * key_columns] = rows[:, query_columns : query_columns + key_columns]
         value_ref[:, part * key_columns : (part + 1) * key_columns] = rows[:, query_columns + key_columns :]
 
+    wait_bytes(early_ref.at[pl.ds(0, everyone - 1)], early_recv)
+    early_total_ref[...] = jnp.sum(early_in[...], axis=0)
+    wait_bytes(late_in.at[pl.ds(0, everyone - 1)], late_recv)
+    late_total_ref[...] = jnp.sum(late_in[...], axis=0)
+    wait_bytes(early_ref.at[pl.ds(0, everyone - 1)], early_send)
+    wait_bytes(late_in.at[pl.ds(0, everyone - 1)], late_send)
+    for slot in range(2):
+        wait_bytes(tall.at[slot], result_sem.at[slot])
     wait_bytes(wo_home, swap_recv)
     output_ref[...] = wo_home[...].astype(F32)
 
@@ -1046,7 +1191,10 @@
         wait_bytes(wo_out.at[plane], line_send.at[1, plane])
 
 
-def run_reduce(planes, across, shards, wq_grad, wo_grad, first_part, query_columns, key_columns):
+def run_reduce(
+    planes, across, shards, wq_grad, wo_grad, first_part, hidden, middle, expert_sum, middle_grad, scale, early, shared,
+    rows_in, gate_grad, up_grad, units, pair_grad, query_columns, key_columns,
+):
     rings = planes * across
     everyone = rings * shards
     width = wq_grad.shape[0]
@@ -1054,19 +1202,27 @@
     wq_rows, wo_rows = width // rings, wo_grad.shape[0] // rings
     tokens = first_part.shape[0] // shards
     mine = wq_rows // shards
+    depth, wide = units.shape
+    late_rows = width // 128 + 8
     hbm = pl.BlockSpec(memory_space=pl.ANY)
     vmem = pl.BlockSpec(memory_space=pltpu.VMEM)
     dma = pltpu.SemaphoreType.DMA
     return pl.pallas_call(
         functools.partial(reduce_kernel, planes, across, shards),
-        in_specs=[hbm] * 3,
-        out_specs=[vmem] * 5,
+        in_specs=[hbm] * 3 + [vmem] + [hbm] * 3 + [vmem] * 3 + [hbm] * 5,
+        out_specs=[vmem] * 8 + [hbm] * 3,
         out_shape=[
             jax.ShapeDtypeStruct((mine, query_columns), F32),
             jax.ShapeDtypeStruct((mine, key_columns), F32),
             jax.ShapeDtypeStruct((mine, key_columns), F32),
             jax.ShapeDtypeStruct((wo_rows, width), F32),
+            jax.ShapeDtypeStruct((tokens, width), BF16),
             jax.ShapeDtypeStruct((tokens, width), F32),
+            jax.ShapeDtypeStruct(early.shape[1:], F32),
+            jax.ShapeDtypeStruct((late_rows, 128), F32),
+            jax.ShapeDtypeStruct((width, wide), F32),
+            jax.ShapeDtypeStruct((width, wide), F32),
+            jax.ShapeDtypeStruct((wide, width), F32),
         ],
         scratch_shapes=[
             pltpu.VMEM((planes, across, wq_rows, wq_wide), BF16),
@@ -1082,52 +1238,25 @@
             pltpu.VMEM((shards, mine, wq_wide), BF16),
             pltpu.VMEM((wo_rows, width), BF16),
             pltpu.VMEM((shards, tokens, width), BF16),
+            pltpu.VMEM(early.shape, F32),
+            pltpu.VMEM((late_rows, 128), F32),
+            pltpu.VMEM((everyone, late_rows, 128), F32),
+            pltpu.VMEM((tokens, width), F32),
+            pltpu.VMEM((tokens, width), F32),
+            pltpu.VMEM((depth, wide), BF16),
+            pltpu.VMEM((wide, depth), BF16),
+            pltpu.VMEM((2, depth, 256), BF16),
+            pltpu.VMEM((2, 256, wide), F32),
+            pltpu.VMEM((2, wide, 256), F32),
             dma((2, planes)), dma((2, planes)), dma((2, planes)), dma((2, planes + 1)), dma((shards,)), dma((shards,)),
-            dma, dma, dma((shards,)), dma((shards,)),
+            dma, dma, dma((shards,)), dma((shards,)), dma, dma, dma, dma, dma((2,)), dma, dma((2,)), dma((2,)),
         ],
         compiler_params=pltpu.CompilerParams(vmem_limit_bytes=VMEM_LIMIT, collective_id=3, has_side_effects=True),
         cost_estimate=pl.CostEstimate(flops=70 * 10**9, bytes_accessed=40 * 10**6, transcendentals=0),
-    )(wq_grad, wo_grad, first_part)
-
-
-def total_kernel(planes, across, shards, parts_ref, total_ref, parts_in, send, recv):
-    z, x, w = lax.axis_index("z"), lax.axis_index("x"), lax.axis_index("w")
-    everyone = planes * across * shards
-    linear = (z * across + x) * shards + w
-    barrier = pltpu.get_barrier_semaphore()
-
-    def place(index):
-        return (index // shards // across, index // shards % across, index % shards)
-
-    @pl.loop(1, everyone)
-    def _(offset):
-        pl.semaphore_signal(barrier, inc=1, device_id=place((linear + offset) % everyone), device_id_type=MESH)
-
-    pl.semaphore_wait(barrier, everyone - 1)
-
-    @pl.loop(1, everyone)
-    def _(offset):
-        other = (linear + offset) % everyone
-        remote(parts_ref.at[other], parts_in.at[linear], send, recv, place(other)).start()
-
-    parts_in[linear] = parts_ref[linear]
-    wait_bytes(parts_ref.at[pl.ds(0, everyone - 1)], recv)
-    total_ref[...] = jnp.sum(parts_in[...], axis=0)
-    wait_bytes(parts_ref.at[pl.ds(0, everyone - 1)], send)
-
-
-def run_total(planes, across, shards, parts):
-    everyone, rows, lanes = parts.shape
-    return pl.pallas_call(
-        functools.partial(total_kernel, planes, across, shards),
-        in_specs=[pl.BlockSpec(memory_space=pltpu.VMEM)],
-        out_specs=pl.BlockSpec(memory_space=pltpu.VMEM),
-        out_shape=jax.ShapeDtypeStruct((rows, lanes), F32),
-        scratch_shapes=[
-            pltpu.VMEM((everyone, rows, lanes), F32), pltpu.SemaphoreType.DMA, pltpu.SemaphoreType.DMA,
-        ],
-        compiler_params=pltpu.CompilerParams(vmem_limit_bytes=VMEM_LIMIT, collective_id=4, has_side_effects=True),
-    )(parts)
+    )(
+        wq_grad, wo_grad, first_part, hidden, middle, expert_sum, middle_grad, scale, early, shared, rows_in, gate_grad,
+        up_grad, units, pair_grad,
+    )
 
 
 def expert_kernel(
@@ -1155,6 +1284,10 @@
     def order(step):
         return line_order(z, planes, step)
 
+    inner = ((z > 0) & (z < planes - 1)).astype(jnp.int32)
+    first_back = 2 - (z == 1).astype(jnp.int32)
+    second_back = 3 - inner * first_back
+    third_back = 1 + 2 * inner
     greet_plane_and_line(planes, across, shards)
 
     def line_up(block, hop):
@@ -1333,7 +1466,7 @@
             values = columns[slice_of(index), 0:1]
             share_back[block, index] = jnp.sum(jnp.where(mine, values, 0.0), axis=0, keepdims=True)
 
-        @pl.when(step > 1)
+        @pl.when((step == first_back) | (step == second_back))
         def _():
             start_back(step, block)
 
@@ -1383,7 +1516,11 @@
         wait_bytes(share_back.at[0, pl.ds(0, in_plane - 1)], back_share_send.at[step])
 
     def sum_copy(block):
-        return remote(plane_rows.at[block], partial_in.at[z], sum_send.at[block], sum_recv.at[z], (block, x, w))
+        up = (block > z).astype(jnp.int32)
+        relayed = (jnp.abs(block - z) == planes - 1).astype(jnp.int32)
+        slot = z + relayed * (planes - z)
+        goal = block + relayed * (1 - 2 * up) * (planes - 2)
+        return remote(plane_rows.at[block], partial_in.at[slot], sum_send.at[block], sum_recv.at[slot], (goal, x, w))
 
     def sum_share_copy(block):
         return remote(
@@ -1393,7 +1530,7 @@
 
     @pl.loop(0, planes)
     def _(turn):
-        step = jnp.where(turn < planes - 2, turn + 2, planes - 1 - turn)
+        step = jnp.where(turn == 0, first_back, jnp.where(turn == 1, second_back, jnp.where(turn == 2, third_back, 0)))
         block, _, _ = order(step)
         wait_bytes(back_hbm.at[block], back_recv.at[step])
         load = pltpu.make_async_copy(back_hbm.at[block], rows, load_sem)
@@ -1405,10 +1542,24 @@
         def _():
             sum_share_copy(block).start()
 
+            merges = (inner == 1) & (jnp.abs(block - z) == 2)
+
+            @pl.when(merges)
+            def _():
+                wait_bytes(partial_in.at[planes], sum_recv.at[planes])
+
             @pl.loop(0, width // chunk)
             def _(part):
                 wide = pl.ds(pl.multiple_of(part * chunk, chunk), chunk)
-                plane_rows[block, :, wide] = dot_tn(chosen[step], rows[:, wide]).astype(BF16)
+                summed = dot_tn(chosen[step], rows[:, wide])
+
+                @pl.when(merges)
+                def _():
+                    plane_rows[block, :, wide] = (summed + partial_in[planes, :, wide].astype(F32)).astype(BF16)
+
+                @pl.when(jnp.logical_not(merges))
+                def _():
+                    plane_rows[block, :, wide] = summed.astype(BF16)
 
             sum_copy(block).start()
 
@@ -1421,26 +1572,29 @@
                 wide = pl.ds(pl.multiple_of(part * chunk, chunk), chunk)
                 row_grad_ref[:, wide] = dot_tn(chosen[0], rows[:, wide])
 
-        @pl.when(turn == planes - 4)
-        def _():
-            wait_back(planes - 1)
-            start_back(1, order(1)[0])
-
-        @pl.when(turn == planes - 3)
-        def _():
-            wait_back(1)
+        @pl.when(turn == 0)
+        def _():
+            wait_back(second_back)
+            start_back(third_back, order(third_back)[0])
+
+        @pl.when(turn == 1)
+        def _():
+            wait_back(third_back)
             start_back(0, z)
 
     @pl.loop(1, planes)
     def _(offset):
         other = (z + offset) % planes
-        wait_bytes(partial_in.at[other], sum_recv.at[other])
         wait_bytes(share_home.at[other], sum_share_recv.at[other])
 
-        @pl.loop(0, width // chunk)
-        def _(part):
-            wide = pl.ds(pl.multiple_of(part * chunk, chunk), chunk)
-            row_grad_ref[:, wide] += partial_in[other, :, wide].astype(F32)
+        @pl.when(jnp.abs(other - z) < planes - 1)
+        def _():
+            wait_bytes(partial_in.at[other], sum_recv.at[other])
+
+            @pl.loop(0, width // chunk)
+            def _(part):
+                wide = pl.ds(pl.multiple_of(part * chunk, chunk), chunk)
+                row_grad_ref[:, wide] += partial_in[other, :, wide].astype(F32)
 
     @pl.loop(1, planes)
     def _(offset):
@@ -1449,8 +1603,7 @@
         wait_bytes(share_home.at[other], sum_share_send.at[other])
 
     wait_back(0)
-    for step in range(2, planes - 1):
-        wait_back(step)
+    wait_back(first_back)
 
 
 def run_experts(planes, across, shards, capacity, own, shares, slots, my_slots, w_gate, w_up, w_down, top_rows):
@@ -1492,11 +1645,11 @@
             pltpu.VMEM((count, units), BF16),
             pltpu.VMEM((count, units), BF16),
             pltpu.VMEM((count, 128), F32),
-            pltpu.VMEM((planes, tokens, width), BF16),
+            pltpu.VMEM((planes + 1, tokens, width), BF16),
             dma((2, planes + 1)), dma((2, planes + 1)), dma((planes,)), dma((planes,)),
             dma((planes,)), dma((planes,)), dma((planes,)), dma((planes,)),
             dma((planes,)), dma((planes,)), dma((planes,)), dma((planes,)),
-            dma((planes,)), dma((planes,)), dma((planes,)), dma((planes,)),
+            dma((planes,)), dma((planes + 1,)), dma((planes,)), dma((planes,)),
             dma, dma, dma((5,)),
         ],
         compiler_params=pltpu.CompilerParams(vmem_limit_bytes=VMEM_LIMIT, collective_id=1, has_side_effects=True),
@@ -1535,7 +1688,6 @@
     router_full = small_all[:experts].astype(BF16)
     ffn_scale, attn_scale = small_all[experts : experts + 1], small_all[experts + 1 : experts + 2]
     source = hidden_in.astype(F32)
-    first_normed, first_scale = norm_forward(source)
     middle = source + branch
     second_normed, second_scale = norm_forward(middle)
     second_input = (second_normed * ffn_scale).astype(BF16)
@@ -1552,11 +1704,7 @@
         top_rows,
     )
     share_grad = share_grad[:, 0, :]
-    rows_in, pair_grad = rows_in.reshape(-1, width), pair_grad.reshape(-1, width)
     units = w_gate.shape[2]
-    grad_down = dot_tn(hidden_units.reshape(-1, units), pair_grad)[None]
-    grad_gate = dot_tn(rows_in, gate_grad.reshape(-1, units))[None]
-    grad_up = dot_tn(rows_in, up_grad.reshape(-1, units))[None]
     grad_top = cotangent.astype(F32)
     share_center = jnp.sum(shares * share_grad, axis=0, keepdims=True)
     logit_grad = (shares * (share_grad - share_center)).astype(BF16)
@@ -1568,35 +1716,35 @@
         planes, across, shards, capacity, middle_grad.astype(BF16), w_output, attended, query_raw, key_raw, value,
         first_input, weights, query_gain_row, key_gain_row, cosine, sine, slots_flat, weighted,
     )
-    hidden_out = (middle + expert_sum).astype(BF16)
-    sum_query, sum_key, sum_value, sum_output, first_grad = run_reduce(
-        planes, across, shards, wq_grad, wo_grad, first_part, w_query.shape[1], key_projection.shape[1]
+    mine = width // device_count
+    early = jnp.concatenate(
+        [router_grad.reshape(device_count, mine * experts), ffn_gain_grad.reshape(device_count, mine)], axis=1
     )
-    attn_gain_grad = jnp.sum(first_grad * first_normed, axis=0)
-    grad_in = middle_grad + norm_backward(first_grad * attn_scale, first_normed, first_scale)
-
-    squares = jnp.stack(
-        [jnp.sum(source * source), jnp.sum(branch * branch), jnp.sum(expert_sum * expert_sum), jnp.sum(grad_in * grad_in)]
+    early = jnp.pad(early, ((0, 0), (0, -early.shape[1] % 1024))).reshape(device_count, -1, 128)
+    squares = jnp.stack([jnp.sum(source * source), jnp.sum(branch * branch)])
+    shared = jnp.concatenate(
+        [
+            query_gain_grad[0:1],
+            key_gain_grad[0:1],
+            jnp.pad(squares, (0, head_size - 2))[None, :],
+            jnp.zeros((5, head_size), F32),
+        ],
+        axis=0,
     )
-    mine = width // device_count
-    shared = jnp.concatenate([query_gain_grad[0], key_gain_grad[0], squares])
-    parts = jnp.concatenate(
-        [
-            router_grad.reshape(device_count, mine * experts),
-            ffn_gain_grad.reshape(device_count, mine),
-            attn_gain_grad.reshape(device_count, mine),
-            jnp.broadcast_to(shared[None, :], (device_count, shared.shape[0])),
-        ],
-        axis=1,
+    (
+        sum_query, sum_key, sum_value, sum_output, hidden_out, grad_in, early_total, late_total, grad_gate, grad_up, grad_down,
+    ) = run_reduce(
+        planes, across, shards, wq_grad, wo_grad, first_part, hidden_in, middle, expert_sum, middle_grad, attn_scale, early,
+        shared, rows_in.reshape(-1, width), gate_grad.reshape(-1, units), up_grad.reshape(-1, units),
+        hidden_units.reshape(-1, units), pair_grad.reshape(-1, width), w_query.shape[1], key_projection.shape[1],
     )
-    length = parts.shape[1]
-    padded = -(-length // 1024) * 1024
-    parts = jnp.pad(parts, ((0, 0), (0, padded - length))).reshape(device_count, padded // 128, 128)
-    summed = run_total(planes, across, shards, parts).reshape(-1)
-    sum_router = summed[: mine * experts].reshape(mine, experts)
-    sum_ffn = summed[mine * experts : mine * (experts + 1)]
-    sum_attn = summed[mine * (experts + 1) : mine * (experts + 2)]
-    totals = summed[mine * (experts + 2) : length]
+    early_total = early_total.reshape(-1)
+    sum_router = early_total[: mine * experts].reshape(mine, experts)
+    sum_ffn = early_total[mine * experts : mine * (experts + 1)]
+    linear = (lax.axis_index("z") * across + lax.axis_index("x")) * shards + lax.axis_index("w")
+    sum_attn = lax.dynamic_slice_in_dim(late_total[: width // 128].reshape(-1), linear * mine, mine)
+    late_total = late_total[width // 128 :]
+    totals = jnp.concatenate([late_total[0], late_total[1], late_total[2, :4]])
     root_mean_squares = jnp.sqrt(totals[2 * head_size :] / (tokens_here * device_count * width))
     return (
         hidden_out,
@@ -1610,9 +1758,9 @@
         sum_output,
         sum_ffn,
         sum_router,
-        grad_gate,
-        grad_up,
-        grad_down,
+        grad_gate[None],
+        grad_up[None],
+        grad_down[None],
         root_mean_squares,
     )
 

time: 820 us -> 775 us (0.945)
  matrix products: 38.5 us -> 5.23 us
  Pallas kernels: 736 us -> 713 us
  local copies, waits for them, and re-layouts: 18.5 us -> 32.2 us
    dot_general x4 -> x1, matrix products: 36.7 us -> 0.48 us  [dot_tn(): lax.dot_general(left, right, (((0,), (0,)), ((), ())), preferred_element_...]
    pallas_call x1 -> x0, Pallas kernels: 17.5 us -> none  [run_total(): pl.pallas_call(functools.partial(total_kernel, planes, across, shards), i...]
    pallas_call x1, Pallas kernels: 130 us -> 144 us  [run_reduce(): pl.pallas_call(functools.partial(reduce_kernel, planes, across, shards),...]
    unnamed x78 -> x64, local copies, waits for them, and re-layouts: 8.09 us -> 21.5 us
    pallas_call x1, Pallas kernels: 168 us -> 156 us  [run_backward(): pl.pallas_call(functools.partial(attention_backward, planes, across, shar...]
    reduce_sum x2 -> x0, other arithmetic: 8.85 us -> none  [the longest x1 5.54 us: local(): jnp.sum(expert_sum * expert_sum)]
where the time goes in v5:
time: 775 us; the launch traced here: 769 us
  Pallas kernels  713 us (92%)
  local copies, waits for them, and re-layouts  32.2 us (4%)
  other arithmetic  18 us (2%)
    pallas_call x1, Pallas kernels, run_experts(): pl.pallas_call(functools.partial(expert_kernel, planes, across, shards, c...  242 us
    pallas_call x1, Pallas kernels, run_forward(): pl.pallas_call(functools.partial(attention_forward, planes, across, shard...  171 us
    pallas_call x1, Pallas kernels, run_backward(): pl.pallas_call(functools.partial(attention_backward, planes, across, shar...  156 us
    pallas_call x1, Pallas kernels, run_reduce(): pl.pallas_call(functools.partial(reduce_kernel, planes, across, shards),...  144 us
    unnamed x64, local copies, waits for them, and re-layouts  21.5 us

profile of v5, /device:TPU:1, one launch (start us, length us, event | category | flops | bytes accessed | tf_op | source)
XLA Modules:
  0.0 769.1 jit_solution(1830778389797625528)
XLA Ops:
  3.4 1.4 fusion.12.small_ref
  4.8 2.0 fusion.5
  6.8 1.3 pad_maximum_fusion
  8.1 170.8 %shard_map.262 = (bf16[1024,2048]{1,0:T(8,128)(2,1)}, f32[1024,1024]{1,0:T(8,128)}, f32[1024,128]{1,0:T(8,128)}, bf16[1024,128]{1,0:T(8,128)(2,1)}, bf16[1024,10...) custom-call(bf16[256,2048]{1,0:T(8,128)(2,1)} %hidden_ref.1, ...), custom_call_target="tpu_custom_call" | custom-call | flops 70000001024 | bytes 40000000 | tf_op jit(solution)/shard_map/pallas_call | solution.py:715
  178.9 3.0 multiply_reduce_fusion.3
  182.0 1.9 fusion.19
  183.9 1.5 fusion.21
  185.4 1.0 fusion.6
  188.5 241.7 %shard_map.263 = (bf16[4,640,2048]{2,1,0:T(8,128)(2,1)}, bf16[4,640,2048]{2,1,0:T(8,128)(2,1)}, bf16[4,640,2048]{2,1,0:T(8,128)(2,1)}, bf16[4,640,768]{2,1,0:T(8...) custom-call(bf16[256,2048]{1,0:T(8,128)(2,1)} %copy-done.2, ...), custom_call_target="tpu_custom_call" | custom-call | flops 193273528320 | bytes 100000000 | tf_op jit(solution)/shard_map/pallas_call | solution.py:1619
  431.8 4.3 multiply_reduce_fusion.1
  438.7 3.8 fusion.20
  442.5 156.2 %shard_map.264 = (bf16[1024,2048]{1,0:T(8,128)(2,1)}, bf16[2048,1280]{1,0:T(8,128)(2,1)}, bf16[1024,2048]{1,0:T(8,128)(2,1)}, f32[8,128]{1,0:T(8,128)}, f32[8,12...) custom-call(bf16[256,2048]{1,0:T(8,128)(2,1)} %get-tuple-element.134.own_grad_ref, ...), custom_call_target="tpu_custom_call" | custom-call | flops 70000001024 | bytes 60000000 | tf_op jit(solution)/shard_map/pallas_call | solution.py:797
  600.7 143.8 %shard_map.265 = (f32[64,4096]{1,0:T(8,128)}, f32[64,512]{1,0:T(8,128)}, f32[64,512]{1,0:T(8,128)}, f32[128,2048]{1,0:T(8,128)}, bf16[256,2048]{1,0:T(8,128)(2,1...) custom-call(bf16[2048,1280]{1,0:T(8,128)(2,1)} %get-tuple-element.65, ...), custom_call_target="tpu_custom_call" | custom-call | flops 70000001024 | bytes 40000000 | tf_op jit(solution)/shard_map/pallas_call | solution.py:1210
  744.5 1.3 slice.59
  745.9 1.2 sqrt_bitcast_fusion
  747.1 1.3 slice_bitcast_fusion.1
  751.1 2.5 copy.52
  753.5 1.3 copy.53
  754.9 1.0 copy.54
  757.2 1.0 copy.57
  758.1 3.2 copy.58
  761.5 3.2 copy.59
  765.2 0.9 slice-done.1
  766.1 2.7 copy.60
  (84 shorter events, 15.6 us)
Async XLA Ops:
  8.1 170.8 %copy-start.8 = (bf16[256,2048]{1,0:T(8,128)(2,1)S(1)}, bf16[256,2048]{1,0:T(8,128)(2,1)}, u32[]{:S(2)}) copy-start(bf16[256,2048]{1,0:T(8,128)(2,1)} %hidden_ref.1) | copy-start | bytes 3145732
  182.0 5.2 copy-start
  182.0 5.2 copy-start.18
  185.4 1.7 copy-start.16
  186.7 1.8 copy-start.2
  188.5 241.7 %copy-start.13 = (f32[32,256]{1,0:T(8,128)S(1)}, f32[32,256]{1,0:T(8,128)}, u32[]{:S(2)}) copy-start(f32[32,256]{1,0:T(8,128)} %copy-done.12) | copy-start | bytes 98308
  188.5 243.3 %copy-start.7 = (bf16[4,4,8,512]{3,2,0,1:T(8,128)(2,1)S(1)}, bf16[4,4,8,512]{3,2,0,1:T(8,128)(2,1)}, u32[]{:S(2)}) copy-start(bf16[4,4,8,512]{3,2,0,1:T(8,128)(2,1)} %copy-done.6) | copy-start | bytes 393220
  188.5 243.3 %copy-start.17 = (f32[1,4,512]{2,0,1:T(1,128)S(1)}, f32[1,4,512]{2,0,1:T(1,128)}, u32[]{:S(2)}) copy-start(f32[1,4,512]{2,0,1:T(1,128)} %copy-done.16) | copy-start | bytes 24580
  188.5 243.3 %copy-start.19 = (f32[256]{0:T(256)S(1)}, f32[256]{0:T(256)}, u32[]{:S(2)}) copy-start(f32[256]{0:T(256)} %copy-done.18) | copy-start | bytes 3076
  431.8 4.3 copy-start.3
  436.2 1.9 copy-start.1
  437.1 1.5 copy-start.11
  442.5 157.5 %copy-start.20 = (f32[8]{0:T(128)S(1)}, f32[8]{0:T(128)}, u32[]{:S(2)}) copy-start(f32[8]{0:T(128)} %pad.21.clone) | copy-start | bytes 100
  442.5 157.5 %copy-start.21 = (f32[1,128]{1,0:T(1,128)S(1)}, f32[1,128]{1,0:T(1,128)}, u32[]{:S(2)}) copy-start(f32[1,128]{1,0:T(1,128)} %fusion.19) | copy-start | bytes 1540
  744.5 9.0 %copy-start.5 = (f32[256,2048]{1,0:T(8,128)S(1)}, f32[256,2048]{1,0:T(8,128)}, u32[]{:S(2)}) copy-start(f32[256,2048]{1,0:T(8,128)} %get-tuple-element.168) | copy-start | bytes 6291460
  751.1 3.8 copy-start.10
  751.1 4.8 copy-start.15
  751.1 5.4 copy-start.14
  751.1 6.1 copy-start.9
  753.5 4.6 copy-start.4
  754.9 6.5 slice-start.2
  758.1 3.4 slice-start.3
  758.1 7.1 slice-start
  761.5 4.6 slice-start.1
  (2 other events, 1.4 us)

commit v6 on v5

--- a/solution.py
+++ b/solution.py
@@ -2,6 +2,7 @@
 
 import jax
 import jax.numpy as jnp
+import numpy as np
 from jax import lax
 from jax.experimental import pallas as pl
 from jax.experimental.pallas import tpu as pltpu
@@ -13,7 +14,7 @@
 ROPE_BASE = 1000000.0
 F32 = jnp.float32
 BF16 = jnp.bfloat16
-VMEM_LIMIT = 62 * 1024 * 1024
+VMEM_LIMIT = 65024 * 1024
 
 
 def dot(left, right):
@@ -29,11 +30,11 @@
 
 
 def rope_tables(seq_length, head_size):
-    indices = jnp.arange(head_size // 2, dtype=F32)
-    frequency = ROPE_BASE ** (-2.0 * indices / head_size)
-    angles = jnp.arange(seq_length, dtype=F32)[:, None] * frequency[None, :]
-    cosine, sine = jnp.cos(angles), jnp.sin(angles)
-    return jnp.concatenate([cosine, cosine], axis=1), jnp.concatenate([-sine, sine], axis=1)
+    indices = np.arange(head_size // 2, dtype=np.float32)
+    frequency = (np.float32(ROPE_BASE) ** (np.float32(-2.0) * indices / np.float32(head_size))).astype(np.float32)
+    angles = np.arange(seq_length, dtype=np.float32)[:, None] * frequency[None, :]
+    cosine, sine = np.cos(angles), np.sin(angles)
+    return np.concatenate([cosine, cosine], axis=1), np.concatenate([-sine, sine], axis=1)
 
 
 def norm_forward(values):
@@ -100,12 +101,13 @@
 def attention_forward(
     planes, across, shards, capacity, heads_a_step,
     own_ref, small_ref, routes_ref, top_ref, wq_hbm, wk_hbm, wv_hbm, query_gain_ref, key_gain_ref, cosine_ref, sine_ref, wo_ref,
-    input_ref, query_raw_ref, key_raw_ref, value_ref, attended_ref, branch_ref, slots_ref, my_slots_ref, small_hbm,
+    input_ref, query_raw_ref, key_raw_ref, value_ref, attended_ref, middle_ref, slots_ref, my_slots_ref, shares_ref, squares_ref,
+    second_hbm, small_hbm,
     weights_hbm, top_rows_hbm,
     hidden, small_in, weights, key_rot_ref, routes_in, far_slots, plane_rows, stage, chosen, pair_out, far_out,
     gather_send, gather_recv, small_send, small_recv, weight_send, weight_recv, route_send, route_recv, plane_route_send,
     plane_route_recv, far_send, far_recv,
-    line_send, line_recv, top_send, top_recv, pair_send, pair_recv, store_sem, small_sem,
+    line_send, line_recv, top_send, top_recv, pair_send, pair_recv, store_sem, small_sem, second_sem,
 ):
     step = pl.program_id(0)
     head_size = cosine_ref.shape[1]
@@ -435,7 +437,7 @@
         project(opposite, far_out, pl.ds(0, tokens))
         far_copy.start()
         wait_bytes(hidden.at[pl.ds(tokens, tokens)], pair_recv.at[1])
-        project(w, branch_ref, pl.ds(tokens, tokens))
+        project(w, middle_ref, pl.ds(tokens, tokens))
         @pl.loop(1, in_plane)
         def _(offset):
             index = (me + offset) % in_plane
@@ -448,7 +450,44 @@
         relay(1, 3)
         pack(1, 3, far_slots)
         wait_bytes(hidden.at[far_at], pair_recv.at[2])
-        branch_ref[...] += hidden[far_at, :].astype(F32)
+        wait_bytes(far_out, pair_send.at[2])
+        ffn_row = jnp.concatenate([small_in[part, experts : experts + 1, :] for part in range(shards)], axis=1)
+
+        def finish_rows(piece, carry):
+            at = pl.ds(pl.multiple_of(piece * 64, 64), 64)
+            far = pl.ds(pl.multiple_of(2 * tokens + piece * 64, 64), 64)
+            branch = middle_ref[at, :] + hidden[far, :].astype(F32)
+            source = own_ref[at, :].astype(F32)
+            middle = source + branch
+            middle_ref[at, :] = middle
+            normed, _ = norm_forward(middle)
+            far_out[at, :] = (normed * ffn_row).astype(BF16)
+            return (
+                carry[0] + jnp.sum(jnp.sum(source * source, axis=1, keepdims=True), axis=0, keepdims=True),
+                carry[1] + jnp.sum(jnp.sum(branch * branch, axis=1, keepdims=True), axis=0, keepdims=True),
+            )
+
+        zero = jnp.zeros((1, 1), F32)
+        source_square, branch_square = lax.fori_loop(0, tokens // 64, finish_rows, (zero, zero))
+        second_store = pltpu.make_async_copy(far_out, second_hbm, second_sem)
+        second_store.start()
+        lane = lax.broadcasted_iota(jnp.int32, (8, 128), 1)
+        row = lax.broadcasted_iota(jnp.int32, (8, 128), 0)
+        values = jnp.where(lane == 0, source_square, 0.0) + jnp.where(lane == 1, branch_square, 0.0)
+        squares_ref[...] = jnp.where(row == 2, values, 0.0)
+        logits = jnp.zeros((experts, tokens), F32)
+        for part in range(shards):
+            logits += dot_nt(small_in[part, :experts, :].astype(BF16), far_out[:, part * depth : (part + 1) * depth])
+        expert_ids = lax.broadcasted_iota(jnp.int32, (experts, tokens), 0)
+        hits = jnp.zeros((experts, tokens), F32)
+        for k in range(routes_ref.shape[0]):
+            hits += (routes_ref[k : k + 1, :] == expert_ids).astype(F32)
+        routed = hits > 0.0
+        peaks = jnp.max(jnp.where(routed, logits, -jnp.inf), axis=0, keepdims=True)
+        shifted = jnp.where(routed, jnp.exp(jnp.where(routed, logits - peaks, 0.0)), 0.0)
+        shares = shifted / jnp.sum(shifted, axis=0, keepdims=True)
+        for expert in range(experts):
+            shares_ref[expert] = shares[expert : expert + 1, :]
 
         @pl.loop(0, planes)
         def _(block):
@@ -457,7 +496,7 @@
                 for column in range(2):
                     wait_bytes(stage.at[column, 0, pl.ds(0, (targets - 1) * capacity)], top_send.at[column, block])
 
-        for kind in range(3):
+        for kind in range(2):
             wait_bytes(far_out, pair_send.at[kind])
 
         @pl.loop(1, shards)
@@ -488,6 +527,7 @@
 
         store.wait()
         small_store.wait()
+        second_store.wait()
 
 
 def attention_backward(
@@ -738,6 +778,9 @@
             whole((tokens, width)),
             whole(slots_shape),
             whole(slots_shape),
+            whole(slots_shape),
+            whole((8, 128)),
+            hbm,
             hbm,
             hbm,
             hbm,
@@ -751,6 +794,9 @@
             jax.ShapeDtypeStruct((tokens, width), F32),
             jax.ShapeDtypeStruct(slots_shape, jnp.int32),
             jax.ShapeDtypeStruct(slots_shape, jnp.int32),
+            jax.ShapeDtypeStruct(slots_shape, F32),
+            jax.ShapeDtypeStruct((8, 128), F32),
+            jax.ShapeDtypeStruct((tokens, width), BF16),
             jax.ShapeDtypeStruct((shards,) + small.shape, F32),
             jax.ShapeDtypeStruct((width, (steps + 1) * wide), BF16),
             jax.ShapeDtypeStruct((planes, count, width), BF16),
@@ -769,7 +815,7 @@
             pltpu.VMEM((tokens, width), BF16),
             dma((3,)), dma((3,)), dma((shards,)), dma((shards,)), dma((steps + 1,)), dma((steps + 1,)),
             dma((planes,)), dma((planes,)), dma, dma((in_plane,)), dma, dma,
-            dma((2, 2, planes + 1)), dma((2, 2, planes + 1)), dma((2, planes)), dma((planes,)), dma((3,)), dma((3,)), dma, dma,
+            dma((2, 2, planes + 1)), dma((2, 2, planes + 1)), dma((2, planes)), dma((planes,)), dma((3,)), dma((3,)), dma, dma, dma,
         ],
         compiler_params=pltpu.CompilerParams(vmem_limit_bytes=VMEM_LIMIT, collective_id=5, has_side_effects=True),
         cost_estimate=pl.CostEstimate(flops=70 * 10**9, bytes_accessed=40 * 10**6, transcendentals=6 * 10**6),
@@ -1261,16 +1307,17 @@
 
 def expert_kernel(
     planes, across, shards, capacity,
-    own_ref, share_ref, slots_ref, my_slots_ref, gate_ref, up_ref, down_ref, top_hbm,
-    rows_hbm, back_hbm, weighted_hbm, units_hbm, gate_grad_hbm, up_grad_hbm, pair_grad_hbm, row_grad_ref, share_grad_ref,
-    plane_rows, plane_shares, share_in, share_back, share_home, stage, chosen, rows, top, units,
+    own_ref, share_ref, slots_ref, my_slots_ref, gate_ref, up_ref, down_ref, small_ref, top_hbm,
+    middle_hbm, cotangent_hbm, rows_hbm, back_hbm, weighted_hbm, units_hbm, gate_grad_hbm, up_grad_hbm, pair_grad_hbm, row_grad_ref, low_grad_hbm, logit_grad_ref, gain_grad_ref,
+    share_grad_ref, middle, plane_rows, plane_shares, share_in, share_back, share_home, stage, chosen, rows, top, units,
     gate_grad, up_grad, columns, partial_in,
     line_send, line_recv, plane_share_send, plane_share_recv, out_send, out_recv, out_share_send, out_share_recv,
     back_send, back_recv, back_share_send, back_share_recv, sum_send, sum_recv, sum_share_send, sum_share_recv,
-    load_sem, top_sem, store_sem,
+    load_sem, top_sem, store_sem, middle_sem,
 ):
     z, x, w = lax.axis_index("z"), lax.axis_index("x"), lax.axis_index("w")
     in_plane = across * shards
+    experts = planes * in_plane
     me = x * shards + w
     tokens, width = own_ref.shape
     count = in_plane * capacity
@@ -1300,6 +1347,8 @@
             plane_rows.at[block], plane_rows.at[block], line_send.at[1, hop], line_recv.at[1, hop], (z - 1, x, w)
         )
 
+    middle_load = pltpu.make_async_copy(middle_hbm, middle, middle_sem)
+    middle_load.start()
     plane_rows[z] = own_ref[...]
 
     @pl.when(z + 1 < planes)
@@ -1518,8 +1567,8 @@
     def sum_copy(block):
         up = (block > z).astype(jnp.int32)
         relayed = (jnp.abs(block - z) == planes - 1).astype(jnp.int32)
-        slot = z + relayed * (planes - z)
         goal = block + relayed * (1 - 2 * up) * (planes - 2)
+        slot = z + relayed * (goal - z)
         return remote(plane_rows.at[block], partial_in.at[slot], sum_send.at[block], sum_recv.at[slot], (goal, x, w))
 
     def sum_share_copy(block):
@@ -1546,7 +1595,7 @@
 
             @pl.when(merges)
             def _():
-                wait_bytes(partial_in.at[planes], sum_recv.at[planes])
+                wait_bytes(partial_in.at[z], sum_recv.at[z])
 
             @pl.loop(0, width // chunk)
             def _(part):
@@ -1555,7 +1604,7 @@
 
                 @pl.when(merges)
                 def _():
-                    plane_rows[block, :, wide] = (summed + partial_in[planes, :, wide].astype(F32)).astype(BF16)
+                    plane_rows[block, :, wide] = (summed + partial_in[z, :, wide].astype(F32)).astype(BF16)
 
                 @pl.when(jnp.logical_not(merges))
                 def _():
@@ -1581,6 +1630,9 @@
         def _():
             wait_back(third_back)
             start_back(0, z)
+
+    cotangent_load = pltpu.make_async_copy(cotangent_hbm, rows.at[pl.ds(0, tokens)], load_sem)
+    cotangent_load.start()
 
     @pl.loop(1, planes)
     def _(offset):
@@ -1602,11 +1654,36 @@
         wait_bytes(plane_rows.at[other], sum_send.at[other])
         wait_bytes(share_home.at[other], sum_share_send.at[other])
 
+    cotangent_load.wait()
+    middle_load.wait()
+    depth = width // shards
+    share_grad = jnp.concatenate([share_grad_ref[index] for index in range(experts)], axis=0)
+    shares = jnp.concatenate([share_ref[index] for index in range(experts)], axis=0)
+    center = jnp.sum(shares * share_grad, axis=0, keepdims=True)
+    logit_grad_ref[...] = (shares * (share_grad - center)).astype(BF16)
+    for part in range(shards):
+        wide = slice(part * depth, (part + 1) * depth)
+        row_grad_ref[:, wide] += dot_tn(logit_grad_ref[...], small_ref[part, :experts, :].astype(BF16))
+    ffn_row = jnp.concatenate([small_ref[part, experts : experts + 1, :] for part in range(shards)], axis=1)
+
+    def finish_rows(piece, gain_grad):
+        at = pl.ds(pl.multiple_of(piece * 64, 64), 64)
+        normed, scaling = norm_forward(middle[at, :])
+        second_grad = row_grad_ref[at, :]
+        grad = rows[at, :].astype(F32) + norm_backward(second_grad * ffn_row, normed, scaling)
+        row_grad_ref[at, :] = grad
+        rows[pl.ds(pl.multiple_of(tokens + piece * 64, 64), 64), :] = grad.astype(BF16)
+        return gain_grad + jnp.sum(second_grad * normed, axis=0, keepdims=True)
+
+    gain_grad_ref[...] = lax.fori_loop(0, tokens // 64, finish_rows, jnp.zeros((1, width), F32))
+    low_store = pltpu.make_async_copy(rows.at[pl.ds(tokens, tokens)], low_grad_hbm, middle_sem)
+    low_store.start()
     wait_back(0)
     wait_back(first_back)
-
-
-def run_experts(planes, across, shards, capacity, own, shares, slots, my_slots, w_gate, w_up, w_down, top_rows):
+    low_store.wait()
+
+
+def run_experts(planes, across, shards, capacity, own, shares, slots, my_slots, w_gate, w_up, w_down, small_all, top_rows, middle, cotangent):
     tokens, width = own.shape
     in_plane = across * shards
     count = in_plane * capacity
@@ -1618,8 +1695,8 @@
     flops = 12 * planes * count * width * units
     return pl.pallas_call(
         functools.partial(expert_kernel, planes, across, shards, capacity),
-        in_specs=[vmem] * 7 + [hbm],
-        out_specs=[hbm] * 7 + [vmem] * 2,
+        in_specs=[vmem] * 8 + [hbm] * 3,
+        out_specs=[hbm] * 7 + [vmem, hbm, vmem, vmem],
         out_shape=[
             jax.ShapeDtypeStruct((planes, count, width), BF16),
             jax.ShapeDtypeStruct((planes, count, width), BF16),
@@ -1629,9 +1706,13 @@
             jax.ShapeDtypeStruct((planes, count, units), BF16),
             jax.ShapeDtypeStruct((planes, count, width), BF16),
             jax.ShapeDtypeStruct((tokens, width), F32),
-            jax.ShapeDtypeStruct((experts, 1, tokens), F32),
+            jax.ShapeDtypeStruct((tokens, width), BF16),
+            jax.ShapeDtypeStruct((experts, tokens), BF16),
+            jax.ShapeDtypeStruct((1, width), F32),
         ],
         scratch_shapes=[
+            pltpu.VMEM((experts, 1, tokens), F32),
+            pltpu.VMEM((tokens, width), F32),
             pltpu.VMEM((planes, tokens, width), BF16),
             pltpu.VMEM((planes, in_plane, 1, tokens), F32),
             pltpu.VMEM((planes, in_plane, 1, tokens), F32),
@@ -1645,16 +1726,16 @@
             pltpu.VMEM((count, units), BF16),
             pltpu.VMEM((count, units), BF16),
             pltpu.VMEM((count, 128), F32),
-            pltpu.VMEM((planes + 1, tokens, width), BF16),
+            pltpu.VMEM((planes, tokens, width), BF16),
             dma((2, planes + 1)), dma((2, planes + 1)), dma((planes,)), dma((planes,)),
             dma((planes,)), dma((planes,)), dma((planes,)), dma((planes,)),
             dma((planes,)), dma((planes,)), dma((planes,)), dma((planes,)),
-            dma((planes,)), dma((planes + 1,)), dma((planes,)), dma((planes,)),
-            dma, dma, dma((5,)),
+            dma((planes,)), dma((planes,)), dma((planes,)), dma((planes,)),
+            dma, dma, dma((5,)), dma,
         ],
         compiler_params=pltpu.CompilerParams(vmem_limit_bytes=VMEM_LIMIT, collective_id=1, has_side_effects=True),
         cost_estimate=pl.CostEstimate(flops=4 * flops, bytes_accessed=100 * 10**6, transcendentals=2 * 10**6),
-    )(own, shares, slots, my_slots, w_gate, w_up, w_down, top_rows)
+    )(own, shares, slots, my_slots, w_gate, w_up, w_down, small_all, top_rows, middle, cotangent)
 
 
 def local(
@@ -1678,42 +1759,24 @@
     capacity = -(-capacity // 16) * 16
     small = jnp.concatenate([w_router.T, ffn_gain[None, :], attn_gain[None, :]], axis=0).astype(F32)
     small = jnp.pad(small, ((0, -small.shape[0] % 8), (0, 0)))
-    first_input, query_raw, key_raw, value, attended, branch, slots_flat, my_slots, small_all, weights, top_rows = (
-        run_forward(
-        planes, across, shards, capacity, hidden_in, small, routes.T, cotangent, w_query,
-        key_projection, value_projection, query_gain_row, key_gain_row, cosine, sine, w_output,
-        )
+    (
+        first_input, query_raw, key_raw, value, attended, middle, slots_flat, my_slots, shares, squares, second_input,
+        small_all, weights, top_rows,
+    ) = run_forward(
+        planes, across, shards, capacity, hidden_in, small, routes.T, cotangent, w_query, key_projection,
+        value_projection, query_gain_row, key_gain_row, cosine, sine, w_output,
     )
-    small_all = small_all.transpose(1, 0, 2).reshape(small.shape[0], width)
-    router_full = small_all[:experts].astype(BF16)
-    ffn_scale, attn_scale = small_all[experts : experts + 1], small_all[experts + 1 : experts + 2]
-    source = hidden_in.astype(F32)
-    middle = source + branch
-    second_normed, second_scale = norm_forward(middle)
-    second_input = (second_normed * ffn_scale).astype(BF16)
-    logits = dot_nt(router_full, second_input)
-    expert_ids = jnp.arange(experts, dtype=jnp.int32)
-    routed = jnp.any(routes.T[None, :, :] == expert_ids[:, None, None], axis=1)
-    peaks = jnp.max(jnp.where(routed, logits, -jnp.inf), axis=0, keepdims=True)
-    shifted = jnp.where(routed, jnp.exp(jnp.where(routed, logits - peaks, 0.0)), 0.0)
-    shares = shifted / jnp.sum(shifted, axis=0, keepdims=True)
-
-    rows_in, _, weighted, hidden_units, gate_grad, up_grad, pair_grad, row_grad_sum, share_grad = run_experts(
-        planes, across, shards, capacity, second_input, shares[:, None, :], slots_flat,
-        my_slots, w_gate[0], w_up[0], w_down[0],
-        top_rows,
+    (
+        rows_in, _, weighted, hidden_units, gate_grad, up_grad, pair_grad, middle_grad, low_grad, logit_grad, ffn_gain_grad,
+    ) = run_experts(
+        planes, across, shards, capacity, second_input, shares, slots_flat, my_slots, w_gate[0], w_up[0], w_down[0],
+        small_all, top_rows, middle, cotangent,
     )
-    share_grad = share_grad[:, 0, :]
     units = w_gate.shape[2]
-    grad_top = cotangent.astype(F32)
-    share_center = jnp.sum(shares * share_grad, axis=0, keepdims=True)
-    logit_grad = (shares * (share_grad - share_center)).astype(BF16)
     router_grad = dot_tn(second_input, logit_grad.T)
-    second_grad = row_grad_sum + dot(logit_grad.T, router_full)
-    ffn_gain_grad = jnp.sum(second_grad * second_normed, axis=0)
-    middle_grad = grad_top + norm_backward(second_grad * ffn_scale, second_normed, second_scale)
+    attn_scale = small_all[:, experts + 1, :].reshape(1, width)
     wo_grad, wq_grad, first_part, query_gain_grad, key_gain_grad, _, expert_sum = run_backward(
-        planes, across, shards, capacity, middle_grad.astype(BF16), w_output, attended, query_raw, key_raw, value,
+        planes, across, shards, capacity, low_grad, w_output, attended, query_raw, key_raw, value,
         first_input, weights, query_gain_row, key_gain_row, cosine, sine, slots_flat, weighted,
     )
     mine = width // device_count
@@ -1721,15 +1784,8 @@
         [router_grad.reshape(device_count, mine * experts), ffn_gain_grad.reshape(device_count, mine)], axis=1
     )
     early = jnp.pad(early, ((0, 0), (0, -early.shape[1] % 1024))).reshape(device_count, -1, 128)
-    squares = jnp.stack([jnp.sum(source * source), jnp.sum(branch * branch)])
-    shared = jnp.concatenate(
-        [
-            query_gain_grad[0:1],
-            key_gain_grad[0:1],
-            jnp.pad(squares, (0, head_size - 2))[None, :],
-            jnp.zeros((5, head_size), F32),
-        ],
-        axis=0,
+    shared = squares + jnp.concatenate(
+        [query_gain_grad[0:1], key_gain_grad[0:1], jnp.zeros((6, head_size), F32)], axis=0
     )
     (
         sum_query, sum_key, sum_value, sum_output, hidden_out, grad_in, early_total, late_total, grad_gate, grad_up, grad_down,

time: 775 us -> 777 us (level)
  other arithmetic: 18 us -> 3.96 us
  Pallas kernels: 713 us -> 725 us
    pallas_call x1, Pallas kernels: 156 us -> 168 us  [run_backward(): pl.pallas_call(functools.partial(attention_backward, planes, across, shar...]
    unnamed x64 -> x35, local copies, waits for them, and re-layouts: 21.5 us -> 21.2 us
where the time goes in v6:
time: 777 us; the launch traced here: 764 us
  Pallas kernels  725 us (93%)
  local copies, waits for them, and re-layouts  31.6 us (4%)
    pallas_call x1, Pallas kernels, run_experts(): pl.pallas_call(functools.partial(expert_kernel, planes, across, shards, c...  246 us
    pallas_call x1, Pallas kernels, run_forward(): pl.pallas_call(functools.partial(attention_forward, planes, across, shard...  172 us
    pallas_call x1, Pallas kernels, run_backward(): pl.pallas_call(functools.partial(attention_backward, planes, across, shar...  168 us
    pallas_call x1, Pallas kernels, run_reduce(): pl.pallas_call(functools.partial(reduce_kernel, planes, across, shards),...  139 us
    unnamed x35, local copies, waits for them, and re-layouts  21.2 us

profile of v6, /device:TPU:1, one launch (start us, length us, event | category | flops | bytes accessed | tf_op | source)
XLA Modules:
  0.0 763.5 jit_solution(8749492237538395818)
XLA Ops:
  1.2 0.7 broadcast_in_dim.25
  2.6 1.4 fusion.6.small_ref
  4.0 172.3 %shard_map.280 = (bf16[1024,2048]{1,0:T(8,128)(2,1)}, f32[1024,1024]{1,0:T(8,128)}, f32[1024,128]{1,0:T(8,128)}, bf16[1024,128]{1,0:T(8,128)(2,1)}, bf16[1024,10...) custom-call(bf16[256,2048]{1,0:T(8,128)(2,1)} %hidden_ref.1, ...), custom_call_target="tpu_custom_call" | custom-call | flops 70000001024 | bytes 40000000 | tf_op jit(solution)/shard_map/pallas_call | solution.py:755
  176.3 1.4 slice.32
  177.7 245.5 %shard_map.281 = (bf16[4,640,2048]{2,1,0:T(8,128)(2,1)}, bf16[4,640,2048]{2,1,0:T(8,128)(2,1)}, bf16[4,640,2048]{2,1,0:T(8,128)(2,1)}, bf16[4,640,768]{2,1,0:T(8...) custom-call(bf16[256,2048]{1,0:T(8,128)(2,1)} %get-tuple-element.56., ...), custom_call_target="tpu_custom_call" | custom-call | flops 193273528320 | bytes 100000000 | tf_op jit(solution)/shard_map/pallas_call | solution.py:1696
  423.2 1.7 fusion.7
  425.5 168.3 %shard_map.282 = (bf16[1024,2048]{1,0:T(8,128)(2,1)}, bf16[2048,1280]{1,0:T(8,128)(2,1)}, bf16[1024,2048]{1,0:T(8,128)(2,1)}, f32[8,128]{1,0:T(8,128)}, f32[8,12...) custom-call(bf16[256,2048]{1,0:T(8,128)(2,1)} %get-tuple-element.63.own_grad_ref, ...), custom_call_target="tpu_custom_call" | custom-call | flops 70000001024 | bytes 60000000 | tf_op jit(solution)/shard_map/pallas_call | solution.py:843
  597.1 0.8 copy.36
  597.9 139.0 %shard_map.283 = (f32[64,4096]{1,0:T(8,128)}, f32[64,512]{1,0:T(8,128)}, f32[64,512]{1,0:T(8,128)}, f32[128,2048]{1,0:T(8,128)}, bf16[256,2048]{1,0:T(8,128)(2,1...) custom-call(bf16[2048,1280]{1,0:T(8,128)(2,1)} %get-tuple-element.71, ...), custom_call_target="tpu_custom_call" | custom-call | flops 70000001024 | bytes 40000000 | tf_op jit(solution)/shard_map/pallas_call | solution.py:1256
  736.9 1.3 slice.41
  738.2 1.2 sqrt_bitcast_fusion
  739.4 1.3 slice_bitcast_fusion.1
  740.7 0.7 slice_bitcast_fusion
  741.9 0.7 slice.39
  742.7 0.7 copy.34
  743.4 2.4 copy.46
  745.8 3.3 copy.47
  749.1 1.0 copy.48
  751.4 1.0 copy.51
  752.4 3.2 copy.52
  755.6 3.2 copy.53
  758.8 0.9 slice-done
  759.7 0.8 slice-done.1
  760.4 2.7 copy.54
  (39 shorter events, 7.1 us)
Async XLA Ops:
  425.4 169.7 %copy-start.6 = (f32[8,128]{1,0:T(8,128)S(1)}, f32[8,128]{1,0:T(8,128)}, u32[]{:S(2)}) copy-start(f32[8,128]{1,0:T(8,128)} %get-tuple-element.78) | copy-start | bytes 12292
  425.5 169.7 %copy-start.7 = (f32[8]{0:T(128)S(1)}, f32[8]{0:T(128)}, u32[]{:S(2)}) copy-start(f32[8]{0:T(128)} %pad.15.clone) | copy-start | bytes 100
  425.5 170.8 %copy-start.5 = (f32[1,2048]{1,0:T(1,128)S(1)}, f32[1,2048]{1,0:T(1,128)}, u32[]{:S(2)}) copy-start(f32[1,2048]{1,0:T(1,128)} %get-tuple-element.77) | copy-start | bytes 24580
  736.9 12.2 %copy-start.2 = (f32[64,4096]{1,0:T(8,128)S(1)}, f32[64,4096]{1,0:T(8,128)}, u32[]{:S(2)}) copy-start(f32[64,4096]{1,0:T(8,128)} %get-tuple-element.147) | copy-start | bytes 3145732
  743.4 6.7 copy-start.4
  743.4 7.3 copy-start.3
  743.4 8.0 %copy-start.1 = (f32[128,2048]{1,0:T(8,128)S(1)}, f32[128,2048]{1,0:T(8,128)}, u32[]{:S(2)}) copy-start(f32[128,2048]{1,0:T(8,128)} %get-tuple-element.152) | copy-start | bytes 3145732
  745.8 6.6 copy-start
  749.1 6.5 slice-start.2
  752.4 3.2 slice-start.3
  752.4 7.3 slice-start
  755.6 4.8 slice-start.1

commit v7 on v6

--- a/solution.py
+++ b/solution.py
@@ -382,18 +382,19 @@
             seen = pl.ds(0, (block + 1) * BLOCK)
             query_raw = dot(input_ref[rows, :], weights[:, here])
             query_raw_ref[rows, :] = query_raw
-            parts = []
-            for head in range(heads_a_step):
-                columns = slice(head * head_size, (head + 1) * head_size)
-                query_normed, _ = norm_forward(query_raw[:, columns])
+
+            @pl.loop(0, heads_a_step)
+            def _(head):
+                query_normed, _ = norm_forward(query_raw_ref[rows, columns_at(head * head_size, head_size)])
                 query_rot = rotate(
                     query_normed * query_gain_ref[...], cosine_ref[rows, :], sine_ref[rows, :]
                 ).astype(BF16)
                 scores = dot_nt(query_rot, key_rot_ref[seen, :]) * factor
                 exponent = jnp.exp(scores - jnp.max(scores, axis=-1, keepdims=True))
                 probs = (exponent / jnp.sum(exponent, axis=-1, keepdims=True)).astype(BF16)
-                parts.append(dot(probs, value_ref[seen, :]).astype(BF16))
-            attended_ref[rows, here] = jnp.concatenate(parts, axis=1)
+                attended_ref[rows, columns_at(step * wide + head * head_size, head_size)] = dot(
+                    probs, value_ref[seen, :]
+                ).astype(BF16)
 
     @pl.when(step == 1)
     def _():
@@ -651,13 +652,15 @@
         for block in range(blocks):
             rows_here = pl.ds(block * BLOCK, BLOCK)
             seen = pl.ds(0, (block + 1) * BLOCK)
-            attended_grad = dot_nt(grad_ref[rows_here, :], wo_ref[...]).astype(BF16)
-            for head in range(heads_a_step):
-                columns = slice(head * head_size, (head + 1) * head_size)
+            query_grad_ref[rows_here, :] = dot_nt(grad_ref[rows_here, :], wo_ref[...]).astype(BF16)
+
+            @pl.loop(0, heads_a_step)
+            def _(head):
+                columns = pl.ds(pl.multiple_of(head * head_size, head_size), head_size)
                 query_normed, query_scale = norm_forward(query_raw_ref[rows_here, columns])
                 cosine, sine = cosine_ref[rows_here, :], sine_ref[rows_here, :]
                 query_rot = rotate(query_normed * query_gain_ref[...], cosine, sine).astype(BF16)
-                head_grad = attended_grad[:, columns]
+                head_grad = query_grad_ref[rows_here, columns]
                 keys, values = key_rot_ref[seen, :], value_ref[seen, :]
                 scores = dot_nt(query_rot, keys) * factor
                 exponent = jnp.exp(scores - jnp.max(scores, axis=-1, keepdims=True))

time: 777 us -> 766 us (0.986)
  Pallas kernels: 725 us -> 715 us
    pallas_call x1, Pallas kernels: 168 us -> 160 us  [run_backward(): pl.pallas_call(functools.partial(attention_backward, planes, across, shar...]
where the time goes in v7:
time: 766 us; the launch traced here: 753 us
  Pallas kernels  715 us (93%)
  local copies, waits for them, and re-layouts  31.6 us (4%)
    pallas_call x1, Pallas kernels, run_experts(): pl.pallas_call(functools.partial(expert_kernel, planes, across, shards, c...  246 us
    pallas_call x1, Pallas kernels, run_forward(): pl.pallas_call(functools.partial(attention_forward, planes, across, shard...  173 us
    pallas_call x1, Pallas kernels, run_backward(): pl.pallas_call(functools.partial(attention_backward, planes, across, shar...  160 us
    pallas_call x1, Pallas kernels, run_reduce(): pl.pallas_call(functools.partial(reduce_kernel, planes, across, shards),...  136 us
    unnamed x35, local copies, waits for them, and re-layouts  21.2 us

profile of v7, /device:TPU:1, one launch (start us, length us, event | category | flops | bytes accessed | tf_op | source)
XLA Modules:
  0.0 753.4 jit_solution(8079846092618735962)
XLA Ops:
  1.2 0.7 broadcast_in_dim.25
  2.6 1.4 fusion.6.small_ref
  4.0 172.5 %shard_map.280 = (bf16[1024,2048]{1,0:T(8,128)(2,1)}, f32[1024,1024]{1,0:T(8,128)}, f32[1024,128]{1,0:T(8,128)}, bf16[1024,128]{1,0:T(8,128)(2,1)}, bf16[1024,10...) custom-call(bf16[256,2048]{1,0:T(8,128)(2,1)} %hidden_ref.1, ...), custom_call_target="tpu_custom_call" | custom-call | flops 70000001024 | bytes 40000000 | tf_op jit(solution)/shard_map/pallas_call | solution.py:758
  176.6 1.4 slice.32
  178.0 245.7 %shard_map.281 = (bf16[4,640,2048]{2,1,0:T(8,128)(2,1)}, bf16[4,640,2048]{2,1,0:T(8,128)(2,1)}, bf16[4,640,2048]{2,1,0:T(8,128)(2,1)}, bf16[4,640,768]{2,1,0:T(8...) custom-call(bf16[256,2048]{1,0:T(8,128)(2,1)} %get-tuple-element.56., ...), custom_call_target="tpu_custom_call" | custom-call | flops 193273528320 | bytes 100000000 | tf_op jit(solution)/shard_map/pallas_call | solution.py:1699
  423.7 1.7 fusion.7
  425.9 160.3 %shard_map.282 = (bf16[1024,2048]{1,0:T(8,128)(2,1)}, bf16[2048,1280]{1,0:T(8,128)(2,1)}, bf16[1024,2048]{1,0:T(8,128)(2,1)}, f32[8,128]{1,0:T(8,128)}, f32[8,12...) custom-call(bf16[256,2048]{1,0:T(8,128)(2,1)} %get-tuple-element.63.own_grad_ref, ...), custom_call_target="tpu_custom_call" | custom-call | flops 70000001024 | bytes 60000000 | tf_op jit(solution)/shard_map/pallas_call | solution.py:846
  589.6 0.8 copy.36
  590.4 136.3 %shard_map.283 = (f32[64,4096]{1,0:T(8,128)}, f32[64,512]{1,0:T(8,128)}, f32[64,512]{1,0:T(8,128)}, f32[128,2048]{1,0:T(8,128)}, bf16[256,2048]{1,0:T(8,128)(2,1...) custom-call(bf16[2048,1280]{1,0:T(8,128)(2,1)} %get-tuple-element.71, ...), custom_call_target="tpu_custom_call" | custom-call | flops 70000001024 | bytes 40000000 | tf_op jit(solution)/shard_map/pallas_call | solution.py:1259
  726.7 1.3 slice.41
  728.0 1.2 sqrt_bitcast_fusion
  729.2 1.3 slice_bitcast_fusion.1
  730.4 0.7 slice_bitcast_fusion
  731.7 0.7 slice.39
  732.5 0.7 copy.34
  733.2 2.4 copy.46
  735.6 3.3 copy.47
  738.9 1.0 copy.48
  741.2 1.0 copy.51
  742.2 3.2 copy.52
  745.4 3.2 copy.53
  748.6 0.9 slice-done
  749.5 0.8 slice-done.1
  750.2 2.7 copy.54
  (39 shorter events, 7.1 us)
Async XLA Ops:
  425.9 161.7 %copy-start.6 = (f32[8,128]{1,0:T(8,128)S(1)}, f32[8,128]{1,0:T(8,128)}, u32[]{:S(2)}) copy-start(f32[8,128]{1,0:T(8,128)} %get-tuple-element.78) | copy-start | bytes 12292
  425.9 161.7 %copy-start.7 = (f32[8]{0:T(128)S(1)}, f32[8]{0:T(128)}, u32[]{:S(2)}) copy-start(f32[8]{0:T(128)} %pad.15.clone) | copy-start | bytes 100
  425.9 162.9 %copy-start.5 = (f32[1,2048]{1,0:T(1,128)S(1)}, f32[1,2048]{1,0:T(1,128)}, u32[]{:S(2)}) copy-start(f32[1,2048]{1,0:T(1,128)} %get-tuple-element.77) | copy-start | bytes 24580
  726.7 12.2 %copy-start.2 = (f32[64,4096]{1,0:T(8,128)S(1)}, f32[64,4096]{1,0:T(8,128)}, u32[]{:S(2)}) copy-start(f32[64,4096]{1,0:T(8,128)} %get-tuple-element.147) | copy-start | bytes 3145732
  733.2 6.7 copy-start.4
  733.2 7.3 copy-start.3
  733.2 8.0 %copy-start.1 = (f32[128,2048]{1,0:T(8,128)S(1)}, f32[128,2048]{1,0:T(8,128)}, u32[]{:S(2)}) copy-start(f32[128,2048]{1,0:T(8,128)} %get-tuple-element.152) | copy-start | bytes 3145732
  735.6 6.6 copy-start
  738.9 6.5 slice-start.2
  742.2 3.2 slice-start.3
  742.2 7.3 slice-start
  745.4 4.8 slice-start.1

commit v8 on v7

--- a/solution.py
+++ b/solution.py
@@ -175,38 +175,47 @@
         whole_piece = weights.at[:, columns_at(piece * wide, wide)]
         wait_bytes(whole_piece, weight_recv.at[piece])
 
-    def line_copy(column, block, hop, direction):
-        rows = plane_rows.at[column, block]
+    def half_of(half):
+        return pl.ds(half * (width // 2), width // 2)
+
+    def line_copy(column, block, hop, direction, half):
+        rows = plane_rows.at[column, block, :, half_of(half)]
         return remote(
-            rows, rows, line_send.at[column, direction, hop], line_recv.at[column, direction, hop],
+            rows, rows, line_send.at[column, direction, hop, half], line_recv.at[column, direction, hop, half],
             (z + 1 - 2 * direction, x, w),
         )
 
     def start_line(column, block, hop, upward, downward):
-        @pl.when(upward & (z + 1 < planes))
-        def _():
-            line_copy(column, block, hop, 0).start()
-
-        @pl.when(downward & (z > 0))
-        def _():
-            line_copy(column, block, hop, 1).start()
-
-    def relay(column, hop):
+        for half in range(2):
+
+            @pl.when(upward & (z + 1 < planes))
+            def _():
+                line_copy(column, block, hop, 0, half).start()
+
+            @pl.when(downward & (z > 0))
+            def _():
+                line_copy(column, block, hop, 1, half).start()
+
+    def relay_half(column, hop, half):
         @pl.when(z - hop >= 0)
         def _():
-            wait_bytes(plane_rows.at[column, 0], line_recv.at[column, 0, hop])
+            wait_bytes(plane_rows.at[column, 0, :, half_of(half)], line_recv.at[column, 0, hop, half])
 
             @pl.when(z + 1 < planes)
             def _():
-                line_copy(column, z - hop, hop + 1, 0).start()
+                line_copy(column, z - hop, hop + 1, 0, half).start()
 
         @pl.when(z + hop < planes)
         def _():
-            wait_bytes(plane_rows.at[column, 0], line_recv.at[column, 1, hop])
+            wait_bytes(plane_rows.at[column, 0, :, half_of(half)], line_recv.at[column, 1, hop, half])
 
             @pl.when(z > 0)
             def _():
-                line_copy(column, z + hop, hop + 1, 1).start()
+                line_copy(column, z + hop, hop + 1, 1, half).start()
+
+    def relay(column, hop):
+        for half in range(2):
+            relay_half(column, hop, half)
 
     expert_of = z * in_plane + lax.broadcasted_iota(jnp.int32, (in_plane, tokens), 0)
     earlier = (
@@ -225,7 +234,7 @@
             for index in range(in_plane):
                 table[block * in_plane + index] = slots[index : index + 1, :]
 
-    def pack(column, turn, table):
+    def pack(column, turn, table, halves=(0, 1)):
         block, _, _ = line_order(z, planes, turn)
 
         def index_of(target):
@@ -235,7 +244,9 @@
             slots = table[block * in_plane + index_of(target)]
             chosen[target * capacity : (target + 1) * capacity, :] = (slot_ids == slots).astype(F32).astype(BF16)
 
-        @pl.loop(0, width // chunk)
+        wide_at = pl.ds(halves[0] * (width // 2), len(halves) * (width // 2))
+
+        @pl.loop(halves[0] * (width // 2) // chunk, (halves[-1] + 1) * (width // 2) // chunk)
         def _(part):
             here = pl.ds(pl.multiple_of(part * chunk, chunk), chunk)
             stage[column, turn, :, here] = dot(chosen[...], plane_rows[column, block, :, here]).astype(BF16)
@@ -247,12 +258,13 @@
         def _(offset):
             target = (mine + offset) % targets
             remote(
-                stage.at[column, turn, slice_of(target)], top_rows_hbm.at[block, slice_of(source)],
+                stage.at[column, turn, slice_of(target), wide_at], top_rows_hbm.at[block, slice_of(source), wide_at],
                 top_send.at[column, turn], top_recv.at[block], (z, target // 2, pair * 2 + target % 2),
             ).start()
 
         pltpu.make_async_copy(
-            stage.at[column, turn, slice_of(mine)], top_rows_hbm.at[block, slice_of(source)], top_recv.at[block]
+            stage.at[column, turn, slice_of(mine), wide_at], top_rows_hbm.at[block, slice_of(source), wide_at],
+            top_recv.at[block],
         ).start()
 
     def route_copy(offset):
@@ -448,8 +460,9 @@
                 wait_bytes(routes_in.at[index], plane_route_recv.at[index])
 
         fill_my_slots()
-        relay(1, 3)
-        pack(1, 3, far_slots)
+        for half in range(2):
+            relay_half(1, 3, half)
+            pack(1, 3, far_slots, (half,))
         wait_bytes(hidden.at[far_at], pair_recv.at[2])
         wait_bytes(far_out, pair_send.at[2])
         ffn_row = jnp.concatenate([small_in[part, experts : experts + 1, :] for part in range(shards)], axis=1)
@@ -520,11 +533,13 @@
 
                 @pl.when((z - (hop - 1) >= 0) & (z + 1 < planes))
                 def _():
-                    wait_bytes(plane_rows.at[0, 0], line_send.at[column, 0, hop])
+                    for half in range(2):
+                        wait_bytes(plane_rows.at[0, 0, :, half_of(half)], line_send.at[column, 0, hop, half])
 
                 @pl.when((z + (hop - 1) < planes) & (z > 0))
                 def _():
-                    wait_bytes(plane_rows.at[0, 0], line_send.at[column, 1, hop])
+                    for half in range(2):
+                        wait_bytes(plane_rows.at[0, 0, :, half_of(half)], line_send.at[column, 1, hop, half])
 
         store.wait()
         small_store.wait()
@@ -573,7 +588,7 @@
             back_send.at[block], back_recv.at[block], (z, index // shards, index % shards),
         )
 
-    pace = [(1, 1), (2, 2), (3, 3)]
+    pace = [(1, 0), (2, 1), (3, 2)]
 
     def start_back(turn, near, far):
         block, _, _ = line_order(z, planes, planes - 1 - turn)
@@ -818,7 +833,7 @@
             pltpu.VMEM((tokens, width), BF16),
             dma((3,)), dma((3,)), dma((shards,)), dma((shards,)), dma((steps + 1,)), dma((steps + 1,)),
             dma((planes,)), dma((planes,)), dma, dma((in_plane,)), dma, dma,
-            dma((2, 2, planes + 1)), dma((2, 2, planes + 1)), dma((2, planes)), dma((planes,)), dma((3,)), dma((3,)), dma, dma, dma,
+            dma((2, 2, planes + 1, 2)), dma((2, 2, planes + 1, 2)), dma((2, planes)), dma((planes,)), dma((3,)), dma((3,)), dma, dma, dma,
         ],
         compiler_params=pltpu.CompilerParams(vmem_limit_bytes=VMEM_LIMIT, collective_id=5, has_side_effects=True),
         cost_estimate=pl.CostEstimate(flops=70 * 10**9, bytes_accessed=40 * 10**6, transcendentals=6 * 10**6),
@@ -904,7 +919,8 @@
 
 def reduce_kernel(
     planes, across, shards,
-    wq_hbm, wo_hbm, first_hbm, hidden_ref, middle_hbm, expert_sum_hbm, middle_grad_hbm, scale_ref, early_ref, shared_ref,
+    wq_hbm, wo_hbm, first_hbm, hidden_ref, middle_hbm, expert_sum_hbm, middle_grad_hbm, small_ref, early_ref, query_gain_ref,
+    key_gain_ref, squares_ref,
     rows_hbm, gate_grad_hbm, up_grad_hbm, units_hbm, pair_grad_hbm,
     query_ref, key_ref, value_ref, output_ref, hidden_out_ref, grad_in_ref, early_total_ref, late_total_ref,
     gate_out_hbm, up_out_hbm, down_out_hbm,
@@ -988,6 +1004,8 @@
     per_kind = width // lanes
     depth = side.shape[0]
     late_rows = width // 128
+    experts = everyone
+    scale_row = jnp.concatenate([small_ref[part, experts + 1 : experts + 2, :] for part in range(shards)], axis=1)
     pick = (lax.broadcasted_iota(jnp.int32, (8, 128), 0) == 2).astype(F32)
     lane = lax.broadcasted_iota(jnp.int32, (8, 128), 1)
 
@@ -1080,7 +1098,7 @@
             for offset in range(1, shards):
                 first += first_in[offset, at, :].astype(F32)
             normed, scaling = norm_forward(hidden_ref[at, :].astype(F32))
-            grad = held_a[at, :] + norm_backward(first * scale_ref[...], normed, scaling)
+            grad = held_a[at, :] + norm_backward(first * scale_row, normed, scaling)
             grad_in_ref[at, :] = grad
             return (
                 square + jnp.sum(jnp.sum(grad * grad, axis=1, keepdims=True), axis=0, keepdims=True),
@@ -1092,9 +1110,12 @@
         )
         for row in range(late_rows):
             late[row : row + 1, :] = gain_grad[:, row * 128 : (row + 1) * 128]
-        late[late_rows:, :] = shared_ref[...] + pick * (
+        late[late_rows:, :] = squares_ref[...] + pick * (
             jnp.where(lane == 2, expert_square, 0.0) + jnp.where(lane == 3, square, 0.0)
         )
+
+        late[late_rows : late_rows + 1, :] = query_gain_ref[0:1, :]
+        late[late_rows + 1 : late_rows + 2, :] = key_gain_ref[0:1, :]
 
         @pl.loop(1, everyone)
         def _(offset):
@@ -1241,8 +1262,8 @@
 
 
 def run_reduce(
-    planes, across, shards, wq_grad, wo_grad, first_part, hidden, middle, expert_sum, middle_grad, scale, early, shared,
-    rows_in, gate_grad, up_grad, units, pair_grad, query_columns, key_columns,
+    planes, across, shards, wq_grad, wo_grad, first_part, hidden, middle, expert_sum, middle_grad, small_all, early,
+    query_gain_grad, key_gain_grad, squares, rows_in, gate_grad, up_grad, units, pair_grad, query_columns, key_columns,
 ):
     rings = planes * across
     everyone = rings * shards
@@ -1258,7 +1279,7 @@
     dma = pltpu.SemaphoreType.DMA
     return pl.pallas_call(
         functools.partial(reduce_kernel, planes, across, shards),
-        in_specs=[hbm] * 3 + [vmem] + [hbm] * 3 + [vmem] * 3 + [hbm] * 5,
+        in_specs=[hbm] * 3 + [vmem] + [hbm] * 3 + [vmem] * 5 + [hbm] * 5,
         out_specs=[vmem] * 8 + [hbm] * 3,
         out_shape=[
             jax.ShapeDtypeStruct((mine, query_columns), F32),
@@ -1303,8 +1324,8 @@
         compiler_params=pltpu.CompilerParams(vmem_limit_bytes=VMEM_LIMIT, collective_id=3, has_side_effects=True),
         cost_estimate=pl.CostEstimate(flops=70 * 10**9, bytes_accessed=40 * 10**6, transcendentals=0),
     )(
-        wq_grad, wo_grad, first_part, hidden, middle, expert_sum, middle_grad, scale, early, shared, rows_in, gate_grad,
-        up_grad, units, pair_grad,
+        wq_grad, wo_grad, first_part, hidden, middle, expert_sum, middle_grad, small_all, early, query_gain_grad,
+        key_gain_grad, squares, rows_in, gate_grad, up_grad, units, pair_grad,
     )
 
 
@@ -1777,7 +1798,6 @@
     )
     units = w_gate.shape[2]
     router_grad = dot_tn(second_input, logit_grad.T)
-    attn_scale = small_all[:, experts + 1, :].reshape(1, width)
     wo_grad, wq_grad, first_part, query_gain_grad, key_gain_grad, _, expert_sum = run_backward(
         planes, across, shards, capacity, low_grad, w_output, attended, query_raw, key_raw, value,
         first_input, weights, query_gain_row, key_gain_row, cosine, sine, slots_flat, weighted,
@@ -1787,14 +1807,11 @@
         [router_grad.reshape(device_count, mine * experts), ffn_gain_grad.reshape(device_count, mine)], axis=1
     )
     early = jnp.pad(early, ((0, 0), (0, -early.shape[1] % 1024))).reshape(device_count, -1, 128)
-    shared = squares + jnp.concatenate(
-        [query_gain_grad[0:1], key_gain_grad[0:1], jnp.zeros((6, head_size), F32)], axis=0
-    )
     (
         sum_query, sum_key, sum_value, sum_output, hidden_out, grad_in, early_total, late_total, grad_gate, grad_up, grad_down,
     ) = run_reduce(
-        planes, across, shards, wq_grad, wo_grad, first_part, hidden_in, middle, expert_sum, middle_grad, attn_scale, early,
-        shared, rows_in.reshape(-1, width), gate_grad.reshape(-1, units), up_grad.reshape(-1, units),
+        planes, across, shards, wq_grad, wo_grad, first_part, hidden_in, middle, expert_sum, middle_grad, small_all, early,
+        query_gain_grad, key_gain_grad, squares, rows_in.reshape(-1, width), gate_grad.reshape(-1, units), up_grad.reshape(-1, units),
         hidden_units.reshape(-1, units), pair_grad.reshape(-1, width), w_query.shape[1], key_projection.shape[1],
     )
     early_total = early_total.reshape(-1)

time: 766 us -> 759 us (level)
    pallas_call x1, Pallas kernels: 136 us -> 144 us  [run_reduce(): pl.pallas_call(functools.partial(reduce_kernel, planes, across, shards),...]
    unnamed x35 -> x31, local copies, waits for them, and re-layouts: 21.2 us -> 21.2 us
where the time goes in v8:
time: 759 us; the launch traced here: 750 us
  Pallas kernels  716 us (94%)
  local copies, waits for them, and re-layouts  28.3 us (4%)
    pallas_call x1, Pallas kernels, run_experts(): pl.pallas_call(functools.partial(expert_kernel, planes, across, shards, c...  246 us
    pallas_call x1, Pallas kernels, run_forward(): pl.pallas_call(functools.partial(attention_forward, planes, across, shard...  171 us
    pallas_call x1, Pallas kernels, run_backward(): pl.pallas_call(functools.partial(attention_backward, planes, across, shar...  155 us
    pallas_call x1, Pallas kernels, run_reduce(): pl.pallas_call(functools.partial(reduce_kernel, planes, across, shards),...  144 us
    unnamed x31, local copies, waits for them, and re-layouts  21.2 us

profile of v8, /device:TPU:1, one launch (start us, length us, event | category | flops | bytes accessed | tf_op | source)
XLA Modules:
  0.0 750.0 jit_solution(1993420721840256543)
XLA Ops:
  0.7 0.7 broadcast_in_dim.22
  1.3 0.7 broadcast_in_dim.21
  2.0 1.4 fusion.6.small_ref
  3.4 170.9 %shard_map.280 = (bf16[1024,2048]{1,0:T(8,128)(2,1)}, f32[1024,1024]{1,0:T(8,128)}, f32[1024,128]{1,0:T(8,128)}, bf16[1024,128]{1,0:T(8,128)(2,1)}, bf16[1024,10...) custom-call(bf16[256,2048]{1,0:T(8,128)(2,1)} %hidden_ref.1, ...), custom_call_target="tpu_custom_call" | custom-call | flops 70000001024 | bytes 40000000 | tf_op jit(solution)/shard_map/pallas_call | solution.py:773
  174.3 245.7 %shard_map.281 = (bf16[4,640,2048]{2,1,0:T(8,128)(2,1)}, bf16[4,640,2048]{2,1,0:T(8,128)(2,1)}, bf16[4,640,2048]{2,1,0:T(8,128)(2,1)}, bf16[4,640,768]{2,1,0:T(8...) custom-call(bf16[256,2048]{1,0:T(8,128)(2,1)} %get-tuple-element.56., ...), custom_call_target="tpu_custom_call" | custom-call | flops 193273528320 | bytes 100000000 | tf_op jit(solution)/shard_map/pallas_call | solution.py:1720
  420.0 1.7 fusion.7
  422.2 155.0 %shard_map.282 = (bf16[1024,2048]{1,0:T(8,128)(2,1)}, bf16[2048,1280]{1,0:T(8,128)(2,1)}, bf16[1024,2048]{1,0:T(8,128)(2,1)}, f32[8,128]{1,0:T(8,128)}, f32[8,12...) custom-call(bf16[256,2048]{1,0:T(8,128)(2,1)} %get-tuple-element.63.own_grad_ref, ...), custom_call_target="tpu_custom_call" | custom-call | flops 70000001024 | bytes 60000000 | tf_op jit(solution)/shard_map/pallas_call | solution.py:861
  578.5 0.8 copy.36
  579.3 144.0 %shard_map.283 = (f32[64,4096]{1,0:T(8,128)}, f32[64,512]{1,0:T(8,128)}, f32[64,512]{1,0:T(8,128)}, f32[128,2048]{1,0:T(8,128)}, bf16[256,2048]{1,0:T(8,128)(2,1...) custom-call(bf16[2048,1280]{1,0:T(8,128)(2,1)} %get-tuple-element.71, ...), custom_call_target="tpu_custom_call" | custom-call | flops 70000001024 | bytes 40000000 | tf_op jit(solution)/shard_map/pallas_call | solution.py:1280
  723.4 1.3 slice.29
  724.6 1.2 sqrt_bitcast_fusion
  725.8 1.3 slice_bitcast_fusion.1
  727.1 0.7 slice_bitcast_fusion
  728.4 0.7 slice.27
  729.2 0.7 copy.34
  729.9 2.4 copy.46
  732.3 3.3 copy.47
  735.6 1.0 copy.48
  737.8 1.0 copy.51
  738.8 3.2 copy.52
  742.0 3.2 copy.53
  745.2 0.9 slice-done
  746.1 0.8 slice-done.1
  746.9 2.7 copy.54
  (29 shorter events, 3.8 us)
Async XLA Ops:
  422.2 155.6 %copy-start.5 = (f32[1,2048]{1,0:T(1,128)S(1)}, f32[1,2048]{1,0:T(1,128)}, u32[]{:S(2)}) copy-start(f32[1,2048]{1,0:T(1,128)} %get-tuple-element.77) | copy-start | bytes 24580
  723.3 12.2 %copy-start.2 = (f32[64,4096]{1,0:T(8,128)S(1)}, f32[64,4096]{1,0:T(8,128)}, u32[]{:S(2)}) copy-start(f32[64,4096]{1,0:T(8,128)} %get-tuple-element.147) | copy-start | bytes 3145732
  729.8 6.7 copy-start.4
  729.8 7.3 copy-start.3
  729.8 8.0 %copy-start.1 = (f32[128,2048]{1,0:T(8,128)S(1)}, f32[128,2048]{1,0:T(8,128)}, u32[]{:S(2)}) copy-start(f32[128,2048]{1,0:T(8,128)} %get-tuple-element.152) | copy-start | bytes 3145732
  732.3 6.6 copy-start
  735.5 6.5 slice-start.2
  738.8 3.2 slice-start.3
  738.8 7.3 slice-start
  742.0 4.8 slice-start.1

commit v9 on v8

--- a/solution.py
+++ b/solution.py
@@ -413,7 +413,7 @@
         relay(0, 3)
         pack(0, 3, slots_ref)
 
-    @pl.when(step == 2)
+    @pl.when(step == 3)
     def _():
         relay(1, 2)
         pack(1, 2, far_slots)

time: 759 us -> 748 us (0.986)
  Pallas kernels: 716 us -> 705 us
    pallas_call x1, Pallas kernels: 171 us -> 163 us  [run_forward(): pl.pallas_call(functools.partial(attention_forward, planes, across, shard...]
where the time goes in v9:
time: 748 us; the launch traced here: 739 us
  Pallas kernels  705 us (94%)
  local copies, waits for them, and re-layouts  28.3 us (4%)
    pallas_call x1, Pallas kernels, run_experts(): pl.pallas_call(functools.partial(expert_kernel, planes, across, shards, c...  247 us
    pallas_call x1, Pallas kernels, run_forward(): pl.pallas_call(functools.partial(attention_forward, planes, across, shard...  163 us
    pallas_call x1, Pallas kernels, run_backward(): pl.pallas_call(functools.partial(attention_backward, planes, across, shar...  155 us
    pallas_call x1, Pallas kernels, run_reduce(): pl.pallas_call(functools.partial(reduce_kernel, planes, across, shards),...  140 us
    unnamed x31, local copies, waits for them, and re-layouts  21.2 us

profile of v9, /device:TPU:1, one launch (start us, length us, event | category | flops | bytes accessed | tf_op | source)
XLA Modules:
  0.0 739.1 jit_solution(13074014161131973232)
XLA Ops:
  0.7 0.7 broadcast_in_dim.22
  1.3 0.7 broadcast_in_dim.21
  2.0 1.4 fusion.6.small_ref
  3.4 162.8 %shard_map.280 = (bf16[1024,2048]{1,0:T(8,128)(2,1)}, f32[1024,1024]{1,0:T(8,128)}, f32[1024,128]{1,0:T(8,128)}, bf16[1024,128]{1,0:T(8,128)(2,1)}, bf16[1024,10...) custom-call(bf16[256,2048]{1,0:T(8,128)(2,1)} %hidden_ref.1, ...), custom_call_target="tpu_custom_call" | custom-call | flops 70000001024 | bytes 40000000 | tf_op jit(solution)/shard_map/pallas_call | solution.py:773
  166.2 247.1 %shard_map.281 = (bf16[4,640,2048]{2,1,0:T(8,128)(2,1)}, bf16[4,640,2048]{2,1,0:T(8,128)(2,1)}, bf16[4,640,2048]{2,1,0:T(8,128)(2,1)}, bf16[4,640,768]{2,1,0:T(8...) custom-call(bf16[256,2048]{1,0:T(8,128)(2,1)} %get-tuple-element.56., ...), custom_call_target="tpu_custom_call" | custom-call | flops 193273528320 | bytes 100000000 | tf_op jit(solution)/shard_map/pallas_call | solution.py:1720
  413.3 1.7 fusion.7
  415.5 155.2 %shard_map.282 = (bf16[1024,2048]{1,0:T(8,128)(2,1)}, bf16[2048,1280]{1,0:T(8,128)(2,1)}, bf16[1024,2048]{1,0:T(8,128)(2,1)}, f32[8,128]{1,0:T(8,128)}, f32[8,12...) custom-call(bf16[256,2048]{1,0:T(8,128)(2,1)} %get-tuple-element.63.own_grad_ref, ...), custom_call_target="tpu_custom_call" | custom-call | flops 70000001024 | bytes 60000000 | tf_op jit(solution)/shard_map/pallas_call | solution.py:861
  572.0 0.8 copy.36
  572.8 139.6 %shard_map.283 = (f32[64,4096]{1,0:T(8,128)}, f32[64,512]{1,0:T(8,128)}, f32[64,512]{1,0:T(8,128)}, f32[128,2048]{1,0:T(8,128)}, bf16[256,2048]{1,0:T(8,128)(2,1...) custom-call(bf16[2048,1280]{1,0:T(8,128)(2,1)} %get-tuple-element.71, ...), custom_call_target="tpu_custom_call" | custom-call | flops 70000001024 | bytes 40000000 | tf_op jit(solution)/shard_map/pallas_call | solution.py:1280
  712.4 1.3 slice.29
  713.7 1.2 sqrt_bitcast_fusion
  714.9 1.3 slice_bitcast_fusion.1
  716.2 0.7 slice_bitcast_fusion
  717.5 0.7 slice.27
  718.2 0.7 copy.34
  718.9 2.4 copy.46
  721.3 3.3 copy.47
  724.6 1.0 copy.48
  726.9 1.0 copy.51
  727.9 3.2 copy.52
  731.1 3.2 copy.53
  734.3 0.9 slice-done
  735.2 0.8 slice-done.1
  735.9 2.7 copy.54
  (29 shorter events, 3.8 us)
Async XLA Ops:
  415.5 155.7 %copy-start.5 = (f32[1,2048]{1,0:T(1,128)S(1)}, f32[1,2048]{1,0:T(1,128)}, u32[]{:S(2)}) copy-start(f32[1,2048]{1,0:T(1,128)} %get-tuple-element.77) | copy-start | bytes 24580
  712.4 12.2 %copy-start.2 = (f32[64,4096]{1,0:T(8,128)S(1)}, f32[64,4096]{1,0:T(8,128)}, u32[]{:S(2)}) copy-start(f32[64,4096]{1,0:T(8,128)} %get-tuple-element.147) | copy-start | bytes 3145732
  718.9 6.7 copy-start.4
  718.9 7.3 copy-start.3
  718.9 8.0 %copy-start.1 = (f32[128,2048]{1,0:T(8,128)S(1)}, f32[128,2048]{1,0:T(8,128)}, u32[]{:S(2)}) copy-start(f32[128,2048]{1,0:T(8,128)} %get-tuple-element.152) | copy-start | bytes 3145732
  721.3 6.6 copy-start
  724.6 6.5 slice-start.2
  727.9 3.2 slice-start.3
  727.9 7.3 slice-start
  731.1 4.8 slice-start.1
